TPU v7x, 512 devices: a whole 4x8x8 slice. The times are simulated.
512 devices in a mesh: tok: 16 (over y, core), exp: 8 (over z), tp: 4 (over x).
Axes of the slice: x: 4, y: 8, z: 8, core: 2. Of those that a mesh axis runs over, the one named last changes fastest.
Arguments:
- tokens: bfloat16 [2048, 4096], P('tok'), may hold values from -6 to 6
- router_weight: bfloat16 [4096, 8], replicated, may hold values from -4 to 4
- gate_weight: bfloat16 [8, 4096, 8192], P('exp', None, ('tok', 'tp')), may hold values from -0.09375 to 0.09375
- up_weight: bfloat16 [8, 4096, 8192], P('exp', None, ('tok', 'tp')), may hold values from -0.09375 to 0.09375
- down_weight: bfloat16 [8, 8192, 4096], P('exp', 'tok', 'tp'), may hold values from -0.0625 to 0.0625
- assignments: int32 [2048, 2], P('tok'), may hold values from 0 to 7, all different within a row; in each aligned block of 128 rows (0 to 127, 128 to 255, ...) at most 48 rows name the same one
- limits: int32 [16, 8], P('tok'), may hold values from 24 to 48
Outputs:
- mixed_out: bfloat16 [2048, 4096], P(('tok', 'exp'), 'tp')
Inputs may be any that keep to these rules, and one draw needn't show every extreme that they name: `assignments`: each row names 2 different experts; in each aligned block of 128 rows no expert is named by more than 48 rows.
All inputs are finite; a program needn't handle non-finite values.
Results may differ from a plain program's by a relative error of at most 0.024.
Values may be sent and summed in bfloat16 or wider, within the bound.
No kernel may reach another device: no remote copies, remote signals or barrier semaphores. Data moves between devices by JAX's collectives and lax.ppermute only.
A program may use at most 128 MiB of HBM per device.

v0:
```python
import math

import jax
import jax.numpy as jnp
from jax import lax
from jax.sharding import PartitionSpec as P

TOP = 2
ITERS = 4


SOFT_CAP = 8.0


def row_balance(balanced, top_log):
    return balanced - jnp.log(jnp.sum(jnp.exp(balanced), axis=1, keepdims=True)) + top_log


def local(tokens, router_weight, gate_weight, up_weight, down_weight, assignments, limits):
    local_rows = tokens.shape[0]
    experts = router_weight.shape[1]
    shards = lax.axis_size("tok")
    owners = lax.axis_size("exp")
    capacity = min(local_rows, max(2, 3 * local_rows * TOP // (2 * experts)))
    out_rows = local_rows // owners
    top_log = math.log(TOP)
    target_log = math.log(local_rows * shards * TOP / experts)
    logits = jnp.dot(tokens, router_weight, preferred_element_type=jnp.float32)
    balanced = row_balance(SOFT_CAP * jnp.tanh(logits / SOFT_CAP), top_log)
    for repeat in range(ITERS):
        column = lax.psum(jnp.sum(jnp.exp(balanced), axis=0), "tok")
        balanced = row_balance(balanced - jnp.log(column)[None, :] + target_log, top_log)
    expert_ids = jnp.arange(experts, dtype=jnp.int32)
    picked = (assignments[:, :, None] == expert_ids).astype(jnp.float32)
    per_row = jnp.sum(picked, axis=1)
    row_ids = jnp.arange(local_rows, dtype=jnp.int32)
    earlier = (row_ids[None, :] < row_ids[:, None]).astype(jnp.float32)
    before = jnp.dot(earlier, per_row, precision=lax.Precision.HIGHEST)
    slot_pos = jnp.sum(picked * before[:, None, :], axis=2)
    limit_k = jnp.sum(picked * limits[0].astype(jnp.float32)[None, None, :], axis=2)
    retained = slot_pos < limit_k
    gate_values = jnp.where(
        retained, jnp.exp(jnp.take_along_axis(balanced, assignments, axis=1)), 0.0
    )
    slot_index = slot_pos.astype(jnp.int32)
    owner_index = lax.axis_index("exp")
    routed_here = (assignments == owner_index) & retained
    row_hit = jnp.any(routed_here, axis=1)
    row_slot = jnp.sum(jnp.where(routed_here, slot_index, 0), axis=1)
    slot_ids = jnp.arange(capacity, dtype=jnp.int32)
    select = ((slot_ids[:, None] == row_slot[None, :]) & row_hit[None, :]).astype(jnp.bfloat16)
    expert_rows = jnp.dot(select, tokens, preferred_element_type=jnp.float32).astype(jnp.bfloat16)
    w_gate = gate_weight[0]
    w_up = up_weight[0]
    w_down = down_weight[0]
    shard_piece = lax.all_gather(expert_rows, "tok", axis=0, tiled=True)
    gate_sum = jnp.dot(shard_piece, w_gate, preferred_element_type=jnp.float32)
    up_sum = jnp.dot(shard_piece, w_up, preferred_element_type=jnp.float32)
    hidden = (jax.nn.silu(gate_sum) * up_sum).astype(jnp.bfloat16)
    full_hidden = lax.all_gather(hidden, "tp", axis=1, tiled=True)
    expert_out = lax.psum_scatter(
        jnp.dot(full_hidden, w_down, preferred_element_type=jnp.float32).astype(jnp.bfloat16),
        "tok",
        scatter_dimension=0,
        tiled=True,
    )
    own_start = owner_index * out_rows
    slot_columns = assignments * capacity + slot_index
    own_columns = lax.dynamic_slice_in_dim(slot_columns, own_start, out_rows, 0)
    own_gates = lax.dynamic_slice_in_dim(gate_values, own_start, out_rows, 0)
    all_columns = jnp.arange(experts * capacity, dtype=jnp.int32)
    mixing = jnp.sum(
        jnp.where(
            all_columns[None, None, :] == own_columns[:, :, None], own_gates[:, :, None], 0.0
        ),
        axis=1,
    )
    shard_piece = lax.all_gather(expert_out[None], "exp", axis=0, tiled=True)
    values = shard_piece.reshape(-1, shard_piece.shape[2]).astype(jnp.float32)
    result = jnp.dot(mixing, values, precision=lax.Precision.HIGHEST)
    return result.astype(jnp.bfloat16)


def solution(mesh):
    placed = (
        P("tok", None),
        P(),
        P("exp", None, ("tok", "tp")),
        P("exp", None, ("tok", "tp")),
        P("exp", "tok", "tp"),
        P("tok", None),
        P("tok", None),
    )
    return jax.shard_map(
        local, mesh=mesh, in_specs=placed, out_specs=P(("tok", "exp"), "tp"), check_vma=False
    )
```

profile of v0, /device:TPU:2, one launch (start us, length us, event | category | flops | bytes accessed | tf_op | source)
XLA Modules:
  0.0 227.5 jit_solution(11081874976694926192)
XLA Ops:
  6.5 0.8 convert_bitcast_fusion
  7.3 0.7 convert_reduce_fusion
  8.0 0.1 fusion.7
  8.2 0.8 select_reduce_fusion.1
  9.0 0.7 fusion.14
  9.7 0.7 select_reduce_fusion.3
  10.4 2.3 %convolution_convert_fusion = bf16[48,4096]{1,0:T(8,128)(2,1)} fusion(bf16[128,4096]{1,0:T(8,128)(2,1)} %param.7, s32[128]{0:T(128)S(1)} %get-tuple-element.12, pred[128]{0:T(512)(128)(4,1)S(1)} %get-tuple-element.7), kind=kOutput, calls=%fused_computation.1 | convolution fusion | flops 50540544 | bytes 1442432 | tf_op jit(solution)/shard_map/dot_general | solution.py:52
  12.7 53.2 %all-gather.3.cloned.1.call-done = bf16[768,4096]{1,0:T(8,128)(2,1)} async-done(((bf16[48,4096]{1,0:T(8,128)(2,1)}), bf16[768,4096]{1,0:T(8,128)(2,1)}) %all-gather.3.cloned.1.call-update) | async-done | bytes 6291472 | tf_op jit(solution)/shard_map/all_gather | solution.py:56
  66.0 5.0 %fusion.5 = f32[768,128]{1,0:T(8,128)S(1)} fusion(bf16[768,4096]{1,0:T(8,128)(2,1)} %all-gather.3.cloned.1.call-done, bf16[1,4096,128]{2,1,0:T(8,128)(2,1)} %param.9), kind=kOutput, calls=%fused_computation.11 | convolution fusion | flops 805306368 | bytes 7733248 | tf_op jit(solution)/shard_map/dot_general | solution.py:57
  71.0 1.8 fusion
  72.8 17.3 %all_gather.10 = bf16[768,512]{1,0:T(8,128)(2,1)S(1)} all-gather(bf16[768,128]{1,0:T(8,128)(2,1)S(1)} %fusion), channel_id=1, replica_groups=mesh['tok'=16,'exp'=8,'tp'=4] {'tp'}, dimensions={1}, use_global_device_ids=true | all-gather | bytes 983040 | tf_op jit(solution)/shard_map/all_gather | solution.py:60
  90.2 2.1 convolution_convert_fusion.1
  92.3 0.4 exponential_reduce_fusion.8
  92.7 0.1 exponential_reduce_fusion.7
  92.9 24.5 %psum.28 = f32[8]{0:T(128)S(1)} all-reduce(f32[8]{0:T(128)S(1)} %exponential_reduce_fusion.7), channel_id=1, replica_groups=mesh['tok'=16,'exp'=8,'tp'=4] {'tok'}, use_global_device_ids=true, to_apply=%region_5.0 | all-reduce | flops 8 | bytes 64 | tf_op jit(solution)/shard_map/psum | solution.py:31
  117.4 0.1 exponential_reduce_fusion.6
  117.5 0.2 exponential_reduce_fusion.5
  117.7 23.5 %psum.29 = f32[8]{0:T(128)S(1)} all-reduce(f32[8]{0:T(128)S(1)} %exponential_reduce_fusion.5), channel_id=1, replica_groups=mesh['tok'=16,'exp'=8,'tp'=4] {'tok'}, use_global_device_ids=true, to_apply=%region_8.0 | all-reduce | flops 8 | bytes 64 | tf_op jit(solution)/shard_map/psum | solution.py:31
  141.2 0.1 exponential_reduce_fusion.4
  141.3 0.1 exponential_reduce_fusion.3
  141.5 23.5 %psum.30 = f32[8]{0:T(128)S(1)} all-reduce(f32[8]{0:T(128)S(1)} %exponential_reduce_fusion.3), channel_id=1, replica_groups=mesh['tok'=16,'exp'=8,'tp'=4] {'tok'}, use_global_device_ids=true, to_apply=%region_11.0 | all-reduce | flops 8 | bytes 64 | tf_op jit(solution)/shard_map/psum | solution.py:31
  165.0 0.1 exponential_reduce_fusion.2
  165.1 0.2 exponential_reduce_fusion.1
  165.3 23.5 %psum.31 = f32[8]{0:T(128)S(1)} all-reduce(f32[8]{0:T(128)S(1)} %exponential_reduce_fusion.1), channel_id=1, replica_groups=mesh['tok'=16,'exp'=8,'tp'=4] {'tok'}, use_global_device_ids=true, to_apply=%region_14.0 | all-reduce | flops 8 | bytes 64 | tf_op jit(solution)/shard_map/psum | solution.py:31
  188.9 0.1 exponential_reduce_fusion
  189.0 0.1 copy.23
  189.1 0.1 reshape.50
  189.3 1.4 gather_fusion
  190.7 0.1 reshape.53
  191.0 0.1 constant_dynamic-slice_fusion
  191.2 28.4 %all-gather = bf16[384,1024]{1,0:T(8,128)(2,1)S(1)} all-gather(bf16[48,1024]{1,0:T(8,128)(2,1)} %reduce-scatter.2.cloned.1.call-done), channel_id=2, replica_groups=mesh['tok'=16,'exp'=8,'tp'=4] {'exp'}, dimensions={0}, use_global_device_ids=true | all-gather | bytes 884736 | tf_op jit(solution)/shard_map/all_gather | solution.py:78
  219.6 1.0 convolution_convert_fusion.2
  (32 shorter events, 0.5 us)
Async XLA Ops:
  6.5 83.6 %copy-start = (bf16[1,512,1024]{2,1,0:T(8,128)(2,1)S(1)}, bf16[1,512,1024]{2,1,0:T(8,128)(2,1)}, u32[]{:S(2)}) copy-start(bf16[1,512,1024]{2,1,0:T(8,128)(2,1)} %param.11) | copy-start | bytes 3145732
  6.5 64.4 %copy-start.5 = (bf16[1,4096,128]{2,1,0:T(8,128)(2,1)S(1)}, bf16[1,4096,128]{2,1,0:T(8,128)(2,1)}, u32[]{:S(2)}) copy-start(bf16[1,4096,128]{2,1,0:T(8,128)(2,1)} %param.10) | copy-start | bytes 3145732
  6.5 59.4 %all-gather.3.cloned.1.call-start = ((), (), s32[]{:S(2)}) async-start(), calls=%async_computation.1 | async-start | bytes 6684672 | tf_op jit(solution)/shard_map/all_gather | solution.py:56
  12.7 178.5 %reduce-scatter.2.cloned.1.call-start = ((), (), s32[]{:S(2)}) async-start(), calls=%async_computation.2 | async-start | bytes 1671168 | tf_op jit(solution)/shard_map/reduce_scatter | solution.py:61
  66.0 5.0 %copy-start.4 = (bf16[768,4096]{1,0:T(8,128)(2,1)S(1)}, bf16[768,4096]{1,0:T(8,128)(2,1)}, u32[]{:S(2)}) copy-start(bf16[768,4096]{1,0:T(8,128)(2,1)} %all-gather.3.cloned.1.call-done) | copy-start | bytes 18874372
  71.0 21.3 %copy-start.1 = (bf16[128,4096]{1,0:T(8,128)(2,1)S(1)}, bf16[128,4096]{1,0:T(8,128)(2,1)}, u32[]{:S(2)}) copy-start(bf16[128,4096]{1,0:T(8,128)(2,1)} %param.7) | copy-start | bytes 3145732
  71.0 21.3 %copy-start.2 = (bf16[4096,8]{0,1:T(8,128)(2,1)S(1)}, bf16[4096,8]{0,1:T(8,128)(2,1)}, u32[]{:S(2)}) copy-start(bf16[4096,8]{0,1:T(8,128)(2,1)} %param.8) | copy-start | bytes 196612
  72.8 116.2 %copy-start.3 = (s32[128,2]{0,1:T(2,128)S(1)}, s32[128,2]{0,1:T(2,128)}, u32[]{:S(2)}) copy-start(s32[128,2]{0,1:T(2,128)} %param.12) | copy-start | bytes 3076
Sparse Core Ops, SparseCore 0:
  12.8 53.1 all-gather.2
  92.4 58.7 reduce-scatter.1
where the time goes:
time: 228 us; the launch traced here: 227 us
  blocking collectives  141 us (62%)
  waiting for transfers between devices  53.3 us (23%)
  between operations  13.6 us (6%)
  matrix products  12.7 us (6%)
  other arithmetic  4.9 us (2%)
    psum x4, blocking collectives, local(): column = lax.psum(jnp.sum(jnp.exp(balanced), axis=0), 'tok')  95.1 us
    all_gather x1, waiting for transfers between devices, local(): shard_piece = lax.all_gather(expert_rows, 'tok', axis=0, tiled=True)  53.2 us
    all_gather x1, blocking collectives, local(): shard_piece = lax.all_gather(expert_out[None], 'exp', axis=0, tiled=True)  28.4 us
    all_gather x1, blocking collectives, local(): full_hidden = lax.all_gather(hidden, 'tp', axis=1, tiled=True)  17.3 us
    dot_general x1, matrix products, local(): gate_sum = jnp.dot(shard_piece, w_gate, preferred_element_type=jnp.float32)  4.97 us
  transfers between devices with their start and end apart: 2, of which 1 were waited for; matrix products, arithmetic and copies ran while one was open for 2% of the time, Pallas kernels for 0%

commit v1 on v0

v1 whole, which is shorter than its diff:
```python
import functools
import math

import jax
import jax.numpy as jnp
from jax import lax
from jax.experimental import pallas as pl
from jax.experimental.pallas import tpu as pltpu
from jax.sharding import Mesh, PartitionSpec as P

TOP = 2
ITERS = 4
SOFT_CAP = 8.0
CORES = 2


def swap_cores(value):
    return lax.ppermute(value, "core", [(0, 1), (1, 0)])


def ffn_kernel(rows_ref, gate_ref, up_ref, gate2_ref, up2_ref, out_ref, acc_ref, acc2_ref):
    step = pl.program_id(0)
    rows = rows_ref[...]
    own = jnp.dot(
        rows,
        jnp.concatenate([gate_ref[...], up_ref[...]], axis=1),
        preferred_element_type=jnp.float32,
    )
    peer = jnp.dot(
        rows,
        jnp.concatenate([gate2_ref[...], up2_ref[...]], axis=1),
        preferred_element_type=jnp.float32,
    )

    @pl.when(step == 0)
    def _():
        acc_ref[...] = own
        acc2_ref[...] = peer

    @pl.when(step > 0)
    def _():
        acc_ref[...] += own
        acc2_ref[...] += peer

    @pl.when(step == pl.num_programs(0) - 1)
    def _():
        units = gate_ref.shape[1]
        for index, ref in enumerate((acc_ref, acc2_ref)):
            gate = ref[:, :units]
            hidden = gate / (1.0 + jnp.exp(-gate)) * ref[:, units:]
            out_ref[:, index * units : (index + 1) * units] = hidden.astype(out_ref.dtype)


def ffn(rows, gate, up, gate2, up2, chunk=1024):
    count, width = rows.shape
    units = gate.shape[1]
    weight = pl.BlockSpec((chunk, units), lambda k: (k, 0))
    return pl.pallas_call(
        ffn_kernel,
        grid=(width // chunk,),
        in_specs=[pl.BlockSpec((count, chunk), lambda k: (0, k))] + [weight] * 4,
        out_specs=pl.BlockSpec((count, 2 * units), lambda k: (0, 0)),
        out_shape=jax.ShapeDtypeStruct((count, 2 * units), jnp.bfloat16),
        scratch_shapes=[pltpu.VMEM((count, 2 * units), jnp.float32)] * 2,
        compiler_params=pltpu.CompilerParams(vmem_limit_bytes=24 << 20),
        cost_estimate=pl.CostEstimate(
            flops=8 * count * width * units,
            bytes_accessed=2 * count * width + 8 * width * units,
            transcendentals=2 * count * units,
        ),
        name="ffn",
    )(rows, gate, up, gate2, up2)


def down_kernel(hidden_ref, down_ref, down2_ref, out_ref, acc_ref):
    step = pl.program_id(0)
    part = jnp.dot(
        hidden_ref[0],
        jnp.concatenate([down_ref[...], down2_ref[...]], axis=0),
        preferred_element_type=jnp.float32,
    )

    @pl.when(step == 0)
    def _():
        acc_ref[...] = part

    @pl.when(step > 0)
    def _():
        acc_ref[...] += part

    @pl.when(step == pl.num_programs(0) - 1)
    def _():
        out_ref[...] = acc_ref[...].astype(out_ref.dtype)


def down(hidden, weight, weight2):
    parts, count, units = hidden.shape
    columns = weight.shape[1]
    block = pl.BlockSpec((units // 2, columns), lambda k: (k, 0))
    return pl.pallas_call(
        down_kernel,
        grid=(parts,),
        in_specs=[pl.BlockSpec((1, count, units), lambda k: (k, 0, 0)), block, block],
        out_specs=pl.BlockSpec((count, columns), lambda k: (0, 0)),
        out_shape=jax.ShapeDtypeStruct((count, columns), jnp.bfloat16),
        scratch_shapes=[pltpu.VMEM((count, columns), jnp.float32)],
        compiler_params=pltpu.CompilerParams(vmem_limit_bytes=24 << 20),
        cost_estimate=pl.CostEstimate(
            flops=2 * parts * count * units * columns,
            bytes_accessed=2 * parts * units * (count + columns) + 2 * count * columns,
            transcendentals=0,
        ),
        name="down",
    )(hidden, weight, weight2)


def weigh_kernel(parts_ref, pick_ref, gate_ref, out_ref):
    total = jnp.sum(parts_ref[...].astype(jnp.float32), axis=0).astype(jnp.bfloat16)
    chosen = jnp.dot(pick_ref[...], total, preferred_element_type=jnp.float32)
    out_ref[...] = (chosen * gate_ref[...]).astype(out_ref.dtype)


def weigh(parts, pick, gate):
    count = pick.shape[0]
    columns = parts.shape[2]
    return pl.pallas_call(
        weigh_kernel,
        out_shape=jax.ShapeDtypeStruct((count, columns), jnp.bfloat16),
        compiler_params=pltpu.CompilerParams(vmem_limit_bytes=24 << 20),
        cost_estimate=pl.CostEstimate(
            flops=2 * count * pick.shape[1] * columns,
            bytes_accessed=2 * parts.size + 2 * count * columns,
            transcendentals=0,
        ),
        name="weigh",
    )(parts, pick, gate)


def local(tokens, router_weight, gate_weight, up_weight, down_weight, assignments, limits):
    local_rows = tokens.shape[0]
    experts = router_weight.shape[1]
    rings = lax.axis_size("y")
    shards = rings * CORES
    owners = lax.axis_size("exp")
    capacity = min(local_rows, max(2, 3 * local_rows * TOP // (2 * experts)))
    out_rows = local_rows // owners
    target = local_rows * shards * TOP / experts
    owner = lax.axis_index("exp")

    hit = jnp.any(assignments == owner, axis=1)
    row_ids = jnp.arange(local_rows, dtype=jnp.int32)
    earlier = (row_ids[None, :] < row_ids[:, None]) & hit[None, :]
    slot = jnp.sum(earlier.astype(jnp.int32), axis=1)
    kept = hit & (slot < lax.dynamic_index_in_dim(limits[0], owner, keepdims=False))
    slot_ids = jnp.arange(capacity, dtype=jnp.int32)
    select = ((slot_ids[:, None] == slot[None, :]) & kept[None, :]).astype(jnp.bfloat16)
    expert_rows = jnp.dot(select, tokens, preferred_element_type=jnp.float32).astype(jnp.bfloat16)
    rows = lax.all_gather(expert_rows, "y", axis=0, tiled=True)

    w_gate, w_up, w_down, tokens2, expert_rows2 = lax.optimization_barrier(
        (gate_weight[0], up_weight[0], down_weight[0], tokens, expert_rows)
    )
    gate2, up2, down2 = swap_cores(w_gate), swap_cores(w_up), swap_cores(w_down)

    logits = lax.dot_general(
        router_weight, tokens2, (((0,), (1,)), ((), ())), preferred_element_type=jnp.float32
    )
    capped = SOFT_CAP * jnp.tanh(logits / SOFT_CAP)
    scores = lax.all_gather(capped, ("y", "core"), axis=0)
    weights = jnp.exp(scores)
    weights = weights * (TOP / jnp.sum(weights, axis=1, keepdims=True))
    for repeat in range(ITERS):
        weights = weights * (target / jnp.sum(weights, axis=(0, 2), keepdims=True))
        weights = weights * (TOP / jnp.sum(weights, axis=1, keepdims=True))
    shard = lax.axis_index("y") * CORES + lax.axis_index("core")
    own = lax.dynamic_slice(weights, (shard, owner, 0), (1, 1, local_rows)).reshape(local_rows)
    gate_value = jnp.where(kept, own, 0.0)[:, None]
    pick = ((slot_ids[None, :] == slot[:, None]) & kept[:, None]).astype(jnp.bfloat16)

    hidden = ffn(rows, w_gate, w_up, gate2, up2)
    full_hidden = lax.all_gather(hidden, "tp", axis=0)
    partial = down(full_hidden, w_down, down2)
    parts = lax.all_to_all(partial.reshape(rings, capacity, partial.shape[1]), "y", 0, 0)
    shares = weigh(parts, pick, gate_value)
    shares = lax.all_to_all(shares.reshape(owners, out_rows, shares.shape[1]), "exp", 0, 0)
    return jnp.sum(shares.astype(jnp.float32), axis=0).astype(jnp.bfloat16)


def solution(mesh):
    shape = mesh.devices.shape
    fine = Mesh(
        mesh.devices.reshape((shape[0] // CORES, CORES) + shape[1:]), ("y", "core", "exp", "tp")
    )
    tok = ("y", "core")
    placed = (
        P(tok, None),
        P(),
        P("exp", None, tok + ("tp",)),
        P("exp", None, tok + ("tp",)),
        P("exp", tok, "tp"),
        P(tok, None),
        P(tok, None),
    )
    return jax.shard_map(
        local, mesh=fine, in_specs=placed, out_specs=P(tok + ("exp",), "tp"), check_vma=False
    )
```

time: 228 us -> 138 us (0.61)
  the two profiles are of different devices: /device:TPU:2 before, /device:TPU:8 now
where the time goes in v1:
time: 138 us
  blocking collectives  52.2 us (38%)
  waiting for transfers between devices  42.8 us (31%)
  between operations  13.6 us (10%)
  starting transfers between devices  10.7 us (8%)
  Pallas kernels  9.07 us (7%)
  other arithmetic  3.6 us (3%)
  local copies, waits for them, and re-layouts  3.41 us (2%)
  matrix products  2.27 us (2%)
    all_gather x1, waiting for transfers between devices, local(): rows = lax.all_gather(expert_rows, 'y', axis=0, tiled=True)  22.9 us
    all_gather x1, blocking collectives, local(): scores = lax.all_gather(capped, ('y', 'core'), axis=0)  20.2 us
    all_to_all x1, waiting for transfers between devices, local(): lax.all_to_all(partial.reshape(rings, capacity, partial.shape[1]), 'y', 0...  19.9 us
    all_to_all x1, blocking collectives, local(): lax.all_to_all(shares.reshape(owners, out_rows, shares.shape[1]), 'exp',...  17.7 us
    all_gather x1, blocking collectives, local(): full_hidden = lax.all_gather(hidden, 'tp', axis=0)  14.4 us
    ppermute x3, starting transfers between devices, swap_cores(): return lax.ppermute(value, 'core', [(0, 1), (1, 0)])  6.26 us
    all_to_all x1, starting transfers between devices, local(): lax.all_to_all(partial.reshape(rings, capacity, partial.shape[1]), 'y', 0...  4.48 us
    pallas_call x1, Pallas kernels, ffn(): pl.pallas_call(ffn_kernel, grid=(width // chunk,), in_specs=[pl.BlockSpec...  4.42 us
  transfers between devices with their start and end apart: 5, of which 2 were waited for; matrix products, arithmetic and copies ran while one was open for 2% of the time, Pallas kernels for 3%

profile of v1, /device:TPU:8, one launch (start us, length us, event | category | flops | bytes accessed | tf_op | source)
XLA Modules:
  0.0 137.7 jit_solution(8300660535064985737)
XLA Ops:
  6.6 0.8 compare_reduce_fusion
  7.4 0.1 convert_reduce_fusion
  7.5 1.2 constant_dynamic-slice_fusion.2
  8.8 0.7 compare_and_fusion
  9.4 1.1 convolution_convert_fusion
  10.5 0.0 all-gather.4.cloned.1.call-update
  10.5 1.9 %collective-permute-start = (bf16[4096,128]{1,0:T(8,128)(2,1)}, bf16[4096,128]{1,0:T(8,128)(2,1)}, u32[]{:S(2)}, u32[]{:S(2)}) collective-permute-start(bf16[4096,128]{1,0:T(8,128)(2,1)} %bitcast.38), channel_id=1, source_target_pairs={{0,32},{32,0},{1,33},{33,1},{2,34},{34,2},{3,35},{35,3},{4,36},{36... | collective-permute-start | bytes 3145736 | tf_op jit(solution)/shard_map/ppermute | solution.py:18
  12.4 2.4 %collective-permute-start.1 = (bf16[4096,128]{1,0:T(8,128)(2,1)}, bf16[4096,128]{1,0:T(8,128)(2,1)}, u32[]{:S(2)}, u32[]{:S(2)}) collective-permute-start(bf16[4096,128]{1,0:T(8,128)(2,1)} %bitcast.40), channel_id=1, source_target_pairs={{0,32},{32,0},{1,33},{33,1},{2,34},{34,2},{3,35},{35,3},{4,36},{36... | collective-permute-start | bytes 3145736 | tf_op jit(solution)/shard_map/ppermute | solution.py:18
  14.9 1.9 %collective-permute-start.2 = (bf16[512,1024]{1,0:T(8,128)(2,1)}, bf16[512,1024]{1,0:T(8,128)(2,1)}, u32[]{:S(2)}, u32[]{:S(2)}) collective-permute-start(bf16[512,1024]{1,0:T(8,128)(2,1)} %bitcast.42), channel_id=1, source_target_pairs={{0,32},{32,0},{1,33},{33,1},{2,34},{34,2},{3,35},{35,3},{4,36},{36... | collective-permute-start | bytes 3145736 | tf_op jit(solution)/shard_map/ppermute | solution.py:18
  16.8 1.2 fusion.2
  18.0 20.2 %all-gather.1 = f32[128,128]{1,0:T(8,128)S(1)} all-gather(f32[8,128]{1,0:T(8,128)S(1)} %fusion.2), channel_id=3, replica_groups=mesh['y'=8,'core'=2,'exp'=8,'tp'=4] {'y','core'}, dimensions={0}, use_global_device_ids=true | all-gather | bytes 69632 | tf_op jit(solution)/shard_map/all_gather | solution.py:169
  38.3 0.1 fusion.7
  38.4 0.1 fusion.16
  38.5 0.2 multiply_reduce_fusion.2
  38.7 0.1 fusion.8
  38.8 0.1 copy.10
  39.0 0.2 multiply_reduce_fusion.1
  39.2 0.1 fusion.9
  39.3 0.2 multiply_reduce_fusion
  39.5 22.9 %all-gather.4.cloned.1.call-done.rows_ref = bf16[384,4096]{1,0:T(8,128)(2,1)} async-done(((bf16[48,4096]{1,0:T(8,128)(2,1)}), bf16[384,4096]{1,0:T(8,128)(2,1)}) %all-gather.4.cloned.1.call-update) | async-done | bytes 3145744 | tf_op jit(solution)/shard_map/all_gather | solution.py:158
  62.5 1.9 %copy-done.1 = bf16[384,4096]{1,0:T(8,128)(2,1)S(1)} copy-done((bf16[384,4096]{1,0:T(8,128)(2,1)S(1)}, bf16[384,4096]{1,0:T(8,128)(2,1)}, u32[]{:S(2)}) %copy-start.1) | copy-done | bytes 3145752
  64.4 4.4 %ffn.1 = bf16[384,256]{1,0:T(8,128)(2,1)S(1)} custom-call(bf16[384,4096]{1,0:T(8,128)(2,1)S(1)} %copy-done.1, bf16[4096,128]{1,0:T(8,128)(2,1)S(1)} %bitcast.39, bf16[4096,128]{1,0:T(8,128)(2,1)S(1)} %bitcast.41, bf16[4096,128]{1,0:T(8,128)(2,1)} %collective-permute-done.gate2_ref, bf16[4096,128]{1,0:T(8,128)(2,1)} %collective-permute-done.1.up2_ref), custom_call_target="tpu_custom_call" | custom-call | flops 1610612736 | bytes 7340032 | tf_op jit(solution)/shard_map/ffn/pallas_call | solution.py:58
  68.8 14.4 %all-gather = bf16[1536,256]{1,0:T(8,128)(2,1)S(1)} all-gather(bf16[384,256]{1,0:T(8,128)(2,1)S(1)} %ffn.1), channel_id=2, replica_groups=mesh['y'=8,'core'=2,'exp'=8,'tp'=4] {'tp'}, dimensions={0}, use_global_device_ids=true | all-gather | bytes 983040 | tf_op jit(solution)/shard_map/all_gather | solution.py:181
  83.2 4.4 %down.1 = bf16[384,1024]{1,0:T(8,128)(2,1)} custom-call(bf16[4,384,256]{2,1,0:T(8,128)(2,1)S(1)} %bitcast.37, bf16[512,1024]{1,0:T(8,128)(2,1)S(1)} %bitcast.43, bf16[512,1024]{1,0:T(8,128)(2,1)} %collective-permute-done.2.down2_ref), custom_call_target="tpu_custom_call" | custom-call | flops 805306368 | bytes 3670016 | tf_op jit(solution)/shard_map/down/pallas_call | solution.py:100
  87.5 4.5 %all-to-all-start = ((bf16[8,48,1024]{2,1,0:T(8,128)(2,1)}), bf16[8,48,1024]{2,1,0:T(8,128)(2,1)S(1)}, u32[]{:S(2)}, u32[]{:S(2)}) async-start(bf16[8,48,1024]{2,1,0:T(8,128)(2,1)} %bitcast.5), calls=%async_computation | async-start | bytes 1572864 | tf_op jit(solution)/shard_map/all_to_all | solution.py:183
  92.0 0.1 fusion.17
  92.2 0.1 copy.11
  92.3 0.1 fusion.5.pick_ref
  92.4 19.9 %all-to-all-done.parts_ref = bf16[8,48,1024]{2,1,0:T(8,128)(2,1)S(1)} async-done(((bf16[8,48,1024]{2,1,0:T(8,128)(2,1)}), bf16[8,48,1024]{2,1,0:T(8,128)(2,1)S(1)}, u32[]{:S(2)}, u32[]{:S(2)}) %all-to-all-start) | async-done | bytes 786464 | tf_op jit(solution)/shard_map/all_to_all | solution.py:183
  112.3 0.3 weigh.1
  112.6 17.7 %all_to_all.10 = bf16[8,16,1024]{2,1,0:T(8,128)(2,1)S(1)} all-to-all(bf16[8,16,1024]{2,1,0:T(8,128)(2,1)S(1)} %bitcast.44), channel_id=1, replica_groups=mesh['y'=8,'core'=2,'exp'=8,'tp'=4] {'exp'}, dimensions={0} | all-to-all | bytes 524288 | tf_op jit(solution)/shard_map/all_to_all | solution.py:185
  130.2 0.7 reduce_sum.112
  (26 shorter events, 0.1 us)
Async XLA Ops:
  6.5 2.9 %copy-start = (bf16[128,4096]{1,0:T(8,128)(2,1)S(1)}, bf16[128,4096]{1,0:T(8,128)(2,1)}, u32[]{:S(2)}) copy-start(bf16[128,4096]{1,0:T(8,128)(2,1)} %param.7) | copy-start | bytes 3145732
  6.5 55.9 %copy-start.2 = (bf16[1,4096,128]{2,1,0:T(8,128)(2,1)S(1)}, bf16[1,4096,128]{2,1,0:T(8,128)(2,1)}, u32[]{:S(2)}) copy-start(bf16[1,4096,128]{2,1,0:T(8,128)(2,1)} %param.9) | copy-start | bytes 3145732
  6.5 55.9 %copy-start.3 = (bf16[1,4096,128]{2,1,0:T(8,128)(2,1)S(1)}, bf16[1,4096,128]{2,1,0:T(8,128)(2,1)}, u32[]{:S(2)}) copy-start(bf16[1,4096,128]{2,1,0:T(8,128)(2,1)} %param.10) | copy-start | bytes 3145732
  6.5 55.9 %all-gather.4.cloned.1.call-start = ((), (), s32[]{:S(2)}) async-start(), calls=%async_computation.2 | async-start | bytes 3538944 | tf_op jit(solution)/shard_map/all_gather | solution.py:158
  10.5 29.0 %collective-permute-start = (bf16[4096,128]{1,0:T(8,128)(2,1)}, bf16[4096,128]{1,0:T(8,128)(2,1)}, u32[]{:S(2)}, u32[]{:S(2)}) collective-permute-start(bf16[4096,128]{1,0:T(8,128)(2,1)} %bitcast.38), channel_id=1, source_target_pairs={{0,32},{32,0},{1,33},{33,1},{2,34},{34,2},{3,35},{35,3},{4,36},{36... | collective-permute-start | bytes 3145736 | tf_op jit(solution)/shard_map/ppermute | solution.py:18
  12.4 27.1 %collective-permute-start.1 = (bf16[4096,128]{1,0:T(8,128)(2,1)}, bf16[4096,128]{1,0:T(8,128)(2,1)}, u32[]{:S(2)}, u32[]{:S(2)}) collective-permute-start(bf16[4096,128]{1,0:T(8,128)(2,1)} %bitcast.40), channel_id=1, source_target_pairs={{0,32},{32,0},{1,33},{33,1},{2,34},{34,2},{3,35},{35,3},{4,36},{36... | collective-permute-start | bytes 3145736 | tf_op jit(solution)/shard_map/ppermute | solution.py:18
  14.9 68.3 %collective-permute-start.2 = (bf16[512,1024]{1,0:T(8,128)(2,1)}, bf16[512,1024]{1,0:T(8,128)(2,1)}, u32[]{:S(2)}, u32[]{:S(2)}) collective-permute-start(bf16[512,1024]{1,0:T(8,128)(2,1)} %bitcast.42), channel_id=1, source_target_pairs={{0,32},{32,0},{1,33},{33,1},{2,34},{34,2},{3,35},{35,3},{4,36},{36... | collective-permute-start | bytes 3145736 | tf_op jit(solution)/shard_map/ppermute | solution.py:18
  62.5 1.9 %copy-start.1 = (bf16[384,4096]{1,0:T(8,128)(2,1)S(1)}, bf16[384,4096]{1,0:T(8,128)(2,1)}, u32[]{:S(2)}) copy-start(bf16[384,4096]{1,0:T(8,128)(2,1)} %all-gather.4.cloned.1.call-done.rows_ref) | copy-start | bytes 9437188
  64.4 18.8 %copy-start.4 = (bf16[1,512,1024]{2,1,0:T(8,128)(2,1)S(1)}, bf16[1,512,1024]{2,1,0:T(8,128)(2,1)}, u32[]{:S(2)}) copy-start(bf16[1,512,1024]{2,1,0:T(8,128)(2,1)} %param.11) | copy-start | bytes 3145732
  87.5 24.8 %all-to-all-start = ((bf16[8,48,1024]{2,1,0:T(8,128)(2,1)}), bf16[8,48,1024]{2,1,0:T(8,128)(2,1)S(1)}, u32[]{:S(2)}, u32[]{:S(2)}) async-start(bf16[8,48,1024]{2,1,0:T(8,128)(2,1)} %bitcast.5), calls=%async_computation | async-start | bytes 1572864 | tf_op jit(solution)/shard_map/all_to_all | solution.py:183
Sparse Core Ops, SparseCore 0:
  10.6 51.7 all-gather.3

commit v2 on v1

v2 whole, which is shorter than its diff:
```python
import jax
import jax.numpy as jnp
from jax import lax
from jax.experimental import pallas as pl
from jax.experimental.pallas import tpu as pltpu
from jax.sharding import Mesh, PartitionSpec as P

TOP = 2
ITERS = 4
SOFT_CAP = 8.0
CORES = 2


def swap_cores(value):
    return lax.ppermute(value, "core", [(0, 1), (1, 0)])


def route_kernel(owner_ref, limits_ref, assign_ref, tokens_ref, select_ref, rows_ref):
    owner = owner_ref[0]
    count = assign_ref.shape[1]
    capacity = select_ref.shape[0]
    hit = jnp.sum(jnp.where(assign_ref[...] == owner, 1.0, 0.0), axis=0, keepdims=True)
    row = lax.broadcasted_iota(jnp.int32, (count, count), 0)
    column = lax.broadcasted_iota(jnp.int32, (count, count), 1)
    earlier = jnp.where(row < column, 1.0, 0.0).astype(jnp.bfloat16)
    named = jnp.broadcast_to(hit, (16, count)).astype(jnp.bfloat16)
    slot = jnp.dot(named, earlier, preferred_element_type=jnp.float32)[:1].astype(jnp.int32)
    slot = jnp.where((hit > 0.0) & (slot < limits_ref[0, owner]), slot, -1)
    slot_ids = lax.broadcasted_iota(jnp.int32, (capacity, count), 0)
    select = jnp.where(slot_ids == slot, 1.0, 0.0).astype(jnp.bfloat16)
    select_ref[...] = select
    rows_ref[...] = jnp.dot(
        select, tokens_ref[...], preferred_element_type=jnp.float32
    ).astype(rows_ref.dtype)


def route(owner, limits, assignments, tokens, capacity):
    count, width = tokens.shape
    whole = pl.BlockSpec(memory_space=pltpu.VMEM)
    scalars = pl.BlockSpec(memory_space=pltpu.SMEM)
    return pl.pallas_call(
        route_kernel,
        in_specs=[scalars, scalars, whole, whole],
        out_specs=[whole, whole],
        out_shape=[
            jax.ShapeDtypeStruct((capacity, count), jnp.bfloat16),
            jax.ShapeDtypeStruct((capacity, width), jnp.bfloat16),
        ],
        compiler_params=pltpu.CompilerParams(vmem_limit_bytes=16 << 20),
        cost_estimate=pl.CostEstimate(
            flops=2 * capacity * count * width,
            bytes_accessed=2 * (count + capacity) * width,
            transcendentals=0,
        ),
        name="route",
    )(owner, limits, assignments, tokens)


def ffn_kernel(rows_hbm, gate_ref, up_ref, gate2_ref, up2_ref, out_ref, rows_ref, sems):
    chunks, _, chunk = rows_ref.shape
    copies = [
        pltpu.make_async_copy(
            rows_hbm.at[:, pl.ds(index * chunk, chunk)], rows_ref.at[index], sems.at[index]
        )
        for index in range(chunks)
    ]
    for copy in copies:
        copy.start()
    units = gate_ref.shape[1]
    totals = [None, None]
    for index in range(chunks):
        copies[index].wait()
        rows = rows_ref[index]
        part = pl.ds(index * chunk, chunk)
        for side, (gate, up) in enumerate(((gate_ref, up_ref), (gate2_ref, up2_ref))):
            both = jnp.concatenate([gate[part, :], up[part, :]], axis=1)
            product = jnp.dot(rows, both, preferred_element_type=jnp.float32)
            totals[side] = product if index == 0 else totals[side] + product
    for side, total in enumerate(totals):
        gate = total[:, :units]
        hidden = gate / (1.0 + jnp.exp(-gate)) * total[:, units:]
        out_ref[:, side * units : (side + 1) * units] = hidden.astype(out_ref.dtype)


def ffn(rows, gate, up, gate2, up2, chunk=1024):
    count, width = rows.shape
    units = gate.shape[1]
    whole = pl.BlockSpec(memory_space=pltpu.VMEM)
    return pl.pallas_call(
        ffn_kernel,
        in_specs=[pl.BlockSpec(memory_space=pltpu.HBM)] + [whole] * 4,
        out_specs=whole,
        out_shape=jax.ShapeDtypeStruct((count, 2 * units), jnp.bfloat16),
        scratch_shapes=[
            pltpu.VMEM((width // chunk, count, chunk), jnp.bfloat16),
            pltpu.SemaphoreType.DMA((width // chunk,)),
        ],
        compiler_params=pltpu.CompilerParams(vmem_limit_bytes=32 << 20),
        cost_estimate=pl.CostEstimate(
            flops=8 * count * width * units,
            bytes_accessed=2 * count * width + 8 * width * units,
            transcendentals=2 * count * units,
        ),
        name="ffn",
    )(rows, gate, up, gate2, up2)


def down_kernel(hidden_ref, down_ref, down2_ref, out_ref):
    parts = hidden_ref.shape[0]
    units = down_ref.shape[0] // parts
    total = None
    for index in range(parts):
        part = pl.ds(index * units, units)
        both = jnp.concatenate([down_ref[part, :], down2_ref[part, :]], axis=0)
        product = jnp.dot(hidden_ref[index], both, preferred_element_type=jnp.float32)
        total = product if index == 0 else total + product
    out_ref[...] = total.astype(out_ref.dtype)


def down(hidden, weight, weight2):
    parts, count, units = hidden.shape
    columns = weight.shape[1]
    return pl.pallas_call(
        down_kernel,
        out_shape=jax.ShapeDtypeStruct((count, columns), jnp.bfloat16),
        compiler_params=pltpu.CompilerParams(vmem_limit_bytes=24 << 20),
        cost_estimate=pl.CostEstimate(
            flops=2 * parts * count * units * columns,
            bytes_accessed=2 * parts * units * (count + columns) + 2 * count * columns,
            transcendentals=0,
        ),
        name="down",
    )(hidden, weight, weight2)


def weigh_kernel(parts_ref, select_ref, gate_ref, out_ref):
    select = select_ref[...]
    total = jnp.sum(parts_ref[...].astype(jnp.float32), axis=0).astype(jnp.bfloat16)
    gate = jnp.sum(select.astype(jnp.float32) * gate_ref[...], axis=1, keepdims=True)
    weighted = (total.astype(jnp.float32) * gate).astype(jnp.bfloat16)
    out_ref[...] = lax.dot_general(
        select, weighted, (((0,), (0,)), ((), ())), preferred_element_type=jnp.float32
    ).astype(out_ref.dtype)


def weigh(parts, select, gate):
    count = select.shape[1]
    columns = parts.shape[2]
    return pl.pallas_call(
        weigh_kernel,
        out_shape=jax.ShapeDtypeStruct((count, columns), jnp.bfloat16),
        compiler_params=pltpu.CompilerParams(vmem_limit_bytes=24 << 20),
        cost_estimate=pl.CostEstimate(
            flops=2 * count * select.shape[0] * columns,
            bytes_accessed=2 * parts.size + 2 * count * columns,
            transcendentals=0,
        ),
        name="weigh",
    )(parts, select, gate)


def local(tokens, router_weight, gate_weight, up_weight, down_weight, assignments, limits):
    local_rows = tokens.shape[0]
    experts = router_weight.shape[1]
    rings = lax.axis_size("y")
    shards = rings * CORES
    owners = lax.axis_size("exp")
    capacity = min(local_rows, max(2, 3 * local_rows * TOP // (2 * experts)))
    out_rows = local_rows // owners
    target = local_rows * shards * TOP / experts
    owner = lax.axis_index("exp")

    select, expert_rows = route(
        jnp.reshape(owner, (1,)).astype(jnp.int32), limits, assignments.T, tokens, capacity
    )
    rows = lax.all_gather(expert_rows, "y", axis=0, tiled=True)

    w_gate, w_up, w_down, tokens2, _ = lax.optimization_barrier(
        (gate_weight[0], up_weight[0], down_weight[0], tokens, expert_rows)
    )
    gate2, up2, down2 = swap_cores(w_gate), swap_cores(w_up), swap_cores(w_down)

    logits = lax.dot_general(
        router_weight, tokens2, (((0,), (1,)), ((), ())), preferred_element_type=jnp.float32
    )
    capped = SOFT_CAP * jnp.tanh(logits / SOFT_CAP)
    scores = lax.all_gather(capped, ("y", "core"), axis=0)
    weights = jnp.exp(scores)
    weights = weights * (TOP / jnp.sum(weights, axis=1, keepdims=True))
    for repeat in range(ITERS):
        weights = weights * (target / jnp.sum(weights, axis=(0, 2), keepdims=True))
        weights = weights * (TOP / jnp.sum(weights, axis=1, keepdims=True))
    shard = lax.axis_index("y") * CORES + lax.axis_index("core")
    own = lax.dynamic_slice(weights, (shard, owner, 0), (1, 1, local_rows))[0]

    hidden = ffn(rows, w_gate, w_up, gate2, up2)
    full_hidden = lax.all_gather(hidden, "tp", axis=0)
    partial = down(full_hidden, w_down, down2)
    parts = lax.all_to_all(partial.reshape(rings, capacity, partial.shape[1]), "y", 0, 0)
    shares = weigh(parts, select, own)
    shares = lax.all_to_all(shares.reshape(owners, out_rows, shares.shape[1]), "exp", 0, 0)
    return jnp.sum(shares.astype(jnp.float32), axis=0).astype(jnp.bfloat16)


def solution(mesh):
    shape = mesh.devices.shape
    fine = Mesh(
        mesh.devices.reshape((shape[0] // CORES, CORES) + shape[1:]), ("y", "core", "exp", "tp")
    )
    tok = ("y", "core")
    placed = (
        P(tok, None),
        P(),
        P("exp", None, tok + ("tp",)),
        P("exp", None, tok + ("tp",)),
        P("exp", tok, "tp"),
        P(tok, None),
        P(tok, None),
    )
    return jax.shard_map(
        local, mesh=fine, in_specs=placed, out_specs=P(tok + ("exp",), "tp"), check_vma=False
    )
```

time: 138 us -> 137 us (level)
  local copies, waits for them, and re-layouts: 3.41 us -> 6.7 us
  other arithmetic: 3.6 us -> 1.89 us
  Pallas kernels: 9.07 us -> 7.43 us
    unnamed x10 -> x20, local copies, waits for them, and re-layouts: 1.91 us -> 6.69 us
    pallas_call x2 -> x3, Pallas kernels: 8.8 us -> 7.14 us  [the longest x1 3.08 us: down(): pl.pallas_call(down_kernel, out_shape=jax.ShapeDtypeStruct((count, column...]
  transfers between devices with their start and end apart: 5 -> 5, of which waited for: 2 -> 2; matrix products, arithmetic and copies ran while one was open for 2% -> 2% of each run, Pallas kernels for 3% -> 2%
where the time goes in v2:
time: 137 us; the launch traced here: 136 us
  blocking collectives  52.1 us (38%)
  waiting for transfers between devices  41.9 us (31%)
  between operations  13.6 us (10%)
  starting transfers between devices  10.8 us (8%)
  Pallas kernels  7.43 us (5%)
  local copies, waits for them, and re-layouts  6.7 us (5%)
  other arithmetic  1.89 us (1%)
  matrix products  1.6 us (1%)
    all_gather x1, waiting for transfers between devices, local(): rows = lax.all_gather(expert_rows, 'y', axis=0, tiled=True)  22.1 us
    all_gather x1, blocking collectives, local(): scores = lax.all_gather(capped, ('y', 'core'), axis=0)  20.2 us
    all_to_all x1, waiting for transfers between devices, local(): lax.all_to_all(partial.reshape(rings, capacity, partial.shape[1]), 'y', 0...  19.8 us
    all_to_all x1, blocking collectives, local(): lax.all_to_all(shares.reshape(owners, out_rows, shares.shape[1]), 'exp',...  17.7 us
    all_gather x1, blocking collectives, local(): full_hidden = lax.all_gather(hidden, 'tp', axis=0)  14.3 us
    unnamed x20, local copies, waits for them, and re-layouts  6.69 us
    ppermute x3, starting transfers between devices, swap_cores(): return lax.ppermute(value, 'core', [(0, 1), (1, 0)])  6.25 us
    all_to_all x1, starting transfers between devices, local(): lax.all_to_all(partial.reshape(rings, capacity, partial.shape[1]), 'y', 0...  4.58 us
  transfers between devices with their start and end apart: 5, of which 2 were waited for; matrix products, arithmetic and copies ran while one was open for 2% of the time, Pallas kernels for 2%

profile of v2, /device:TPU:8, one launch (start us, length us, event | category | flops | bytes accessed | tf_op | source)
XLA Modules:
  0.0 136.0 jit_solution(6392497926989320227)
XLA Ops:
  6.5 1.3 copy-done.1
  7.8 0.7 copy-done.8
  8.5 0.7 copy-done.9
  9.1 1.7 %route.1 = (bf16[48,128]{1,0:T(8,128)(2,1)S(1)}, bf16[48,4096]{1,0:T(8,128)(2,1)}) custom-call(s32[1]{0:T(128)} %bitcast.owner_ref, s32[1,8]{1,0:T(1,128)S(1)} %copy-done.9, s32[2,128]{1,0:T(2,128)S(1)} %bitcast.44, bf16[128,4096]{1,0:T(8,128)(2,1)S(1)} %copy-done.1), custom_call_target="tpu_custom_call" | custom-call | flops 50331648 | bytes 1441792 | tf_op jit(solution)/shard_map/route/pallas_call | solution.py:41
  10.8 0.0 all-gather.4.cloned.1.call-update
  10.9 1.9 %collective-permute-start = (bf16[4096,128]{1,0:T(8,128)(2,1)}, bf16[4096,128]{1,0:T(8,128)(2,1)S(1)}, u32[]{:S(2)}, u32[]{:S(2)}) collective-permute-start(bf16[4096,128]{1,0:T(8,128)(2,1)} %bitcast.37), channel_id=1, source_target_pairs={{0,32},{32,0},{1,33},{33,1},{2,34},{34,2},{3,35},{35,3},{4,36},{36... | collective-permute-start | bytes 3145736 | tf_op jit(solution)/shard_map/ppermute | solution.py:15
  12.8 2.4 %collective-permute-start.1 = (bf16[4096,128]{1,0:T(8,128)(2,1)}, bf16[4096,128]{1,0:T(8,128)(2,1)S(1)}, u32[]{:S(2)}, u32[]{:S(2)}) collective-permute-start(bf16[4096,128]{1,0:T(8,128)(2,1)} %bitcast.39), channel_id=1, source_target_pairs={{0,32},{32,0},{1,33},{33,1},{2,34},{34,2},{3,35},{35,3},{4,36},{36... | collective-permute-start | bytes 3145736 | tf_op jit(solution)/shard_map/ppermute | solution.py:15
  15.2 1.9 %collective-permute-start.2 = (bf16[512,1024]{1,0:T(8,128)(2,1)}, bf16[512,1024]{1,0:T(8,128)(2,1)}, u32[]{:S(2)}, u32[]{:S(2)}) collective-permute-start(bf16[512,1024]{1,0:T(8,128)(2,1)} %bitcast.41), channel_id=1, source_target_pairs={{0,32},{32,0},{1,33},{33,1},{2,34},{34,2},{3,35},{35,3},{4,36},{36... | collective-permute-start | bytes 3145736 | tf_op jit(solution)/shard_map/ppermute | solution.py:15
  17.1 1.6 %fusion.2 = f32[8,128]{1,0:T(8,128)S(1)} fusion(bf16[128,4096]{1,0:T(8,128)(2,1)} %tokens_ref.1, bf16[4096,8]{0,1:T(8,128)(2,1)S(1)} %copy-done), kind=kOutput, calls=%fused_computation.3 | convolution fusion | flops 8390656 | bytes 1118208 | tf_op jit(solution)/shard_map/dot_general | solution.py:183
  18.7 20.2 %all-gather.1 = f32[128,128]{1,0:T(8,128)S(1)} all-gather(f32[8,128]{1,0:T(8,128)S(1)} %fusion.2), channel_id=3, replica_groups=mesh['y'=8,'core'=2,'exp'=8,'tp'=4] {'y','core'}, dimensions={0}, use_global_device_ids=true | all-gather | bytes 69632 | tf_op jit(solution)/shard_map/all_gather | solution.py:187
  39.0 0.1 fusion.4
  39.1 0.1 fusion.8
  39.2 0.2 multiply_reduce_fusion.2
  39.4 0.1 fusion.5
  39.6 0.2 multiply_reduce_fusion.1
  39.8 0.0 collective-permute-done.gate2_ref
  39.8 0.0 collective-permute-done.1.up2_ref
  39.8 1.0 copy-done.6
  40.8 22.1 %all-gather.4.cloned.1.call-done.rows_hbm = bf16[384,4096]{1,0:T(8,128)(2,1)} async-done(((bf16[48,4096]{1,0:T(8,128)(2,1)}), bf16[384,4096]{1,0:T(8,128)(2,1)}) %all-gather.4.cloned.1.call-update) | async-done | bytes 3145744 | tf_op jit(solution)/shard_map/all_gather | solution.py:176
  62.9 1.9 %copy-done.2 = bf16[384,4096]{1,0:T(8,128)(2,1)S(1)} copy-done((bf16[384,4096]{1,0:T(8,128)(2,1)S(1)}, bf16[384,4096]{1,0:T(8,128)(2,1)}, u32[]{:S(2)}) %copy-start.2) | copy-done | bytes 3145752
  64.7 1.2 copy-done.7
  66.0 2.4 %ffn.1 = bf16[384,256]{1,0:T(8,128)(2,1)S(1)} custom-call(bf16[384,4096]{1,0:T(8,128)(2,1)S(1)} %copy-done.2, bf16[4096,128]{1,0:T(8,128)(2,1)S(1)} %bitcast.38, bf16[4096,128]{1,0:T(8,128)(2,1)S(1)} %bitcast.40, bf16[4096,128]{1,0:T(8,128)(2,1)S(1)} %collective-permute-done.gate2_ref, bf16[4096,128]{1,0:T(8,128)(2,1)S(1)} %copy-done.7), custom_call_target="tpu_custom_call" | custom-call | flops 1610612736 | bytes 7340032 | tf_op jit(solution)/shard_map/ffn/pallas_call | solution.py:89
  68.3 14.3 %all-gather = bf16[1536,256]{1,0:T(8,128)(2,1)S(1)} all-gather(bf16[384,256]{1,0:T(8,128)(2,1)S(1)} %ffn.1), channel_id=2, replica_groups=mesh['y'=8,'core'=2,'exp'=8,'tp'=4] {'tp'}, dimensions={0}, use_global_device_ids=true | all-gather | bytes 983040 | tf_op jit(solution)/shard_map/all_gather | solution.py:197
  82.6 3.1 %down.1 = bf16[384,1024]{1,0:T(8,128)(2,1)} custom-call(bf16[4,384,256]{2,1,0:T(8,128)(2,1)S(1)} %bitcast.36, bf16[512,1024]{1,0:T(8,128)(2,1)S(1)} %bitcast.42, bf16[512,1024]{1,0:T(8,128)(2,1)} %collective-permute-done.2.down2_ref), custom_call_target="tpu_custom_call" | custom-call | flops 805306368 | bytes 3670016 | tf_op jit(solution)/shard_map/down/pallas_call | solution.py:123
  85.7 4.6 %all-to-all-start = ((bf16[8,48,1024]{2,1,0:T(8,128)(2,1)}), bf16[8,48,1024]{2,1,0:T(8,128)(2,1)S(1)}, u32[]{:S(2)}, u32[]{:S(2)}) async-start(bf16[8,48,1024]{2,1,0:T(8,128)(2,1)} %bitcast.6), calls=%async_computation | async-start | bytes 1572864 | tf_op jit(solution)/shard_map/all_to_all | solution.py:199
  90.3 0.1 fusion.6
  90.4 0.2 multiply_reduce_fusion
  90.6 0.1 fusion.9
  90.8 19.8 %all-to-all-done.parts_ref = bf16[8,48,1024]{2,1,0:T(8,128)(2,1)S(1)} async-done(((bf16[8,48,1024]{2,1,0:T(8,128)(2,1)}), bf16[8,48,1024]{2,1,0:T(8,128)(2,1)S(1)}, u32[]{:S(2)}, u32[]{:S(2)}) %all-to-all-start) | async-done | bytes 786464 | tf_op jit(solution)/shard_map/all_to_all | solution.py:199
  110.5 0.3 weigh.1
  110.8 17.7 %all_to_all.10 = bf16[8,16,1024]{2,1,0:T(8,128)(2,1)S(1)} all-to-all(bf16[8,16,1024]{2,1,0:T(8,128)(2,1)S(1)} %bitcast.43), channel_id=1, replica_groups=mesh['y'=8,'core'=2,'exp'=8,'tp'=4] {'exp'}, dimensions={0} | all-to-all | bytes 524288 | tf_op jit(solution)/shard_map/all_to_all | solution.py:201
  128.5 0.7 reduce_sum.102
  (28 shorter events, 0.1 us)
Async XLA Ops:
  6.5 10.6 %copy-start = (bf16[4096,8]{0,1:T(8,128)(2,1)S(1)}, bf16[4096,8]{0,1:T(8,128)(2,1)}, u32[]{:S(2)}) copy-start(bf16[4096,8]{0,1:T(8,128)(2,1)} %param.8) | copy-start | bytes 196612
  6.5 56.3 %all-gather.4.cloned.1.call-start = ((), (), s32[]{:S(2)}) async-start(), calls=%async_computation.2 | async-start | bytes 3538944 | tf_op jit(solution)/shard_map/all_gather | solution.py:176
  6.5 1.3 copy-start.1
  7.8 0.7 copy-start.8
  8.5 0.7 copy-start.9
  9.1 53.7 %copy-start.3 = (bf16[1,4096,128]{2,1,0:T(8,128)(2,1)S(1)}, bf16[1,4096,128]{2,1,0:T(8,128)(2,1)}, u32[]{:S(2)}) copy-start(bf16[1,4096,128]{2,1,0:T(8,128)(2,1)} %param.9) | copy-start | bytes 3145732
  9.1 53.7 %copy-start.4 = (bf16[1,4096,128]{2,1,0:T(8,128)(2,1)S(1)}, bf16[1,4096,128]{2,1,0:T(8,128)(2,1)}, u32[]{:S(2)}) copy-start(bf16[1,4096,128]{2,1,0:T(8,128)(2,1)} %param.10) | copy-start | bytes 3145732
  10.9 28.9 %collective-permute-start = (bf16[4096,128]{1,0:T(8,128)(2,1)}, bf16[4096,128]{1,0:T(8,128)(2,1)S(1)}, u32[]{:S(2)}, u32[]{:S(2)}) collective-permute-start(bf16[4096,128]{1,0:T(8,128)(2,1)} %bitcast.37), channel_id=1, source_target_pairs={{0,32},{32,0},{1,33},{33,1},{2,34},{34,2},{3,35},{35,3},{4,36},{36... | collective-permute-start | bytes 3145736 | tf_op jit(solution)/shard_map/ppermute | solution.py:15
  12.8 27.0 %collective-permute-start.1 = (bf16[4096,128]{1,0:T(8,128)(2,1)}, bf16[4096,128]{1,0:T(8,128)(2,1)S(1)}, u32[]{:S(2)}, u32[]{:S(2)}) collective-permute-start(bf16[4096,128]{1,0:T(8,128)(2,1)} %bitcast.39), channel_id=1, source_target_pairs={{0,32},{32,0},{1,33},{33,1},{2,34},{34,2},{3,35},{35,3},{4,36},{36... | collective-permute-start | bytes 3145736 | tf_op jit(solution)/shard_map/ppermute | solution.py:15
  15.2 67.4 %collective-permute-start.2 = (bf16[512,1024]{1,0:T(8,128)(2,1)}, bf16[512,1024]{1,0:T(8,128)(2,1)}, u32[]{:S(2)}, u32[]{:S(2)}) collective-permute-start(bf16[512,1024]{1,0:T(8,128)(2,1)} %bitcast.41), channel_id=1, source_target_pairs={{0,32},{32,0},{1,33},{33,1},{2,34},{34,2},{3,35},{35,3},{4,36},{36... | collective-permute-start | bytes 3145736 | tf_op jit(solution)/shard_map/ppermute | solution.py:15
  39.8 1.0 copy-start.6
  62.9 1.9 %copy-start.2 = (bf16[384,4096]{1,0:T(8,128)(2,1)S(1)}, bf16[384,4096]{1,0:T(8,128)(2,1)}, u32[]{:S(2)}) copy-start(bf16[384,4096]{1,0:T(8,128)(2,1)} %all-gather.4.cloned.1.call-done.rows_hbm) | copy-start | bytes 9437188
  64.7 1.2 copy-start.7
  66.0 16.6 %copy-start.5 = (bf16[1,512,1024]{2,1,0:T(8,128)(2,1)S(1)}, bf16[1,512,1024]{2,1,0:T(8,128)(2,1)}, u32[]{:S(2)}) copy-start(bf16[1,512,1024]{2,1,0:T(8,128)(2,1)} %param.11) | copy-start | bytes 3145732
  85.7 24.8 %all-to-all-start = ((bf16[8,48,1024]{2,1,0:T(8,128)(2,1)}), bf16[8,48,1024]{2,1,0:T(8,128)(2,1)S(1)}, u32[]{:S(2)}, u32[]{:S(2)}) async-start(bf16[8,48,1024]{2,1,0:T(8,128)(2,1)} %bitcast.6), calls=%async_computation | async-start | bytes 1572864 | tf_op jit(solution)/shard_map/all_to_all | solution.py:199
Sparse Core Ops, SparseCore 0:
  11.0 51.8 all-gather.3

commit v3 on v2

--- a/solution.py
+++ b/solution.py
@@ -9,13 +9,23 @@
 ITERS = 4
 SOFT_CAP = 8.0
 CORES = 2
+VMEM_BYTES = 64 << 20
 
 
 def swap_cores(value):
     return lax.ppermute(value, "core", [(0, 1), (1, 0)])
 
 
-def route_kernel(owner_ref, limits_ref, assign_ref, tokens_ref, select_ref, rows_ref):
+def route_kernel(owner_ref, limits_ref, assign_ref, tokens_hbm, select_ref, rows_ref, tokens_ref, sems):
+    width = tokens_ref.shape[1]
+    chunks = sems.shape[0]
+    parts = [pl.ds(index * (width // chunks), width // chunks) for index in range(chunks)]
+    copies = [
+        pltpu.make_async_copy(tokens_hbm.at[:, part], tokens_ref.at[:, part], sems.at[index])
+        for index, part in enumerate(parts)
+    ]
+    for copy in copies:
+        copy.start()
     owner = owner_ref[0]
     count = assign_ref.shape[1]
     capacity = select_ref.shape[0]
@@ -29,24 +39,30 @@
     slot_ids = lax.broadcasted_iota(jnp.int32, (capacity, count), 0)
     select = jnp.where(slot_ids == slot, 1.0, 0.0).astype(jnp.bfloat16)
     select_ref[...] = select
-    rows_ref[...] = jnp.dot(
-        select, tokens_ref[...], preferred_element_type=jnp.float32
-    ).astype(rows_ref.dtype)
-
-
-def route(owner, limits, assignments, tokens, capacity):
+    for copy, part in zip(copies, parts):
+        copy.wait()
+        rows_ref[:, part] = jnp.dot(
+            select, tokens_ref[:, part], preferred_element_type=jnp.float32
+        ).astype(rows_ref.dtype)
+
+
+def route(owner, limits, assignments, tokens, capacity, chunks=4):
     count, width = tokens.shape
     whole = pl.BlockSpec(memory_space=pltpu.VMEM)
     scalars = pl.BlockSpec(memory_space=pltpu.SMEM)
     return pl.pallas_call(
         route_kernel,
-        in_specs=[scalars, scalars, whole, whole],
+        in_specs=[scalars, scalars, whole, pl.BlockSpec(memory_space=pltpu.HBM)],
         out_specs=[whole, whole],
         out_shape=[
             jax.ShapeDtypeStruct((capacity, count), jnp.bfloat16),
             jax.ShapeDtypeStruct((capacity, width), jnp.bfloat16),
         ],
-        compiler_params=pltpu.CompilerParams(vmem_limit_bytes=16 << 20),
+        scratch_shapes=[
+            pltpu.VMEM((count, width), jnp.bfloat16),
+            pltpu.SemaphoreType.DMA((chunks,)),
+        ],
+        compiler_params=pltpu.CompilerParams(vmem_limit_bytes=VMEM_BYTES),
         cost_estimate=pl.CostEstimate(
             flops=2 * capacity * count * width,
             bytes_accessed=2 * (count + capacity) * width,
@@ -56,46 +72,56 @@
     )(owner, limits, assignments, tokens)
 
 
-def ffn_kernel(rows_hbm, gate_ref, up_ref, gate2_ref, up2_ref, out_ref, rows_ref, sems):
-    chunks, _, chunk = rows_ref.shape
-    copies = [
-        pltpu.make_async_copy(
-            rows_hbm.at[:, pl.ds(index * chunk, chunk)], rows_ref.at[index], sems.at[index]
-        )
-        for index in range(chunks)
-    ]
-    for copy in copies:
-        copy.start()
-    units = gate_ref.shape[1]
-    totals = [None, None]
+def ffn_kernel(rows_hbm, gate_hbm, up_hbm, gate2_hbm, up2_hbm, out_ref, rows_ref, weight_ref, sems):
+    chunks, chunk, width = weight_ref.shape
+    units = width // 4
+    copies = []
     for index in range(chunks):
-        copies[index].wait()
-        rows = rows_ref[index]
         part = pl.ds(index * chunk, chunk)
-        for side, (gate, up) in enumerate(((gate_ref, up_ref), (gate2_ref, up2_ref))):
-            both = jnp.concatenate([gate[part, :], up[part, :]], axis=1)
-            product = jnp.dot(rows, both, preferred_element_type=jnp.float32)
-            totals[side] = product if index == 0 else totals[side] + product
-    for side, total in enumerate(totals):
-        gate = total[:, :units]
-        hidden = gate / (1.0 + jnp.exp(-gate)) * total[:, units:]
+        ends = [(rows_hbm.at[:, part], rows_ref.at[index])]
+        for place, ref in enumerate((gate_hbm, up_hbm, gate2_hbm, up2_hbm)):
+            ends.append(
+                (ref.at[part, :], weight_ref.at[index, :, pl.ds(place * units, units)])
+            )
+        copies.append(
+            [
+                pltpu.make_async_copy(source, sink, sems.at[index, place])
+                for place, (source, sink) in enumerate(ends)
+            ]
+        )
+    for group in copies:
+        for copy in group:
+            copy.start()
+    total = None
+    for index, group in enumerate(copies):
+        for copy in group:
+            copy.wait()
+        product = jnp.dot(
+            rows_ref[index], weight_ref[index], preferred_element_type=jnp.float32
+        )
+        total = product if index == 0 else total + product
+    for side in range(2):
+        gate = total[:, 2 * side * units : (2 * side + 1) * units]
+        up = total[:, (2 * side + 1) * units : (2 * side + 2) * units]
+        hidden = gate / (1.0 + jnp.exp(-gate)) * up
         out_ref[:, side * units : (side + 1) * units] = hidden.astype(out_ref.dtype)
 
 
 def ffn(rows, gate, up, gate2, up2, chunk=1024):
     count, width = rows.shape
     units = gate.shape[1]
-    whole = pl.BlockSpec(memory_space=pltpu.VMEM)
+    chunks = width // chunk
     return pl.pallas_call(
         ffn_kernel,
-        in_specs=[pl.BlockSpec(memory_space=pltpu.HBM)] + [whole] * 4,
-        out_specs=whole,
+        in_specs=[pl.BlockSpec(memory_space=pltpu.HBM)] * 5,
+        out_specs=pl.BlockSpec(memory_space=pltpu.VMEM),
         out_shape=jax.ShapeDtypeStruct((count, 2 * units), jnp.bfloat16),
         scratch_shapes=[
-            pltpu.VMEM((width // chunk, count, chunk), jnp.bfloat16),
-            pltpu.SemaphoreType.DMA((width // chunk,)),
-        ],
-        compiler_params=pltpu.CompilerParams(vmem_limit_bytes=32 << 20),
+            pltpu.VMEM((chunks, count, chunk), jnp.bfloat16),
+            pltpu.VMEM((chunks, chunk, 4 * units), jnp.bfloat16),
+            pltpu.SemaphoreType.DMA((chunks, 5)),
+        ],
+        compiler_params=pltpu.CompilerParams(vmem_limit_bytes=VMEM_BYTES),
         cost_estimate=pl.CostEstimate(
             flops=8 * count * width * units,
             bytes_accessed=2 * count * width + 8 * width * units,
@@ -105,14 +131,33 @@
     )(rows, gate, up, gate2, up2)
 
 
-def down_kernel(hidden_ref, down_ref, down2_ref, out_ref):
-    parts = hidden_ref.shape[0]
-    units = down_ref.shape[0] // parts
+def down_kernel(hidden_hbm, down_hbm, down2_hbm, out_ref, hidden_ref, weight_ref, sems):
+    parts, count, units = hidden_ref.shape
+    half = units // 2
+    copies = []
+    for index in range(parts):
+        part = pl.ds(index * half, half)
+        ends = (
+            (hidden_hbm.at[index], hidden_ref.at[index]),
+            (down_hbm.at[part, :], weight_ref.at[index, pl.ds(0, half), :]),
+            (down2_hbm.at[part, :], weight_ref.at[index, pl.ds(half, half), :]),
+        )
+        copies.append(
+            [
+                pltpu.make_async_copy(source, sink, sems.at[index, place])
+                for place, (source, sink) in enumerate(ends)
+            ]
+        )
+    for group in copies:
+        for copy in group:
+            copy.start()
     total = None
-    for index in range(parts):
-        part = pl.ds(index * units, units)
-        both = jnp.concatenate([down_ref[part, :], down2_ref[part, :]], axis=0)
-        product = jnp.dot(hidden_ref[index], both, preferred_element_type=jnp.float32)
+    for index, group in enumerate(copies):
+        for copy in group:
+            copy.wait()
+        product = jnp.dot(
+            hidden_ref[index], weight_ref[index], preferred_element_type=jnp.float32
+        )
         total = product if index == 0 else total + product
     out_ref[...] = total.astype(out_ref.dtype)
 
@@ -122,8 +167,15 @@
     columns = weight.shape[1]
     return pl.pallas_call(
         down_kernel,
+        in_specs=[pl.BlockSpec(memory_space=pltpu.HBM)] * 3,
+        out_specs=pl.BlockSpec(memory_space=pltpu.VMEM),
         out_shape=jax.ShapeDtypeStruct((count, columns), jnp.bfloat16),
-        compiler_params=pltpu.CompilerParams(vmem_limit_bytes=24 << 20),
+        scratch_shapes=[
+            pltpu.VMEM((parts, count, units), jnp.bfloat16),
+            pltpu.VMEM((parts, units, columns), jnp.bfloat16),
+            pltpu.SemaphoreType.DMA((parts, 3)),
+        ],
+        compiler_params=pltpu.CompilerParams(vmem_limit_bytes=VMEM_BYTES),
         cost_estimate=pl.CostEstimate(
             flops=2 * parts * count * units * columns,
             bytes_accessed=2 * parts * units * (count + columns) + 2 * count * columns,
@@ -149,7 +201,7 @@
     return pl.pallas_call(
         weigh_kernel,
         out_shape=jax.ShapeDtypeStruct((count, columns), jnp.bfloat16),
-        compiler_params=pltpu.CompilerParams(vmem_limit_bytes=24 << 20),
+        compiler_params=pltpu.CompilerParams(vmem_limit_bytes=VMEM_BYTES),
         cost_estimate=pl.CostEstimate(
             flops=2 * count * select.shape[0] * columns,
             bytes_accessed=2 * parts.size + 2 * count * columns,
@@ -184,6 +236,11 @@
         router_weight, tokens2, (((0,), (1,)), ((), ())), preferred_element_type=jnp.float32
     )
     capped = SOFT_CAP * jnp.tanh(logits / SOFT_CAP)
+    hidden = ffn(rows, w_gate, w_up, gate2, up2)
+    full_hidden = lax.all_gather(hidden, "tp", axis=0)
+    partial = down(full_hidden, w_down, down2)
+    capped, partial = lax.optimization_barrier((capped, partial))
+    parts = lax.all_to_all(partial.reshape(rings, capacity, partial.shape[1]), "y", 0, 0)
     scores = lax.all_gather(capped, ("y", "core"), axis=0)
     weights = jnp.exp(scores)
     weights = weights * (TOP / jnp.sum(weights, axis=1, keepdims=True))
@@ -193,10 +250,6 @@
     shard = lax.axis_index("y") * CORES + lax.axis_index("core")
     own = lax.dynamic_slice(weights, (shard, owner, 0), (1, 1, local_rows))[0]
 
-    hidden = ffn(rows, w_gate, w_up, gate2, up2)
-    full_hidden = lax.all_gather(hidden, "tp", axis=0)
-    partial = down(full_hidden, w_down, down2)
-    parts = lax.all_to_all(partial.reshape(rings, capacity, partial.shape[1]), "y", 0, 0)
     shares = weigh(parts, select, own)
     shares = lax.all_to_all(shares.reshape(owners, out_rows, shares.shape[1]), "exp", 0, 0)
     return jnp.sum(shares.astype(jnp.float32), axis=0).astype(jnp.bfloat16)

time: 137 us -> 151 us (1.10)
  the two profiles are of different devices: /device:TPU:8 before, /device:TPU:1 now
where the time goes in v3:
time: 151 us
  blocking collectives  63.9 us (42%)
  waiting for transfers between devices  37.2 us (25%)
  starting transfers between devices  17.8 us (12%)
  Pallas kernels  13.5 us (9%)
  between operations  13.5 us (9%)
  other arithmetic  2.43 us (2%)
  matrix products  2.21 us (1%)
    all_gather x1, waiting for transfers between devices, local(): rows = lax.all_gather(expert_rows, 'y', axis=0, tiled=True)  37.1 us
    all_gather x1, blocking collectives, local(): scores = lax.all_gather(capped, ('y', 'core'), axis=0)  31.3 us
    all_to_all x1, blocking collectives, local(): lax.all_to_all(shares.reshape(owners, out_rows, shares.shape[1]), 'exp',...  19.4 us
    all_gather x1, blocking collectives, local(): full_hidden = lax.all_gather(hidden, 'tp', axis=0)  13.2 us
    ppermute x3, starting transfers between devices, swap_cores(): return lax.ppermute(value, 'core', [(0, 1), (1, 0)])  13.1 us
    pallas_call x1, Pallas kernels, ffn(): pl.pallas_call(ffn_kernel, in_specs=[pl.BlockSpec(memory_space=pltpu.HBM)...  4.75 us
    all_to_all x1, starting transfers between devices, local(): lax.all_to_all(partial.reshape(rings, capacity, partial.shape[1]), 'y', 0...  4.67 us
    pallas_call x1, Pallas kernels, down(): pl.pallas_call(down_kernel, in_specs=[pl.BlockSpec(memory_space=pltpu.HBM...  3.42 us
  transfers between devices with their start and end apart: 5, of which 1 were waited for; matrix products, arithmetic and copies ran while one was open for 3% of the time, Pallas kernels for 3%

profile of v3, /device:TPU:1, one launch (start us, length us, event | category | flops | bytes accessed | tf_op | source)
XLA Modules:
  0.0 150.5 jit_solution(1430341749618894643)
XLA Ops:
  6.5 0.0 all-gather.4.cloned.1.call-start
  6.5 3.1 %route.1 = (bf16[48,128]{1,0:T(8,128)(2,1)}, bf16[48,4096]{1,0:T(8,128)(2,1)}) custom-call(s32[1]{0:T(128)} %bitcast.3.owner_ref, s32[1,8]{1,0:T(1,128)} %limits_ref.1, s32[2,128]{1,0:T(2,128)} %bitcast.45, bf16[128,4096]{1,0:T(8,128)(2,1)} %tokens_hbm.1), custom_call_target="tpu_custom_call" | custom-call | flops 50331648 | bytes 1441792 | tf_op jit(solution)/shard_map/route/pallas_call | solution.py:53
  9.7 0.0 all-gather.4.cloned.1.call-update
  9.7 8.8 %collective-permute-start = (bf16[4096,128]{1,0:T(8,128)(2,1)}, bf16[4096,128]{1,0:T(8,128)(2,1)}, u32[]{:S(2)}, u32[]{:S(2)}) collective-permute-start(bf16[4096,128]{1,0:T(8,128)(2,1)} %bitcast.38), channel_id=1, source_target_pairs={{0,32},{32,0},{1,33},{33,1},{2,34},{34,2},{3,35},{35,3},{4,36},{36... | collective-permute-start | bytes 3145736 | tf_op jit(solution)/shard_map/ppermute | solution.py:16
  18.5 1.9 %collective-permute-start.1 = (bf16[4096,128]{1,0:T(8,128)(2,1)}, bf16[4096,128]{1,0:T(8,128)(2,1)}, u32[]{:S(2)}, u32[]{:S(2)}) collective-permute-start(bf16[4096,128]{1,0:T(8,128)(2,1)} %bitcast.40), channel_id=1, source_target_pairs={{0,32},{32,0},{1,33},{33,1},{2,34},{34,2},{3,35},{35,3},{4,36},{36... | collective-permute-start | bytes 3145736 | tf_op jit(solution)/shard_map/ppermute | solution.py:16
  20.4 2.4 %collective-permute-start.2 = (bf16[512,1024]{1,0:T(8,128)(2,1)}, bf16[512,1024]{1,0:T(8,128)(2,1)}, u32[]{:S(2)}, u32[]{:S(2)}) collective-permute-start(bf16[512,1024]{1,0:T(8,128)(2,1)} %bitcast.42), channel_id=1, source_target_pairs={{0,32},{32,0},{1,33},{33,1},{2,34},{34,2},{3,35},{35,3},{4,36},{36... | collective-permute-start | bytes 3145736 | tf_op jit(solution)/shard_map/ppermute | solution.py:16
  22.9 2.2 %fusion.2 = f32[8,128]{1,0:T(8,128)} fusion(bf16[128,4096]{1,0:T(8,128)(2,1)} %tokens_hbm.1, bf16[4096,8]{0,1:T(8,128)(2,1)} %param.8), kind=kOutput, calls=%fused_computation.3 | convolution fusion | flops 8390656 | bytes 1118208 | tf_op jit(solution)/shard_map/dot_general | solution.py:235
  25.1 0.0 collective-permute-done.gate2_hbm
  25.1 0.0 collective-permute-done.1.up2_hbm
  25.1 37.1 %all-gather.4.cloned.1.call-done.rows_hbm = bf16[384,4096]{1,0:T(8,128)(2,1)} async-done(((bf16[48,4096]{1,0:T(8,128)(2,1)}), bf16[384,4096]{1,0:T(8,128)(2,1)}) %all-gather.4.cloned.1.call-update) | async-done | bytes 3145744 | tf_op jit(solution)/shard_map/all_gather | solution.py:228
  62.2 4.8 %ffn.1 = bf16[384,256]{1,0:T(8,128)(2,1)} custom-call(bf16[384,4096]{1,0:T(8,128)(2,1)} %all-gather.4.cloned.1.call-done.rows_hbm, bf16[4096,128]{1,0:T(8,128)(2,1)} %bitcast.39, bf16[4096,128]{1,0:T(8,128)(2,1)} %bitcast.41, bf16[4096,128]{1,0:T(8,128)(2,1)} %collective-permute-done.gate2_hbm, bf16[4096,128]{1,0:T(8,128)(2,1)} %collective-permute-done.1.up2_hbm), custom_call_target="tpu_custom_call" | custom-call | flops 1610612736 | bytes 7340032 | tf_op jit(solution)/shard_map/ffn/pallas_call | solution.py:114
  67.0 13.2 %all-gather = bf16[1536,256]{1,0:T(8,128)(2,1)} all-gather(bf16[384,256]{1,0:T(8,128)(2,1)} %ffn.1), channel_id=2, replica_groups=mesh['y'=8,'core'=2,'exp'=8,'tp'=4] {'tp'}, dimensions={0}, use_global_device_ids=true | all-gather | bytes 983040 | tf_op jit(solution)/shard_map/all_gather | solution.py:240
  80.2 0.0 collective-permute-done.2.down2_hbm
  80.2 3.4 %down.1 = bf16[384,1024]{1,0:T(8,128)(2,1)} custom-call(bf16[4,384,256]{2,1,0:T(8,128)(2,1)} %bitcast.37, bf16[512,1024]{1,0:T(8,128)(2,1)} %bitcast.43, bf16[512,1024]{1,0:T(8,128)(2,1)} %collective-permute-done.2.down2_hbm), custom_call_target="tpu_custom_call" | custom-call | flops 805306368 | bytes 3670016 | tf_op jit(solution)/shard_map/down/pallas_call | solution.py:168
  83.6 4.7 %all-to-all-start = ((bf16[8,48,1024]{2,1,0:T(8,128)(2,1)}), bf16[8,48,1024]{2,1,0:T(8,128)(2,1)}, u32[]{:S(2)}, u32[]{:S(2)}) async-start(bf16[8,48,1024]{2,1,0:T(8,128)(2,1)} %bitcast.36), calls=%async_computation | async-start | bytes 1572864 | tf_op jit(solution)/shard_map/all_to_all | solution.py:243
  88.3 31.3 %all-gather.1 = f32[128,128]{1,0:T(8,128)S(1)} all-gather(f32[8,128]{1,0:T(8,128)} %fusion.2), channel_id=3, replica_groups=mesh['y'=8,'core'=2,'exp'=8,'tp'=4] {'y','core'}, dimensions={0}, use_global_device_ids=true | all-gather | bytes 69632 | tf_op jit(solution)/shard_map/all_gather | solution.py:244
  119.7 0.1 fusion.4
  119.9 0.1 fusion.8
  120.0 0.2 multiply_reduce_fusion.2
  120.2 0.1 fusion.5
  120.3 0.2 multiply_reduce_fusion.1
  120.5 0.1 fusion.6
  120.6 0.2 multiply_reduce_fusion
  120.8 0.1 fusion.9
  121.0 0.6 fusion.7.gate_ref
  121.5 0.0 all-to-all-done.parts_ref
  121.5 2.1 %weigh.1 = bf16[128,1024]{1,0:T(8,128)(2,1)} custom-call(bf16[8,48,1024]{2,1,0:T(8,128)(2,1)} %all-to-all-done.parts_ref, bf16[48,128]{1,0:T(8,128)(2,1)} %get-tuple-element.19.select_ref, f32[1,128]{1,0:T(1,128)} %fusion.7.gate_ref), custom_call_target="tpu_custom_call" | custom-call | flops 12582912 | bytes 1048576 | tf_op jit(solution)/shard_map/weigh/pallas_call | solution.py:201
  123.7 19.4 %all_to_all.10 = bf16[8,16,1024]{2,1,0:T(8,128)(2,1)S(1)} all-to-all(bf16[8,16,1024]{2,1,0:T(8,128)(2,1)} %bitcast.44), channel_id=1, replica_groups=mesh['y'=8,'core'=2,'exp'=8,'tp'=4] {'exp'}, dimensions={0} | all-to-all | bytes 524288 | tf_op jit(solution)/shard_map/all_to_all | solution.py:254
  143.0 0.7 reduce_sum.102
  (11 shorter events, 0.1 us)
Async XLA Ops:
  6.5 55.7 %all-gather.4.cloned.1.call-start = ((), (), s32[]{:S(2)}) async-start(), calls=%async_computation.2 | async-start | bytes 3538944 | tf_op jit(solution)/shard_map/all_gather | solution.py:228
  9.7 15.4 %collective-permute-start = (bf16[4096,128]{1,0:T(8,128)(2,1)}, bf16[4096,128]{1,0:T(8,128)(2,1)}, u32[]{:S(2)}, u32[]{:S(2)}) collective-permute-start(bf16[4096,128]{1,0:T(8,128)(2,1)} %bitcast.38), channel_id=1, source_target_pairs={{0,32},{32,0},{1,33},{33,1},{2,34},{34,2},{3,35},{35,3},{4,36},{36... | collective-permute-start | bytes 3145736 | tf_op jit(solution)/shard_map/ppermute | solution.py:16
  18.5 6.6 %collective-permute-start.1 = (bf16[4096,128]{1,0:T(8,128)(2,1)}, bf16[4096,128]{1,0:T(8,128)(2,1)}, u32[]{:S(2)}, u32[]{:S(2)}) collective-permute-start(bf16[4096,128]{1,0:T(8,128)(2,1)} %bitcast.40), channel_id=1, source_target_pairs={{0,32},{32,0},{1,33},{33,1},{2,34},{34,2},{3,35},{35,3},{4,36},{36... | collective-permute-start | bytes 3145736 | tf_op jit(solution)/shard_map/ppermute | solution.py:16
  20.4 59.8 %collective-permute-start.2 = (bf16[512,1024]{1,0:T(8,128)(2,1)}, bf16[512,1024]{1,0:T(8,128)(2,1)}, u32[]{:S(2)}, u32[]{:S(2)}) collective-permute-start(bf16[512,1024]{1,0:T(8,128)(2,1)} %bitcast.42), channel_id=1, source_target_pairs={{0,32},{32,0},{1,33},{33,1},{2,34},{34,2},{3,35},{35,3},{4,36},{36... | collective-permute-start | bytes 3145736 | tf_op jit(solution)/shard_map/ppermute | solution.py:16
  83.6 37.9 %all-to-all-start = ((bf16[8,48,1024]{2,1,0:T(8,128)(2,1)}), bf16[8,48,1024]{2,1,0:T(8,128)(2,1)}, u32[]{:S(2)}, u32[]{:S(2)}) async-start(bf16[8,48,1024]{2,1,0:T(8,128)(2,1)} %bitcast.36), calls=%async_computation | async-start | bytes 1572864 | tf_op jit(solution)/shard_map/all_to_all | solution.py:243
Sparse Core Ops, SparseCore 0:
  9.8 52.3 all-gather.3

commit v4 on v3

--- a/solution.py
+++ b/solution.py
@@ -9,60 +9,80 @@
 ITERS = 4
 SOFT_CAP = 8.0
 CORES = 2
-VMEM_BYTES = 64 << 20
+ALL_VMEM = 64 << 20
 
 
 def swap_cores(value):
     return lax.ppermute(value, "core", [(0, 1), (1, 0)])
 
 
-def route_kernel(owner_ref, limits_ref, assign_ref, tokens_hbm, select_ref, rows_ref, tokens_ref, sems):
+def route_kernel(
+    owner_ref, limits_hbm, assign_hbm, tokens_hbm, select_ref, rows_hbm,
+    limits_ref, assign_ref, tokens_ref, rows_ref, sems, out_sems
+):
     width = tokens_ref.shape[1]
-    chunks = sems.shape[0]
+    chunks = out_sems.shape[0]
     parts = [pl.ds(index * (width // chunks), width // chunks) for index in range(chunks)]
+    small = [
+        pltpu.make_async_copy(limits_hbm, limits_ref, sems.at[chunks]),
+        pltpu.make_async_copy(assign_hbm, assign_ref, sems.at[chunks + 1]),
+    ]
     copies = [
         pltpu.make_async_copy(tokens_hbm.at[:, part], tokens_ref.at[:, part], sems.at[index])
         for index, part in enumerate(parts)
     ]
-    for copy in copies:
+    for copy in small + copies:
         copy.start()
     owner = owner_ref[0]
-    count = assign_ref.shape[1]
-    capacity = select_ref.shape[0]
-    hit = jnp.sum(jnp.where(assign_ref[...] == owner, 1.0, 0.0), axis=0, keepdims=True)
+    capacity, count = select_ref.shape
     row = lax.broadcasted_iota(jnp.int32, (count, count), 0)
     column = lax.broadcasted_iota(jnp.int32, (count, count), 1)
     earlier = jnp.where(row < column, 1.0, 0.0).astype(jnp.bfloat16)
+    slot_ids = lax.broadcasted_iota(jnp.int32, (capacity, count), 0)
+    for copy in small:
+        copy.wait()
+    hit = jnp.sum(jnp.where(assign_ref[...] == owner, 1.0, 0.0), axis=0, keepdims=True)
     named = jnp.broadcast_to(hit, (16, count)).astype(jnp.bfloat16)
     slot = jnp.dot(named, earlier, preferred_element_type=jnp.float32)[:1].astype(jnp.int32)
     slot = jnp.where((hit > 0.0) & (slot < limits_ref[0, owner]), slot, -1)
-    slot_ids = lax.broadcasted_iota(jnp.int32, (capacity, count), 0)
     select = jnp.where(slot_ids == slot, 1.0, 0.0).astype(jnp.bfloat16)
     select_ref[...] = select
-    for copy, part in zip(copies, parts):
-        copy.wait()
+    outs = []
+    for index, part in enumerate(parts):
+        copies[index].wait()
         rows_ref[:, part] = jnp.dot(
             select, tokens_ref[:, part], preferred_element_type=jnp.float32
         ).astype(rows_ref.dtype)
+        outs.append(
+            pltpu.make_async_copy(
+                rows_ref.at[:, part], rows_hbm.at[:, part], out_sems.at[index]
+            )
+        )
+        outs[-1].start()
+    for copy in outs:
+        copy.wait()
 
 
 def route(owner, limits, assignments, tokens, capacity, chunks=4):
     count, width = tokens.shape
-    whole = pl.BlockSpec(memory_space=pltpu.VMEM)
-    scalars = pl.BlockSpec(memory_space=pltpu.SMEM)
+    far = pl.BlockSpec(memory_space=pltpu.HBM)
     return pl.pallas_call(
         route_kernel,
-        in_specs=[scalars, scalars, whole, pl.BlockSpec(memory_space=pltpu.HBM)],
-        out_specs=[whole, whole],
+        in_specs=[pl.BlockSpec(memory_space=pltpu.SMEM), far, far, far],
+        out_specs=[pl.BlockSpec(memory_space=pltpu.VMEM), far],
         out_shape=[
             jax.ShapeDtypeStruct((capacity, count), jnp.bfloat16),
             jax.ShapeDtypeStruct((capacity, width), jnp.bfloat16),
         ],
         scratch_shapes=[
+            pltpu.SMEM(limits.shape, jnp.int32),
+            pltpu.VMEM(assignments.shape, jnp.int32),
             pltpu.VMEM((count, width), jnp.bfloat16),
+            pltpu.VMEM((capacity, width), jnp.bfloat16),
+            pltpu.SemaphoreType.DMA((chunks + 2,)),
             pltpu.SemaphoreType.DMA((chunks,)),
         ],
-        compiler_params=pltpu.CompilerParams(vmem_limit_bytes=VMEM_BYTES),
+        compiler_params=pltpu.CompilerParams(vmem_limit_bytes=ALL_VMEM),
         cost_estimate=pl.CostEstimate(
             flops=2 * capacity * count * width,
             bytes_accessed=2 * (count + capacity) * width,
@@ -107,7 +127,7 @@
         out_ref[:, side * units : (side + 1) * units] = hidden.astype(out_ref.dtype)
 
 
-def ffn(rows, gate, up, gate2, up2, chunk=1024):
+def ffn(rows, gate, up, gate2, up2, chunk=512):
     count, width = rows.shape
     units = gate.shape[1]
     chunks = width // chunk
@@ -121,7 +141,7 @@
             pltpu.VMEM((chunks, chunk, 4 * units), jnp.bfloat16),
             pltpu.SemaphoreType.DMA((chunks, 5)),
         ],
-        compiler_params=pltpu.CompilerParams(vmem_limit_bytes=VMEM_BYTES),
+        compiler_params=pltpu.CompilerParams(vmem_limit_bytes=ALL_VMEM),
         cost_estimate=pl.CostEstimate(
             flops=8 * count * width * units,
             bytes_accessed=2 * count * width + 8 * width * units,
@@ -131,33 +151,14 @@
     )(rows, gate, up, gate2, up2)
 
 
-def down_kernel(hidden_hbm, down_hbm, down2_hbm, out_ref, hidden_ref, weight_ref, sems):
-    parts, count, units = hidden_ref.shape
-    half = units // 2
-    copies = []
+def down_kernel(hidden_ref, down_ref, down2_ref, out_ref):
+    parts = hidden_ref.shape[0]
+    units = down_ref.shape[0] // parts
+    total = None
     for index in range(parts):
-        part = pl.ds(index * half, half)
-        ends = (
-            (hidden_hbm.at[index], hidden_ref.at[index]),
-            (down_hbm.at[part, :], weight_ref.at[index, pl.ds(0, half), :]),
-            (down2_hbm.at[part, :], weight_ref.at[index, pl.ds(half, half), :]),
-        )
-        copies.append(
-            [
-                pltpu.make_async_copy(source, sink, sems.at[index, place])
-                for place, (source, sink) in enumerate(ends)
-            ]
-        )
-    for group in copies:
-        for copy in group:
-            copy.start()
-    total = None
-    for index, group in enumerate(copies):
-        for copy in group:
-            copy.wait()
-        product = jnp.dot(
-            hidden_ref[index], weight_ref[index], preferred_element_type=jnp.float32
-        )
+        part = pl.ds(index * units, units)
+        both = jnp.concatenate([down_ref[part, :], down2_ref[part, :]], axis=0)
+        product = jnp.dot(hidden_ref[index], both, preferred_element_type=jnp.float32)
         total = product if index == 0 else total + product
     out_ref[...] = total.astype(out_ref.dtype)
 
@@ -167,15 +168,8 @@
     columns = weight.shape[1]
     return pl.pallas_call(
         down_kernel,
-        in_specs=[pl.BlockSpec(memory_space=pltpu.HBM)] * 3,
-        out_specs=pl.BlockSpec(memory_space=pltpu.VMEM),
         out_shape=jax.ShapeDtypeStruct((count, columns), jnp.bfloat16),
-        scratch_shapes=[
-            pltpu.VMEM((parts, count, units), jnp.bfloat16),
-            pltpu.VMEM((parts, units, columns), jnp.bfloat16),
-            pltpu.SemaphoreType.DMA((parts, 3)),
-        ],
-        compiler_params=pltpu.CompilerParams(vmem_limit_bytes=VMEM_BYTES),
+        compiler_params=pltpu.CompilerParams(vmem_limit_bytes=24 << 20),
         cost_estimate=pl.CostEstimate(
             flops=2 * parts * count * units * columns,
             bytes_accessed=2 * parts * units * (count + columns) + 2 * count * columns,
@@ -201,7 +195,7 @@
     return pl.pallas_call(
         weigh_kernel,
         out_shape=jax.ShapeDtypeStruct((count, columns), jnp.bfloat16),
-        compiler_params=pltpu.CompilerParams(vmem_limit_bytes=VMEM_BYTES),
+        compiler_params=pltpu.CompilerParams(vmem_limit_bytes=24 << 20),
         cost_estimate=pl.CostEstimate(
             flops=2 * count * select.shape[0] * columns,
             bytes_accessed=2 * parts.size + 2 * count * columns,
@@ -236,11 +230,6 @@
         router_weight, tokens2, (((0,), (1,)), ((), ())), preferred_element_type=jnp.float32
     )
     capped = SOFT_CAP * jnp.tanh(logits / SOFT_CAP)
-    hidden = ffn(rows, w_gate, w_up, gate2, up2)
-    full_hidden = lax.all_gather(hidden, "tp", axis=0)
-    partial = down(full_hidden, w_down, down2)
-    capped, partial = lax.optimization_barrier((capped, partial))
-    parts = lax.all_to_all(partial.reshape(rings, capacity, partial.shape[1]), "y", 0, 0)
     scores = lax.all_gather(capped, ("y", "core"), axis=0)
     weights = jnp.exp(scores)
     weights = weights * (TOP / jnp.sum(weights, axis=1, keepdims=True))
@@ -250,6 +239,10 @@
     shard = lax.axis_index("y") * CORES + lax.axis_index("core")
     own = lax.dynamic_slice(weights, (shard, owner, 0), (1, 1, local_rows))[0]
 
+    hidden = ffn(rows, w_gate, w_up, gate2, up2)
+    full_hidden = lax.all_gather(hidden, "tp", axis=0)
+    partial = down(full_hidden, w_down, down2)
+    parts = lax.all_to_all(partial.reshape(rings, capacity, partial.shape[1]), "y", 0, 0)
     shares = weigh(parts, select, own)
     shares = lax.all_to_all(shares.reshape(owners, out_rows, shares.shape[1]), "exp", 0, 0)
     return jnp.sum(shares.astype(jnp.float32), axis=0).astype(jnp.bfloat16)

time: 151 us -> 136 us (0.901)
  the two profiles are of different devices: /device:TPU:1 before, /device:TPU:8 now
where the time goes in v4:
time: 136 us
  blocking collectives  52.5 us (39%)
  waiting for transfers between devices  42.2 us (31%)
  between operations  13.7 us (10%)
  Pallas kernels  11 us (8%)
  starting transfers between devices  10.8 us (8%)
  other arithmetic  2.46 us (2%)
  matrix products  1.6 us (1%)
    all_gather x1, waiting for transfers between devices, local(): rows = lax.all_gather(expert_rows, 'y', axis=0, tiled=True)  22.5 us
    all_gather x1, blocking collectives, local(): scores = lax.all_gather(capped, ('y', 'core'), axis=0)  20.2 us
    all_to_all x1, waiting for transfers between devices, local(): lax.all_to_all(partial.reshape(rings, capacity, partial.shape[1]), 'y', 0...  19.7 us
    all_to_all x1, blocking collectives, local(): lax.all_to_all(shares.reshape(owners, out_rows, shares.shape[1]), 'exp',...  17.7 us
    all_gather x1, blocking collectives, local(): full_hidden = lax.all_gather(hidden, 'tp', axis=0)  14.6 us
    ppermute x3, starting transfers between devices, swap_cores(): return lax.ppermute(value, 'core', [(0, 1), (1, 0)])  6.26 us
    pallas_call x1, Pallas kernels, ffn(): pl.pallas_call(ffn_kernel, in_specs=[pl.BlockSpec(memory_space=pltpu.HBM)...  4.63 us
    all_to_all x1, starting transfers between devices, local(): lax.all_to_all(partial.reshape(rings, capacity, partial.shape[1]), 'y', 0...  4.53 us
  transfers between devices with their start and end apart: 5, of which 2 were waited for; matrix products, arithmetic and copies ran while one was open for 3% of the time, Pallas kernels for 3%

profile of v4, /device:TPU:8, one launch (start us, length us, event | category | flops | bytes accessed | tf_op | source)
XLA Modules:
  0.0 135.5 jit_solution(2300352889490446271)
XLA Ops:
  6.5 3.0 %route.1 = (bf16[48,128]{1,0:T(8,128)(2,1)}, bf16[48,4096]{1,0:T(8,128)(2,1)}) custom-call(s32[1]{0:T(128)} %bitcast.owner_ref, s32[1,8]{1,0:T(1,128)} %limits_hbm.1, s32[2,128]{1,0:T(2,128)} %bitcast.44, bf16[128,4096]{1,0:T(8,128)(2,1)} %tokens_hbm.1), custom_call_target="tpu_custom_call" | custom-call | flops 50331648 | bytes 1441792 | tf_op jit(solution)/shard_map/route/pallas_call | solution.py:69
  9.5 0.0 all-gather.4.cloned.1.call-update
  9.6 1.9 %collective-permute-start = (bf16[4096,128]{1,0:T(8,128)(2,1)}, bf16[4096,128]{1,0:T(8,128)(2,1)}, u32[]{:S(2)}, u32[]{:S(2)}) collective-permute-start(bf16[4096,128]{1,0:T(8,128)(2,1)} %bitcast.40), channel_id=1, source_target_pairs={{0,32},{32,0},{1,33},{33,1},{2,34},{34,2},{3,35},{35,3},{4,36},{36... | collective-permute-start | bytes 3145736 | tf_op jit(solution)/shard_map/ppermute | solution.py:16
  11.5 2.4 %collective-permute-start.1 = (bf16[4096,128]{1,0:T(8,128)(2,1)}, bf16[4096,128]{1,0:T(8,128)(2,1)}, u32[]{:S(2)}, u32[]{:S(2)}) collective-permute-start(bf16[4096,128]{1,0:T(8,128)(2,1)} %bitcast.42), channel_id=1, source_target_pairs={{0,32},{32,0},{1,33},{33,1},{2,34},{34,2},{3,35},{35,3},{4,36},{36... | collective-permute-start | bytes 3145736 | tf_op jit(solution)/shard_map/ppermute | solution.py:16
  13.9 1.9 %collective-permute-start.2 = (bf16[512,1024]{1,0:T(8,128)(2,1)}, bf16[512,1024]{1,0:T(8,128)(2,1)}, u32[]{:S(2)}, u32[]{:S(2)}) collective-permute-start(bf16[512,1024]{1,0:T(8,128)(2,1)} %bitcast.37), channel_id=1, source_target_pairs={{0,32},{32,0},{1,33},{33,1},{2,34},{34,2},{3,35},{35,3},{4,36},{36... | collective-permute-start | bytes 3145736 | tf_op jit(solution)/shard_map/ppermute | solution.py:16
  15.9 1.6 %fusion.2 = f32[8,128]{1,0:T(8,128)S(1)} fusion(bf16[128,4096]{1,0:T(8,128)(2,1)} %tokens_hbm.1, bf16[4096,8]{0,1:T(8,128)(2,1)} %param.8), kind=kOutput, calls=%fused_computation.3 | convolution fusion | flops 8390656 | bytes 1118208 | tf_op jit(solution)/shard_map/dot_general | solution.py:229
  17.5 20.2 %all-gather.1 = f32[128,128]{1,0:T(8,128)S(1)} all-gather(f32[8,128]{1,0:T(8,128)S(1)} %fusion.2), channel_id=3, replica_groups=mesh['y'=8,'core'=2,'exp'=8,'tp'=4] {'y','core'}, dimensions={0}, use_global_device_ids=true | all-gather | bytes 69632 | tf_op jit(solution)/shard_map/all_gather | solution.py:233
  37.7 0.1 fusion.4
  37.8 0.1 fusion.8
  38.0 0.2 multiply_reduce_fusion.2
  38.2 0.1 fusion.5
  38.3 0.2 multiply_reduce_fusion.1
  38.5 0.6 broadcast_divide_fusion.6
  39.1 0.0 collective-permute-done.gate2_hbm
  39.1 0.0 copy-done.10
  39.1 0.0 copy-done.12
  39.1 0.0 collective-permute-done.1.up2_hbm
  39.1 22.5 %all-gather.4.cloned.1.call-done.rows_hbm = bf16[384,4096]{1,0:T(8,128)(2,1)} async-done(((bf16[48,4096]{1,0:T(8,128)(2,1)}), bf16[384,4096]{1,0:T(8,128)(2,1)}) %all-gather.4.cloned.1.call-update) | async-done | bytes 3145744 | tf_op jit(solution)/shard_map/all_gather | solution.py:222
  61.6 4.6 %ffn.1 = bf16[384,256]{1,0:T(8,128)(2,1)} custom-call(bf16[384,4096]{1,0:T(8,128)(2,1)} %all-gather.4.cloned.1.call-done.rows_hbm, bf16[4096,128]{1,0:T(8,128)(2,1)} %bitcast.41, bf16[4096,128]{1,0:T(8,128)(2,1)} %bitcast.43, bf16[4096,128]{1,0:T(8,128)(2,1)} %collective-permute-done.gate2_hbm, bf16[4096,128]{1,0:T(8,128)(2,1)} %collective-permute-done.1.up2_hbm), custom_call_target="tpu_custom_call" | custom-call | flops 1610612736 | bytes 7340032 | tf_op jit(solution)/shard_map/ffn/pallas_call | solution.py:134
  66.3 0.0 copy-start.1
  66.3 14.6 %all-gather = bf16[1536,256]{1,0:T(8,128)(2,1)S(1)} all-gather(bf16[384,256]{1,0:T(8,128)(2,1)} %ffn.1), channel_id=2, replica_groups=mesh['y'=8,'core'=2,'exp'=8,'tp'=4] {'tp'}, dimensions={0}, use_global_device_ids=true | all-gather | bytes 983040 | tf_op jit(solution)/shard_map/all_gather | solution.py:243
  80.9 0.0 collective-permute-done.2.down2_ref
  80.9 1.2 copy-done
  82.2 3.1 %down.1 = bf16[384,1024]{1,0:T(8,128)(2,1)} custom-call(bf16[4,384,256]{2,1,0:T(8,128)(2,1)S(1)} %bitcast.36, bf16[512,1024]{1,0:T(8,128)(2,1)S(1)} %bitcast.38, bf16[512,1024]{1,0:T(8,128)(2,1)} %collective-permute-done.2.down2_ref), custom_call_target="tpu_custom_call" | custom-call | flops 805306368 | bytes 3670016 | tf_op jit(solution)/shard_map/down/pallas_call | solution.py:169
  85.2 4.5 %all-to-all-start = ((bf16[8,48,1024]{2,1,0:T(8,128)(2,1)}), bf16[8,48,1024]{2,1,0:T(8,128)(2,1)S(1)}, u32[]{:S(2)}, u32[]{:S(2)}) async-start(bf16[8,48,1024]{2,1,0:T(8,128)(2,1)} %bitcast.6), calls=%async_computation | async-start | bytes 1572864 | tf_op jit(solution)/shard_map/all_to_all | solution.py:245
  89.8 0.1 fusion.6
  90.0 0.2 multiply_reduce_fusion
  90.2 0.1 fusion.9
  90.3 19.7 %all-to-all-done.parts_ref = bf16[8,48,1024]{2,1,0:T(8,128)(2,1)S(1)} async-done(((bf16[8,48,1024]{2,1,0:T(8,128)(2,1)}), bf16[8,48,1024]{2,1,0:T(8,128)(2,1)S(1)}, u32[]{:S(2)}, u32[]{:S(2)}) %all-to-all-start) | async-done | bytes 786464 | tf_op jit(solution)/shard_map/all_to_all | solution.py:245
  110.0 0.3 weigh.1
  110.3 17.7 %all_to_all.10 = bf16[8,16,1024]{2,1,0:T(8,128)(2,1)S(1)} all-to-all(bf16[8,16,1024]{2,1,0:T(8,128)(2,1)S(1)} %bitcast.39), channel_id=1, replica_groups=mesh['y'=8,'core'=2,'exp'=8,'tp'=4] {'exp'}, dimensions={0} | all-to-all | bytes 524288 | tf_op jit(solution)/shard_map/all_to_all | solution.py:247
  128.0 0.7 reduce_sum.102
  (38 shorter events, 0.2 us)
Async XLA Ops:
  6.5 55.1 %all-gather.4.cloned.1.call-start = ((), (), s32[]{:S(2)}) async-start(), calls=%async_computation.2 | async-start | bytes 3538944 | tf_op jit(solution)/shard_map/all_gather | solution.py:222
  9.6 29.5 %collective-permute-start = (bf16[4096,128]{1,0:T(8,128)(2,1)}, bf16[4096,128]{1,0:T(8,128)(2,1)}, u32[]{:S(2)}, u32[]{:S(2)}) collective-permute-start(bf16[4096,128]{1,0:T(8,128)(2,1)} %bitcast.40), channel_id=1, source_target_pairs={{0,32},{32,0},{1,33},{33,1},{2,34},{34,2},{3,35},{35,3},{4,36},{36... | collective-permute-start | bytes 3145736 | tf_op jit(solution)/shard_map/ppermute | solution.py:16
  11.5 27.6 %collective-permute-start.1 = (bf16[4096,128]{1,0:T(8,128)(2,1)}, bf16[4096,128]{1,0:T(8,128)(2,1)}, u32[]{:S(2)}, u32[]{:S(2)}) collective-permute-start(bf16[4096,128]{1,0:T(8,128)(2,1)} %bitcast.42), channel_id=1, source_target_pairs={{0,32},{32,0},{1,33},{33,1},{2,34},{34,2},{3,35},{35,3},{4,36},{36... | collective-permute-start | bytes 3145736 | tf_op jit(solution)/shard_map/ppermute | solution.py:16
  13.9 67.0 %collective-permute-start.2 = (bf16[512,1024]{1,0:T(8,128)(2,1)}, bf16[512,1024]{1,0:T(8,128)(2,1)}, u32[]{:S(2)}, u32[]{:S(2)}) collective-permute-start(bf16[512,1024]{1,0:T(8,128)(2,1)} %bitcast.37), channel_id=1, source_target_pairs={{0,32},{32,0},{1,33},{33,1},{2,34},{34,2},{3,35},{35,3},{4,36},{36... | collective-permute-start | bytes 3145736 | tf_op jit(solution)/shard_map/ppermute | solution.py:16
  37.6 0.7 copy-start.2
  37.7 0.8 copy-start.4
  37.8 1.3 copy-start.10
  37.9 1.1 copy-start.6
  38.2 0.9 copy-start.12
  38.3 0.8 copy-start.8
  66.2 23.5 %copy-start.3 = (f32[128,128]{1,0:T(8,128)S(1)}, f32[128,128]{1,0:T(8,128)}, u32[]{:S(2)}) copy-start(f32[128,128]{1,0:T(8,128)} %copy-done.2) | copy-start | bytes 196612
  66.2 23.5 %copy-start.5 = (f32[16,128]{1,0:T(8,128)S(1)}, f32[16,128]{1,0:T(8,128)}, u32[]{:S(2)}) copy-start(f32[16,128]{1,0:T(8,128)} %copy-done.4) | copy-start | bytes 24580
  66.2 23.5 %copy-start.7 = (f32[16,128]{1,0:T(8,128)S(1)}, f32[16,128]{1,0:T(8,128)}, u32[]{:S(2)}) copy-start(f32[16,128]{1,0:T(8,128)} %copy-done.6) | copy-start | bytes 24580
  66.3 23.5 %copy-start.9 = (f32[16,128]{1,0:T(8,128)S(1)}, f32[16,128]{1,0:T(8,128)}, u32[]{:S(2)}) copy-start(f32[16,128]{1,0:T(8,128)} %copy-done.8) | copy-start | bytes 24580
  66.3 23.5 %copy-start.11 = (f32[8]{0:T(128)S(1)}, f32[8]{0:T(128)}, u32[]{:S(2)}) copy-start(f32[8]{0:T(128)} %copy-done.10) | copy-start | bytes 100
  66.3 23.5 %copy-start.13 = (f32[8]{0:T(128)S(1)}, f32[8]{0:T(128)}, u32[]{:S(2)}) copy-start(f32[8]{0:T(128)} %copy-done.12) | copy-start | bytes 100
  66.3 23.5 %copy-start.14 = (f32[8]{0:T(128)S(1)}, f32[8]{0:T(128)}, u32[]{:S(2)}) copy-start(f32[8]{0:T(128)} %broadcast_divide_fusion.6) | copy-start | bytes 100
  66.3 43.7 %copy-start.1 = (bf16[48,128]{1,0:T(8,128)(2,1)S(1)}, bf16[48,128]{1,0:T(8,128)(2,1)}, u32[]{:S(2)}) copy-start(bf16[48,128]{1,0:T(8,128)(2,1)} %get-tuple-element.15.select_ref) | copy-start | bytes 36868
  80.9 1.2 copy-start
  85.2 24.8 %all-to-all-start = ((bf16[8,48,1024]{2,1,0:T(8,128)(2,1)}), bf16[8,48,1024]{2,1,0:T(8,128)(2,1)S(1)}, u32[]{:S(2)}, u32[]{:S(2)}) async-start(bf16[8,48,1024]{2,1,0:T(8,128)(2,1)} %bitcast.6), calls=%async_computation | async-start | bytes 1572864 | tf_op jit(solution)/shard_map/all_to_all | solution.py:245
Sparse Core Ops, SparseCore 0:
  9.7 51.8 all-gather.3

commit v5 on v4

v5 whole, which is shorter than its diff:
```python
import jax
import jax.numpy as jnp
from jax import lax
from jax.experimental import pallas as pl
from jax.experimental.pallas import tpu as pltpu
from jax.sharding import Mesh, PartitionSpec as P

TOP = 2
ITERS = 4
SOFT_CAP = 8.0
CORES = 2
ALL_VMEM = 64 << 20
FFN_VMEM = 60 << 20
DIRECT = 512
LANES = 128


def swap_cores(value):
    return lax.ppermute(value, "core", [(0, 1), (1, 0)])


def route_kernel(
    ids_ref, limits_hbm, assign_hbm, tokens_hbm, select_ref, direct_ref, spread_hbm,
    limits_ref, assign_ref, near_ref, far_ref, own_ref, sems, out_sems
):
    direct = near_ref.shape[1]
    share = far_ref.shape[1]
    owner = ids_ref[0]
    first = pl.multiple_of(direct + ids_ref[1] * share, 128)
    copies = [
        pltpu.make_async_copy(source, sink, sems.at[index])
        for index, (source, sink) in enumerate(
            (
                (limits_hbm, limits_ref),
                (assign_hbm, assign_ref),
                (tokens_hbm.at[:, pl.ds(first, share)], far_ref),
                (tokens_hbm.at[:, pl.ds(0, direct)], near_ref),
            )
        )
    ]
    for copy in copies:
        copy.start()
    capacity, count = select_ref.shape
    row = lax.broadcasted_iota(jnp.int32, (count, count), 0)
    column = lax.broadcasted_iota(jnp.int32, (count, count), 1)
    earlier = jnp.where(row < column, 1.0, 0.0).astype(jnp.bfloat16)
    slot_ids = lax.broadcasted_iota(jnp.int32, (capacity, count), 0)
    copies[0].wait()
    copies[1].wait()
    hit = jnp.sum(jnp.where(assign_ref[...] == owner, 1.0, 0.0), axis=0, keepdims=True)
    named = jnp.broadcast_to(hit, (16, count)).astype(jnp.bfloat16)
    slot = jnp.dot(named, earlier, preferred_element_type=jnp.float32)[:1].astype(jnp.int32)
    slot = jnp.where((hit > 0.0) & (slot < limits_ref[0, owner]), slot, -1)
    select = jnp.where(slot_ids == slot, 1.0, 0.0).astype(jnp.bfloat16)
    select_ref[...] = select
    copies[2].wait()
    own_ref[...] = jnp.dot(
        select, far_ref[...], preferred_element_type=jnp.float32
    ).astype(own_ref.dtype)
    outs = [
        pltpu.make_async_copy(own_ref, spread_hbm.at[index], out_sems.at[index])
        for index in range(spread_hbm.shape[0])
    ]
    for copy in outs:
        copy.start()
    copies[3].wait()
    direct_ref[...] = jnp.dot(
        select, near_ref[...], preferred_element_type=jnp.float32
    ).astype(direct_ref.dtype)
    for copy in outs:
        copy.wait()


def route(ids, limits, assignments, tokens, capacity, direct, share, rings):
    count = tokens.shape[0]
    far = pl.BlockSpec(memory_space=pltpu.HBM)
    near = pl.BlockSpec(memory_space=pltpu.VMEM)
    return pl.pallas_call(
        route_kernel,
        in_specs=[pl.BlockSpec(memory_space=pltpu.SMEM), far, far, far],
        out_specs=[near, near, far],
        out_shape=[
            jax.ShapeDtypeStruct((capacity, count), jnp.bfloat16),
            jax.ShapeDtypeStruct((capacity, direct), jnp.bfloat16),
            jax.ShapeDtypeStruct((rings, capacity, share), jnp.bfloat16),
        ],
        scratch_shapes=[
            pltpu.SMEM(limits.shape, jnp.int32),
            pltpu.VMEM(assignments.shape, jnp.int32),
            pltpu.VMEM((count, direct), jnp.bfloat16),
            pltpu.VMEM((count, share), jnp.bfloat16),
            pltpu.VMEM((capacity, share), jnp.bfloat16),
            pltpu.SemaphoreType.DMA((4,)),
            pltpu.SemaphoreType.DMA((rings,)),
        ],
        compiler_params=pltpu.CompilerParams(vmem_limit_bytes=ALL_VMEM),
        cost_estimate=pl.CostEstimate(
            flops=2 * capacity * count * (direct + share),
            bytes_accessed=2 * (count + capacity) * (direct + share),
            transcendentals=0,
        ),
        name="route",
    )(ids, limits, assignments, tokens)


def ffn_kernel(
    near_hbm, far_hbm, gate_hbm, up_hbm, gate2_hbm, up2_hbm, out_ref,
    near_ref, far_ref, weight_ref, sems
):
    rings, capacity, direct = near_ref.shape
    shares, _, share = far_ref.shape
    width, columns = weight_ref.shape
    units = columns // 4
    copies = []
    for index in range(shares + 1):
        first, size = (0, direct) if index == 0 else (direct + (index - 1) * share, share)
        part = pl.ds(first, size)
        if index == 0:
            ends = [(near_hbm.at[:, pl.ds(0, capacity), :], near_ref)]
        else:
            ends = [(far_hbm.at[index - 1], far_ref.at[index - 1])]
        for place, ref in enumerate((gate_hbm, up_hbm, gate2_hbm, up2_hbm)):
            ends.append((ref.at[part, :], weight_ref.at[part, pl.ds(place * units, units)]))
        copies.append(
            [
                pltpu.make_async_copy(source, sink, sems.at[index, place])
                for place, (source, sink) in enumerate(ends)
            ]
        )
    for group in copies:
        for copy in group:
            copy.start()
    total = None
    for index, group in enumerate(copies):
        for copy in group:
            copy.wait()
        if index == 0:
            rows = near_ref[...].reshape(rings * capacity, direct)
            part = pl.ds(0, direct)
        else:
            rows = far_ref[index - 1]
            part = pl.ds(direct + (index - 1) * share, share)
        product = jnp.dot(rows, weight_ref[part, :], preferred_element_type=jnp.float32)
        total = product if index == 0 else total + product
    for side in range(2):
        gate = total[:, 2 * side * units : (2 * side + 1) * units]
        up = total[:, (2 * side + 1) * units : (2 * side + 2) * units]
        hidden = gate / (1.0 + jnp.exp(-gate)) * up
        out_ref[:, side * units : (side + 1) * units] = hidden.astype(out_ref.dtype)


def ffn(near, far, gate, up, gate2, up2, capacity):
    rings, _, direct = near.shape
    shares, count, share = far.shape
    width, units = gate.shape
    return pl.pallas_call(
        ffn_kernel,
        in_specs=[pl.BlockSpec(memory_space=pltpu.HBM)] * 6,
        out_specs=pl.BlockSpec(memory_space=pltpu.VMEM),
        out_shape=jax.ShapeDtypeStruct((count, 2 * units), jnp.bfloat16),
        scratch_shapes=[
            pltpu.VMEM((rings, capacity, direct), jnp.bfloat16),
            pltpu.VMEM((shares, count, share), jnp.bfloat16),
            pltpu.VMEM((width, 4 * units), jnp.bfloat16),
            pltpu.SemaphoreType.DMA((shares + 1, 5)),
        ],
        compiler_params=pltpu.CompilerParams(vmem_limit_bytes=FFN_VMEM),
        cost_estimate=pl.CostEstimate(
            flops=8 * count * width * units,
            bytes_accessed=2 * count * width + 8 * width * units,
            transcendentals=2 * count * units,
        ),
        name="ffn",
    )(near, far, gate, up, gate2, up2)


def down_kernel(hidden_ref, down_ref, down2_ref, out_ref):
    parts = hidden_ref.shape[0]
    units = down_ref.shape[0] // parts
    total = None
    for index in range(parts):
        part = pl.ds(index * units, units)
        both = jnp.concatenate([down_ref[part, :], down2_ref[part, :]], axis=0)
        product = jnp.dot(hidden_ref[index], both, preferred_element_type=jnp.float32)
        total = product if index == 0 else total + product
    out_ref[...] = total.astype(out_ref.dtype)


def down(hidden, weight, weight2):
    parts, count, units = hidden.shape
    columns = weight.shape[1]
    return pl.pallas_call(
        down_kernel,
        out_shape=jax.ShapeDtypeStruct((count, columns), jnp.bfloat16),
        compiler_params=pltpu.CompilerParams(vmem_limit_bytes=24 << 20),
        cost_estimate=pl.CostEstimate(
            flops=2 * parts * count * units * columns,
            bytes_accessed=2 * parts * units * (count + columns) + 2 * count * columns,
            transcendentals=0,
        ),
        name="down",
    )(hidden, weight, weight2)


def weigh_kernel(parts_ref, select_ref, gate_ref, out_ref):
    select = select_ref[...]
    total = jnp.sum(parts_ref[...].astype(jnp.float32), axis=0).astype(jnp.bfloat16)
    gate = jnp.sum(select.astype(jnp.float32) * gate_ref[...], axis=1, keepdims=True)
    weighted = (total.astype(jnp.float32) * gate).astype(jnp.bfloat16)
    out_ref[...] = lax.dot_general(
        select, weighted, (((0,), (0,)), ((), ())), preferred_element_type=jnp.float32
    ).astype(out_ref.dtype)


def weigh(parts, select, gate):
    count = select.shape[1]
    columns = parts.shape[2]
    return pl.pallas_call(
        weigh_kernel,
        out_shape=jax.ShapeDtypeStruct((count, columns), jnp.bfloat16),
        compiler_params=pltpu.CompilerParams(vmem_limit_bytes=24 << 20),
        cost_estimate=pl.CostEstimate(
            flops=2 * count * select.shape[0] * columns,
            bytes_accessed=2 * parts.size + 2 * count * columns,
            transcendentals=0,
        ),
        name="weigh",
    )(parts, select, gate)


def local(tokens, router_weight, gate_weight, up_weight, down_weight, assignments, limits):
    local_rows, width = tokens.shape
    experts = router_weight.shape[1]
    rings = lax.axis_size("y")
    shards = rings * CORES
    owners = lax.axis_size("exp")
    parts = lax.axis_size("tp")
    capacity = min(local_rows, max(2, 3 * local_rows * TOP // (2 * experts)))
    out_rows = local_rows // owners
    target = local_rows * shards * TOP / experts
    owner = lax.axis_index("exp")
    share = (width - DIRECT) // parts

    ids = jnp.stack([owner, lax.axis_index("tp")]).astype(jnp.int32)
    select, direct, spread = route(
        ids, limits, assignments.T, tokens, capacity, DIRECT, share, rings
    )
    own_share = lax.all_to_all(spread, "y", 0, 0).reshape(1, rings * capacity, share)

    w_gate, w_up, w_down, tokens2, _ = lax.optimization_barrier(
        (gate_weight[0], up_weight[0], down_weight[0], tokens, spread)
    )
    gate2, up2, down2 = swap_cores(w_gate), swap_cores(w_up), swap_cores(w_down)
    logits = lax.dot_general(
        router_weight, tokens2, (((0,), (1,)), ((), ())), preferred_element_type=jnp.float32
    )
    scores = SOFT_CAP * jnp.tanh(logits / SOFT_CAP)
    pieces = []
    for piece in range(3):
        pieces.append(lax.reduce_precision(scores, exponent_bits=8, mantissa_bits=7))
        scores = scores - pieces[-1]
    pieces = jnp.concatenate(pieces, axis=0).astype(jnp.bfloat16)
    count = pieces.shape[0]
    tail_rows = 16
    slots = tail_rows * DIRECT // local_rows
    pieces = jnp.pad(pieces, ((0, slots - count), (0, 0))).reshape(tail_rows, DIRECT)
    payload = jnp.concatenate([direct, pieces], axis=0)

    copies = jnp.broadcast_to(own_share, (parts,) + own_share.shape[1:])
    copies, payload, gate2, up2, down2 = lax.optimization_barrier(
        (copies, payload, gate2, up2, down2)
    )
    far = lax.all_to_all(copies, "tp", 0, 0)
    near = lax.all_gather(payload, "y", axis=0)

    hidden = ffn(near, far, w_gate, w_up, gate2, up2, capacity)
    full_hidden = lax.all_gather(hidden, "tp", axis=0)
    partial = down(full_hidden, w_down, down2)
    near, partial = lax.optimization_barrier((near, partial))
    sums = lax.all_to_all(partial.reshape(rings, capacity, partial.shape[1]), "y", 0, 0)
    tail = near[:, capacity:].reshape(rings, slots, local_rows)[:, :count]
    tail = jnp.sum(tail.reshape(rings, 3, experts, local_rows).astype(jnp.float32), axis=1)
    weights = jnp.exp(jnp.concatenate([tail, swap_cores(tail)], axis=0))
    weights = weights * (TOP / jnp.sum(weights, axis=1, keepdims=True))
    for repeat in range(ITERS):
        weights = weights * (target / jnp.sum(weights, axis=(0, 2), keepdims=True))
        weights = weights * (TOP / jnp.sum(weights, axis=1, keepdims=True))
    own = lax.dynamic_slice(weights, (lax.axis_index("y"), owner, 0), (1, 1, local_rows))[0]

    shares = weigh(sums, select, own)
    shares = lax.all_to_all(shares.reshape(owners, out_rows, shares.shape[1]), "exp", 0, 0)
    return jnp.sum(shares.astype(jnp.float32), axis=0).astype(jnp.bfloat16)


def solution(mesh):
    shape = mesh.devices.shape
    fine = Mesh(
        mesh.devices.reshape((shape[0] // CORES, CORES) + shape[1:]), ("y", "core", "exp", "tp")
    )
    tok = ("y", "core")
    placed = (
        P(tok, None),
        P(),
        P("exp", None, tok + ("tp",)),
        P("exp", None, tok + ("tp",)),
        P("exp", tok, "tp"),
        P(tok, None),
        P(tok, None),
    )
    return jax.shard_map(
        local, mesh=fine, in_specs=placed, out_specs=P(tok + ("exp",), "tp"), check_vma=False
    )
```

time: 136 us -> 147 us (1.081)
  the two profiles are of different devices: /device:TPU:8 before, /device:TPU:1 now
where the time goes in v5:
time: 147 us
  blocking collectives  55.3 us (38%)
  waiting for transfers between devices  39.9 us (27%)
  starting transfers between devices  33.3 us (23%)
  Pallas kernels  10.3 us (7%)
  other arithmetic  3.22 us (2%)
  local copies, waits for them, and re-layouts  2.83 us (2%)
  matrix products  1.61 us (1%)
    all_gather x1, blocking collectives, local(): near = lax.all_gather(payload, 'y', axis=0)  22.9 us
    all_to_all x1, waiting for transfers between devices, local(): lax.all_to_all(partial.reshape(rings, capacity, partial.shape[1]), 'y', 0...  22.3 us
    all_to_all x1, blocking collectives, local(): lax.all_to_all(shares.reshape(owners, out_rows, shares.shape[1]), 'exp',...  20.9 us
    ppermute x4, starting transfers between devices, swap_cores(): return lax.ppermute(value, 'core', [(0, 1), (1, 0)])  15.4 us
    all_gather x1, blocking collectives, local(): full_hidden = lax.all_gather(hidden, 'tp', axis=0)  11.6 us
    all_to_all x1, waiting for transfers between devices, local(): far = lax.all_to_all(copies, 'tp', 0, 0)  10.3 us
    all_to_all x1, starting transfers between devices, local(): lax.all_to_all(spread, 'y', 0, 0).reshape(1, rings * capacity, share)  7.66 us
    all_to_all x1, waiting for transfers between devices, local(): lax.all_to_all(spread, 'y', 0, 0).reshape(1, rings * capacity, share)  7.25 us
  transfers between devices with their start and end apart: 7, of which 3 were waited for; matrix products, arithmetic and copies ran while one was open for 2% of the time, Pallas kernels for 0%

profile of v5, /device:TPU:1, one launch (start us, length us, event | category | flops | bytes accessed | tf_op | source)
XLA Modules:
  0.0 146.8 jit_solution(3473476675855747939)
XLA Ops:
  0.0 0.6 pad_add_fusion.ids_ref
  0.6 3.4 %route.1 = (bf16[48,128]{1,0:T(8,128)(2,1)}, bf16[48,512]{1,0:T(8,128)(2,1)}, bf16[8,48,896]{2,1,0:T(8,128)(2,1)}) custom-call(s32[2]{0:T(128)} %pad_add_fusion.ids_ref, s32[1,8]{1,0:T(1,128)} %limits_hbm.1, s32[2,128]{1,0:T(2,128)} %bitcast.33, bf16[128,4096]{1,0:T(8,128)(2,1)} %tokens_hbm.1), custom_call_target="tpu_custom_call" | custom-call | flops 17301504 | bytes 495616 | tf_op jit(solution)/shard_map/route/pallas_call | solution.py:78
  4.0 7.7 %all-to-all-start = ((bf16[8,48,896]{2,1,0:T(8,128)(2,1)}), bf16[8,48,896]{2,1,0:T(8,128)(2,1)S(1)}, u32[]{:S(2)}, u32[]{:S(2)}) async-start(bf16[8,48,896]{2,1,0:T(8,128)(2,1)} %get-tuple-element.19), calls=%async_computation | async-start | bytes 1376256 | tf_op jit(solution)/shard_map/all_to_all | solution.py:248
  11.6 4.7 %collective-permute-start = (bf16[4096,128]{1,0:T(8,128)(2,1)}, bf16[4096,128]{1,0:T(8,128)(2,1)S(1)}, u32[]{:S(2)}, u32[]{:S(2)}) collective-permute-start(bf16[4096,128]{1,0:T(8,128)(2,1)} %bitcast.29), channel_id=1, source_target_pairs={{0,32},{32,0},{1,33},{33,1},{2,34},{34,2},{3,35},{35,3},{4,36},{36... | collective-permute-start | bytes 3145736 | tf_op jit(solution)/shard_map/ppermute | solution.py:19
  16.3 1.9 %collective-permute-start.1 = (bf16[4096,128]{1,0:T(8,128)(2,1)}, bf16[4096,128]{1,0:T(8,128)(2,1)}, u32[]{:S(2)}, u32[]{:S(2)}) collective-permute-start(bf16[4096,128]{1,0:T(8,128)(2,1)} %bitcast.31), channel_id=1, source_target_pairs={{0,32},{32,0},{1,33},{33,1},{2,34},{34,2},{3,35},{35,3},{4,36},{36... | collective-permute-start | bytes 3145736 | tf_op jit(solution)/shard_map/ppermute | solution.py:19
  18.3 2.4 %collective-permute-start.2 = (bf16[512,1024]{1,0:T(8,128)(2,1)}, bf16[512,1024]{1,0:T(8,128)(2,1)S(1)}, u32[]{:S(2)}, u32[]{:S(2)}) collective-permute-start(bf16[512,1024]{1,0:T(8,128)(2,1)} %bitcast.23), channel_id=1, source_target_pairs={{0,32},{32,0},{1,33},{33,1},{2,34},{34,2},{3,35},{35,3},{4,36},{36... | collective-permute-start | bytes 3145736 | tf_op jit(solution)/shard_map/ppermute | solution.py:19
  20.7 1.6 %reduce-precision_convert_fusion.1 = (bf16[8,128]{1,0:T(8,128)(2,1)S(1)}, bf16[8,128]{1,0:T(8,128)(2,1)S(1)}, bf16[8,128]{1,0:T(8,128)(2,1)S(1)}) fusion(bf16[128,4096]{1,0:T(8,128)(2,1)} %tokens_hbm.1, bf16[4096,8]{0,1:T(8,128)(2,1)} %param.8), kind=kOutput, calls=%fused_computation.27 | convolution fusion | flops 8398848 | bytes 1120256 | tf_op jit(solution)/shard_map/dot_general | solution.py:254
  22.3 0.8 pad_maximum_fusion
  23.2 7.3 %all-to-all-done = bf16[8,48,896]{2,1,0:T(8,128)(2,1)S(1)} async-done(((bf16[8,48,896]{2,1,0:T(8,128)(2,1)}), bf16[8,48,896]{2,1,0:T(8,128)(2,1)S(1)}, u32[]{:S(2)}, u32[]{:S(2)}) %all-to-all-start) | async-done | bytes 688160 | tf_op jit(solution)/shard_map/all_to_all | solution.py:248
  30.4 1.8 %broadcast_in_dim.5 = bf16[4,384,896]{2,1,0:T(8,128)(2,1)} broadcast(bf16[384,896]{1,0:T(8,128)(2,1)S(1)} %bitcast.26), dimensions={1,2} | broadcast | bytes 3440640 | tf_op jit(solution)/shard_map/broadcast_in_dim | solution.py:269
  32.2 6.7 %all-to-all-start.1 = ((bf16[4,384,896]{2,1,0:T(8,128)(2,1)}), bf16[4,384,896]{2,1,0:T(8,128)(2,1)}, u32[]{:S(2)}, u32[]{:S(2)}) async-start(bf16[4,384,896]{2,1,0:T(8,128)(2,1)} %broadcast_in_dim.5), calls=%async_computation.1 | async-start | bytes 5505024 | tf_op jit(solution)/shard_map/all_to_all | solution.py:273
  38.9 22.9 %all-gather = bf16[512,512]{1,0:T(8,128)(2,1)} all-gather(bf16[64,512]{1,0:T(8,128)(2,1)S(1)} %pad_maximum_fusion), channel_id=2, replica_groups=mesh['y'=8,'core'=2,'exp'=8,'tp'=4] {'y'}, dimensions={0}, use_global_device_ids=true | all-gather | bytes 589824 | tf_op jit(solution)/shard_map/all_gather | solution.py:274
  61.8 10.3 %all-to-all-done.1.far_hbm = bf16[4,384,896]{2,1,0:T(8,128)(2,1)} async-done(((bf16[4,384,896]{2,1,0:T(8,128)(2,1)}), bf16[4,384,896]{2,1,0:T(8,128)(2,1)}, u32[]{:S(2)}, u32[]{:S(2)}) %all-to-all-start.1) | async-done | bytes 2752544 | tf_op jit(solution)/shard_map/all_to_all | solution.py:273
  72.0 4.8 %ffn.1 = bf16[384,256]{1,0:T(8,128)(2,1)} custom-call(bf16[8,64,512]{2,1,0:T(8,128)(2,1)} %bitcast.27, bf16[4,384,896]{2,1,0:T(8,128)(2,1)} %all-to-all-done.1.far_hbm, bf16[4096,128]{1,0:T(8,128)(2,1)} %bitcast.30, bf16[4096,128]{1,0:T(8,128)(2,1)} %bitcast.32, bf16[4096,128]{1,0:T(8,128)(2,1)} %copy-done.2, bf16[4096,128]{1,0:T(8,128)(2,1)} %collective-permute-done.1.up2_hbm), custom_call_target="tpu_custom_call" | custom-call | flops 1610612736 | bytes 7340032 | tf_op jit(solution)/shard_map/ffn/pallas_call | solution.py:156
  76.9 11.6 %all-gather.1 = bf16[1536,256]{1,0:T(8,128)(2,1)S(1)} all-gather(bf16[384,256]{1,0:T(8,128)(2,1)} %ffn.1), channel_id=3, replica_groups=mesh['y'=8,'core'=2,'exp'=8,'tp'=4] {'tp'}, dimensions={0}, use_global_device_ids=true | all-gather | bytes 983040 | tf_op jit(solution)/shard_map/all_gather | solution.py:277
  88.5 1.9 %down.1 = bf16[384,1024]{1,0:T(8,128)(2,1)} custom-call(bf16[4,384,256]{2,1,0:T(8,128)(2,1)S(1)} %bitcast.22, bf16[512,1024]{1,0:T(8,128)(2,1)S(1)} %bitcast.24, bf16[512,1024]{1,0:T(8,128)(2,1)S(1)} %collective-permute-done.2.down2_ref), custom_call_target="tpu_custom_call" | custom-call | flops 805306368 | bytes 3670016 | tf_op jit(solution)/shard_map/down/pallas_call | solution.py:192
  90.3 0.9 slice.6
  91.3 0.1 reshape.55
  91.4 6.4 %collective-permute-start.3 = (f32[8,8,128]{2,1,0:T(8,128)S(1)}, f32[8,8,128]{2,1,0:T(8,128)S(1)}, u32[]{:S(2)}, u32[]{:S(2)}) collective-permute-start(f32[8,8,128]{2,1,0:T(8,128)S(1)} %convert_reduce_fusion), channel_id=1, source_target_pairs={{0,32},{32,0},{1,33},{33,1},{2,34},{34,2},{3,35},{35,3},{4,36},{36... | collective-permute-start | bytes 98312 | tf_op jit(solution)/shard_map/ppermute | solution.py:19
  97.8 3.6 %all-to-all-start.2 = ((bf16[8,48,1024]{2,1,0:T(8,128)(2,1)}), bf16[8,48,1024]{2,1,0:T(8,128)(2,1)S(1)}, u32[]{:S(2)}, u32[]{:S(2)}) async-start(bf16[8,48,1024]{2,1,0:T(8,128)(2,1)} %bitcast.10), calls=%async_computation.2 | async-start | bytes 1572864 | tf_op jit(solution)/shard_map/all_to_all | solution.py:280
  101.4 0.1 multiply_reduce_fusion.3
  101.6 0.1 fusion.3
  101.7 0.2 multiply_reduce_fusion.2
  101.9 0.1 fusion.15
  102.0 0.1 multiply_reduce_fusion.1
  102.1 0.1 fusion.4
  102.3 0.2 multiply_reduce_fusion
  102.5 0.1 fusion.14
  102.6 22.3 %all-to-all-done.2.parts_ref = bf16[8,48,1024]{2,1,0:T(8,128)(2,1)S(1)} async-done(((bf16[8,48,1024]{2,1,0:T(8,128)(2,1)}), bf16[8,48,1024]{2,1,0:T(8,128)(2,1)S(1)}, u32[]{:S(2)}, u32[]{:S(2)}) %all-to-all-start.2) | async-done | bytes 786464 | tf_op jit(solution)/shard_map/all_to_all | solution.py:280
  124.9 0.3 weigh.1
  125.2 20.9 %all_to_all.20 = bf16[8,16,1024]{2,1,0:T(8,128)(2,1)S(1)} all-to-all(bf16[8,16,1024]{2,1,0:T(8,128)(2,1)S(1)} %bitcast.25), channel_id=1, replica_groups=mesh['y'=8,'core'=2,'exp'=8,'tp'=4] {'exp'}, dimensions={0} | all-to-all | bytes 524288 | tf_op jit(solution)/shard_map/all_to_all | solution.py:291
  146.1 0.7 reduce_sum.112
  (25 shorter events, 0.2 us)
Async XLA Ops:
  4.0 26.5 %all-to-all-start = ((bf16[8,48,896]{2,1,0:T(8,128)(2,1)}), bf16[8,48,896]{2,1,0:T(8,128)(2,1)S(1)}, u32[]{:S(2)}, u32[]{:S(2)}) async-start(bf16[8,48,896]{2,1,0:T(8,128)(2,1)} %get-tuple-element.19), calls=%async_computation | async-start | bytes 1376256 | tf_op jit(solution)/shard_map/all_to_all | solution.py:248
  11.6 11.5 %collective-permute-start = (bf16[4096,128]{1,0:T(8,128)(2,1)}, bf16[4096,128]{1,0:T(8,128)(2,1)S(1)}, u32[]{:S(2)}, u32[]{:S(2)}) collective-permute-start(bf16[4096,128]{1,0:T(8,128)(2,1)} %bitcast.29), channel_id=1, source_target_pairs={{0,32},{32,0},{1,33},{33,1},{2,34},{34,2},{3,35},{35,3},{4,36},{36... | collective-permute-start | bytes 3145736 | tf_op jit(solution)/shard_map/ppermute | solution.py:19
  16.3 6.8 %collective-permute-start.1 = (bf16[4096,128]{1,0:T(8,128)(2,1)}, bf16[4096,128]{1,0:T(8,128)(2,1)}, u32[]{:S(2)}, u32[]{:S(2)}) collective-permute-start(bf16[4096,128]{1,0:T(8,128)(2,1)} %bitcast.31), channel_id=1, source_target_pairs={{0,32},{32,0},{1,33},{33,1},{2,34},{34,2},{3,35},{35,3},{4,36},{36... | collective-permute-start | bytes 3145736 | tf_op jit(solution)/shard_map/ppermute | solution.py:19
  18.3 4.9 %collective-permute-start.2 = (bf16[512,1024]{1,0:T(8,128)(2,1)}, bf16[512,1024]{1,0:T(8,128)(2,1)S(1)}, u32[]{:S(2)}, u32[]{:S(2)}) collective-permute-start(bf16[512,1024]{1,0:T(8,128)(2,1)} %bitcast.23), channel_id=1, source_target_pairs={{0,32},{32,0},{1,33},{33,1},{2,34},{34,2},{3,35},{35,3},{4,36},{36... | collective-permute-start | bytes 3145736 | tf_op jit(solution)/shard_map/ppermute | solution.py:19
  23.1 9.1 %copy-start.2 = (bf16[4096,128]{1,0:T(8,128)(2,1)}, bf16[4096,128]{1,0:T(8,128)(2,1)S(1)}, u32[]{:S(2)}) copy-start(bf16[4096,128]{1,0:T(8,128)(2,1)S(1)} %collective-permute-done.gate2_hbm) | copy-start | bytes 3145732
  32.2 39.8 %all-to-all-start.1 = ((bf16[4,384,896]{2,1,0:T(8,128)(2,1)}), bf16[4,384,896]{2,1,0:T(8,128)(2,1)}, u32[]{:S(2)}, u32[]{:S(2)}) async-start(bf16[4,384,896]{2,1,0:T(8,128)(2,1)} %broadcast_in_dim.5), calls=%async_computation.1 | async-start | bytes 5505024 | tf_op jit(solution)/shard_map/all_to_all | solution.py:273
  72.0 16.4 %copy-start = (bf16[1,512,1024]{2,1,0:T(8,128)(2,1)S(1)}, bf16[1,512,1024]{2,1,0:T(8,128)(2,1)}, u32[]{:S(2)}) copy-start(bf16[1,512,1024]{2,1,0:T(8,128)(2,1)} %param.11) | copy-start | bytes 3145732
  88.5 36.5 %copy-start.1 = (bf16[48,128]{1,0:T(8,128)(2,1)S(1)}, bf16[48,128]{1,0:T(8,128)(2,1)}, u32[]{:S(2)}) copy-start(bf16[48,128]{1,0:T(8,128)(2,1)} %get-tuple-element.31.select_ref) | copy-start | bytes 36868
  91.4 10.0 %collective-permute-start.3 = (f32[8,8,128]{2,1,0:T(8,128)S(1)}, f32[8,8,128]{2,1,0:T(8,128)S(1)}, u32[]{:S(2)}, u32[]{:S(2)}) collective-permute-start(f32[8,8,128]{2,1,0:T(8,128)S(1)} %convert_reduce_fusion), channel_id=1, source_target_pairs={{0,32},{32,0},{1,33},{33,1},{2,34},{34,2},{3,35},{35,3},{4,36},{36... | collective-permute-start | bytes 98312 | tf_op jit(solution)/shard_map/ppermute | solution.py:19
  97.8 27.1 %all-to-all-start.2 = ((bf16[8,48,1024]{2,1,0:T(8,128)(2,1)}), bf16[8,48,1024]{2,1,0:T(8,128)(2,1)S(1)}, u32[]{:S(2)}, u32[]{:S(2)}) async-start(bf16[8,48,1024]{2,1,0:T(8,128)(2,1)} %bitcast.10), calls=%async_computation.2 | async-start | bytes 1572864 | tf_op jit(solution)/shard_map/all_to_all | solution.py:280

commit v6 on v4

--- a/solution.py
+++ b/solution.py
@@ -10,6 +10,9 @@
 SOFT_CAP = 8.0
 CORES = 2
 ALL_VMEM = 64 << 20
+FFN_VMEM = 60 << 20
+SHARE = 256
+TAIL = 16
 
 
 def swap_cores(value):
@@ -17,12 +20,15 @@
 
 
 def route_kernel(
-    owner_ref, limits_hbm, assign_hbm, tokens_hbm, select_ref, rows_hbm,
-    limits_ref, assign_ref, tokens_ref, rows_ref, sems, out_sems
+    owner_ref, part_ref, limits_hbm, assign_hbm, tokens_hbm, select_ref, rows_hbm, share_ref,
+    limits_ref, assign_ref, tokens_ref, own_ref, rows_ref, sems, out_sems
 ):
     width = tokens_ref.shape[1]
+    share = own_ref.shape[1]
     chunks = out_sems.shape[0]
     parts = [pl.ds(index * (width // chunks), width // chunks) for index in range(chunks)]
+    owner = owner_ref[0]
+    first = pl.multiple_of(width + part_ref[0] * share, 128)
     small = [
         pltpu.make_async_copy(limits_hbm, limits_ref, sems.at[chunks]),
         pltpu.make_async_copy(assign_hbm, assign_ref, sems.at[chunks + 1]),
@@ -31,9 +37,11 @@
         pltpu.make_async_copy(tokens_hbm.at[:, part], tokens_ref.at[:, part], sems.at[index])
         for index, part in enumerate(parts)
     ]
-    for copy in small + copies:
+    last = pltpu.make_async_copy(
+        tokens_hbm.at[:, pl.ds(first, share)], own_ref, sems.at[chunks + 2]
+    )
+    for copy in small + copies + [last]:
         copy.start()
-    owner = owner_ref[0]
     capacity, count = select_ref.shape
     row = lax.broadcasted_iota(jnp.int32, (count, count), 0)
     column = lax.broadcasted_iota(jnp.int32, (count, count), 1)
@@ -59,46 +67,67 @@
             )
         )
         outs[-1].start()
+    last.wait()
+    share_ref[...] = jnp.dot(
+        select, own_ref[...], preferred_element_type=jnp.float32
+    ).astype(share_ref.dtype)
     for copy in outs:
         copy.wait()
 
 
-def route(owner, limits, assignments, tokens, capacity, chunks=4):
-    count, width = tokens.shape
+def route(owner, part, limits, assignments, tokens, capacity, share, parts, chunks=3):
+    count = tokens.shape[0]
+    width = tokens.shape[1] - parts * share
     far = pl.BlockSpec(memory_space=pltpu.HBM)
+    near = pl.BlockSpec(memory_space=pltpu.VMEM)
     return pl.pallas_call(
         route_kernel,
-        in_specs=[pl.BlockSpec(memory_space=pltpu.SMEM), far, far, far],
-        out_specs=[pl.BlockSpec(memory_space=pltpu.VMEM), far],
+        in_specs=[pl.BlockSpec(memory_space=pltpu.SMEM)] * 2 + [far] * 3,
+        out_specs=[near, far, near],
         out_shape=[
             jax.ShapeDtypeStruct((capacity, count), jnp.bfloat16),
             jax.ShapeDtypeStruct((capacity, width), jnp.bfloat16),
+            jax.ShapeDtypeStruct((capacity, share), jnp.bfloat16),
         ],
         scratch_shapes=[
             pltpu.SMEM(limits.shape, jnp.int32),
             pltpu.VMEM(assignments.shape, jnp.int32),
             pltpu.VMEM((count, width), jnp.bfloat16),
+            pltpu.VMEM((count, share), jnp.bfloat16),
             pltpu.VMEM((capacity, width), jnp.bfloat16),
-            pltpu.SemaphoreType.DMA((chunks + 2,)),
+            pltpu.SemaphoreType.DMA((chunks + 3,)),
             pltpu.SemaphoreType.DMA((chunks,)),
         ],
         compiler_params=pltpu.CompilerParams(vmem_limit_bytes=ALL_VMEM),
         cost_estimate=pl.CostEstimate(
-            flops=2 * capacity * count * width,
-            bytes_accessed=2 * (count + capacity) * width,
+            flops=2 * capacity * count * (width + share),
+            bytes_accessed=2 * (count + capacity) * (width + share),
             transcendentals=0,
         ),
         name="route",
-    )(owner, limits, assignments, tokens)
-
-
-def ffn_kernel(rows_hbm, gate_hbm, up_hbm, gate2_hbm, up2_hbm, out_ref, rows_ref, weight_ref, sems):
-    chunks, chunk, width = weight_ref.shape
-    units = width // 4
+    )(owner, part, limits, assignments, tokens)
+
+
+def ffn_kernel(
+    rows_hbm, last_hbm, gate_hbm, up_hbm, gate2_hbm, up2_hbm, out_ref, rows_ref, weight_ref, sems
+):
+    chunks, chunk, columns = weight_ref.shape
+    units = columns // 4
+    share = last_hbm.shape[2]
+    main = rows_hbm.shape[1] // chunk
     copies = []
     for index in range(chunks):
         part = pl.ds(index * chunk, chunk)
-        ends = [(rows_hbm.at[:, part], rows_ref.at[index])]
+        if index < main:
+            ends = [(rows_hbm.at[:, part], rows_ref.at[index])]
+        else:
+            ends = [
+                (
+                    last_hbm.at[(index - main) * (chunk // share) + place],
+                    rows_ref.at[index, :, pl.ds(place * share, share)],
+                )
+                for place in range(chunk // share)
+            ]
         for place, ref in enumerate((gate_hbm, up_hbm, gate2_hbm, up2_hbm)):
             ends.append(
                 (ref.at[part, :], weight_ref.at[index, :, pl.ds(place * units, units)])
@@ -127,28 +156,28 @@
         out_ref[:, side * units : (side + 1) * units] = hidden.astype(out_ref.dtype)
 
 
-def ffn(rows, gate, up, gate2, up2, chunk=512):
-    count, width = rows.shape
-    units = gate.shape[1]
+def ffn(rows, last, gate, up, gate2, up2, chunk=512):
+    count = rows.shape[0]
+    width, units = gate.shape
     chunks = width // chunk
     return pl.pallas_call(
         ffn_kernel,
-        in_specs=[pl.BlockSpec(memory_space=pltpu.HBM)] * 5,
+        in_specs=[pl.BlockSpec(memory_space=pltpu.HBM)] * 6,
         out_specs=pl.BlockSpec(memory_space=pltpu.VMEM),
         out_shape=jax.ShapeDtypeStruct((count, 2 * units), jnp.bfloat16),
         scratch_shapes=[
             pltpu.VMEM((chunks, count, chunk), jnp.bfloat16),
             pltpu.VMEM((chunks, chunk, 4 * units), jnp.bfloat16),
-            pltpu.SemaphoreType.DMA((chunks, 5)),
+            pltpu.SemaphoreType.DMA((chunks, 4 + chunk // last.shape[2])),
         ],
-        compiler_params=pltpu.CompilerParams(vmem_limit_bytes=ALL_VMEM),
+        compiler_params=pltpu.CompilerParams(vmem_limit_bytes=FFN_VMEM),
         cost_estimate=pl.CostEstimate(
             flops=8 * count * width * units,
             bytes_accessed=2 * count * width + 8 * width * units,
             transcendentals=2 * count * units,
         ),
         name="ffn",
-    )(rows, gate, up, gate2, up2)
+    )(rows, last, gate, up, gate2, up2)
 
 
 def down_kernel(hidden_ref, down_ref, down2_ref, out_ref):
@@ -211,39 +240,53 @@
     rings = lax.axis_size("y")
     shards = rings * CORES
     owners = lax.axis_size("exp")
+    parts = lax.axis_size("tp")
     capacity = min(local_rows, max(2, 3 * local_rows * TOP // (2 * experts)))
     out_rows = local_rows // owners
     target = local_rows * shards * TOP / experts
     owner = lax.axis_index("exp")
 
-    select, expert_rows = route(
-        jnp.reshape(owner, (1,)).astype(jnp.int32), limits, assignments.T, tokens, capacity
-    )
-    rows = lax.all_gather(expert_rows, "y", axis=0, tiled=True)
-
-    w_gate, w_up, w_down, tokens2, _ = lax.optimization_barrier(
-        (gate_weight[0], up_weight[0], down_weight[0], tokens, expert_rows)
+    place = [jnp.reshape(lax.axis_index(axis), (1,)) for axis in ("exp", "tp")]
+    select, main, share = route(*place, limits, assignments.T, tokens, capacity, SHARE, parts)
+    rows = lax.all_gather(main, "y", axis=0, tiled=True)
+
+    w_gate, w_up, w_down, tokens2, share, _ = lax.optimization_barrier(
+        (gate_weight[0], up_weight[0], down_weight[0], tokens, share, main)
     )
     gate2, up2, down2 = swap_cores(w_gate), swap_cores(w_up), swap_cores(w_down)
-
     logits = lax.dot_general(
         router_weight, tokens2, (((0,), (1,)), ((), ())), preferred_element_type=jnp.float32
     )
-    capped = SOFT_CAP * jnp.tanh(logits / SOFT_CAP)
-    scores = lax.all_gather(capped, ("y", "core"), axis=0)
-    weights = jnp.exp(scores)
+    scores = SOFT_CAP * jnp.tanh(logits / SOFT_CAP)
+    pieces = []
+    for piece in range(3):
+        pieces.append(lax.reduce_precision(scores, exponent_bits=8, mantissa_bits=7))
+        scores = scores - pieces[-1]
+    pieces = jnp.concatenate(pieces, axis=0).astype(jnp.bfloat16)
+    count = pieces.shape[0]
+    slots = TAIL * SHARE // local_rows
+    pieces = jnp.pad(pieces, ((0, slots - count), (0, 0))).reshape(TAIL, SHARE)
+    payload = jnp.concatenate([share, pieces], axis=0)
+    near = lax.all_to_all(
+        jnp.broadcast_to(payload, (rings,) + payload.shape), "y", 0, 0
+    )
+    own_share = near[:, :capacity].reshape(rings * capacity, SHARE)
+    last = lax.all_gather(own_share, "tp", axis=0)
+
+    tail = near[:, capacity:].reshape(rings, slots, local_rows)[:, :count]
+    tail = jnp.sum(tail.reshape(rings, 3, experts, local_rows).astype(jnp.float32), axis=1)
+    weights = jnp.exp(jnp.concatenate([tail, swap_cores(tail)], axis=0))
     weights = weights * (TOP / jnp.sum(weights, axis=1, keepdims=True))
     for repeat in range(ITERS):
         weights = weights * (target / jnp.sum(weights, axis=(0, 2), keepdims=True))
         weights = weights * (TOP / jnp.sum(weights, axis=1, keepdims=True))
-    shard = lax.axis_index("y") * CORES + lax.axis_index("core")
-    own = lax.dynamic_slice(weights, (shard, owner, 0), (1, 1, local_rows))[0]
-
-    hidden = ffn(rows, w_gate, w_up, gate2, up2)
+    own = lax.dynamic_slice(weights, (lax.axis_index("y"), owner, 0), (1, 1, local_rows))[0]
+
+    hidden = ffn(rows, last, w_gate, w_up, gate2, up2)
     full_hidden = lax.all_gather(hidden, "tp", axis=0)
     partial = down(full_hidden, w_down, down2)
-    parts = lax.all_to_all(partial.reshape(rings, capacity, partial.shape[1]), "y", 0, 0)
-    shares = weigh(parts, select, own)
+    sums = lax.all_to_all(partial.reshape(rings, capacity, partial.shape[1]), "y", 0, 0)
+    shares = weigh(sums, select, own)
     shares = lax.all_to_all(shares.reshape(owners, out_rows, shares.shape[1]), "exp", 0, 0)
     return jnp.sum(shares.astype(jnp.float32), axis=0).astype(jnp.bfloat16)
 

time: 136 us -> 127 us (0.934)
  the two profiles are of different devices: /device:TPU:8 before, /device:TPU:2 now
where the time goes in v6:
time: 127 us
  blocking collectives  46.9 us (37%)
  waiting for transfers between devices  31.3 us (25%)
  starting transfers between devices  20.1 us (16%)
  between operations  13.6 us (11%)
  Pallas kernels  9.68 us (8%)
  other arithmetic  2.56 us (2%)
  matrix products  1.61 us (1%)
    all_to_all x1, blocking collectives, local(): lax.all_to_all(shares.reshape(owners, out_rows, shares.shape[1]), 'exp',...  17.9 us
    all_to_all x1, waiting for transfers between devices, local(): lax.all_to_all(partial.reshape(rings, capacity, partial.shape[1]), 'y', 0...  16.5 us
    all_gather x1, blocking collectives, local(): last = lax.all_gather(own_share, 'tp', axis=0)  15.1 us
    all_gather x1, blocking collectives, local(): full_hidden = lax.all_gather(hidden, 'tp', axis=0)  13.8 us
    all_gather x1, waiting for transfers between devices, local(): rows = lax.all_gather(main, 'y', axis=0, tiled=True)  9.1 us
    ppermute x4, starting transfers between devices, swap_cores(): return lax.ppermute(value, 'core', [(0, 1), (1, 0)])  8.16 us
    all_to_all x1, starting transfers between devices, local(): lax.all_to_all(jnp.broadcast_to(payload, (rings,) + payload.shape), 'y',...  7.1 us
    all_to_all x1, waiting for transfers between devices, local(): lax.all_to_all(jnp.broadcast_to(payload, (rings,) + payload.shape), 'y',...  5.62 us
  transfers between devices with their start and end apart: 7, of which 3 were waited for; matrix products, arithmetic and copies ran while one was open for 3% of the time, Pallas kernels for 4%

profile of v6, /device:TPU:2, one launch (start us, length us, event | category | flops | bytes accessed | tf_op | source)
XLA Modules:
  0.0 126.5 jit_solution(15173753846311260898)
XLA Ops:
  6.5 2.8 %route.1 = (bf16[48,128]{1,0:T(8,128)(2,1)}, bf16[48,3072]{1,0:T(8,128)(2,1)}, bf16[48,256]{1,0:T(8,128)(2,1)}) custom-call(s32[1]{0:T(128)} %bitcast.owner_ref, s32[1]{0:T(128)} %bitcast.1.part_ref, s32[1,8]{1,0:T(1,128)} %limits_hbm.1, s32[2,128]{1,0:T(2,128)} %bitcast.30, bf16[128,4096]{1,0:T(8,128)(2,1)} %tokens_hbm.1), custom_call_target="tpu_custom_call" | custom-call | flops 40894464 | bytes 1171456 | tf_op jit(solution)/shard_map/route/pallas_call | solution.py:83
  9.4 0.0 all-gather.3.cloned.1.call-update
  9.4 1.6 %reduce-precision_convert_fusion.1 = (bf16[8,128]{1,0:T(8,128)(2,1)S(1)}, bf16[8,128]{1,0:T(8,128)(2,1)S(1)}, bf16[8,128]{1,0:T(8,128)(2,1)S(1)}) fusion(bf16[128,4096]{1,0:T(8,128)(2,1)} %tokens_hbm.1, bf16[4096,8]{0,1:T(8,128)(2,1)} %param.8), kind=kOutput, calls=%fused_computation.27 | convolution fusion | flops 8398848 | bytes 1120256 | tf_op jit(solution)/shard_map/dot_general | solution.py:257
  11.0 0.7 pad_maximum_fusion
  11.8 0.7 broadcast_in_dim.2
  12.5 7.1 %all-to-all-start = ((bf16[8,64,256]{2,1,0:T(8,128)(2,1)}), bf16[8,64,256]{2,1,0:T(8,128)(2,1)S(1)}, u32[]{:S(2)}, u32[]{:S(2)}) async-start(bf16[8,64,256]{2,1,0:T(8,128)(2,1)} %broadcast_in_dim.2), calls=%async_computation | async-start | bytes 524288 | tf_op jit(solution)/shard_map/all_to_all | solution.py:270
  19.6 1.9 %collective-permute-start = (bf16[4096,128]{1,0:T(8,128)(2,1)}, bf16[4096,128]{1,0:T(8,128)(2,1)S(1)}, u32[]{:S(2)}, u32[]{:S(2)}) collective-permute-start(bf16[4096,128]{1,0:T(8,128)(2,1)} %bitcast.25), channel_id=1, source_target_pairs={{0,32},{32,0},{1,33},{33,1},{2,34},{34,2},{3,35},{35,3},{4,36},{36... | collective-permute-start | bytes 3145736 | tf_op jit(solution)/shard_map/ppermute | solution.py:19
  21.5 2.4 %collective-permute-start.1 = (bf16[4096,128]{1,0:T(8,128)(2,1)}, bf16[4096,128]{1,0:T(8,128)(2,1)}, u32[]{:S(2)}, u32[]{:S(2)}) collective-permute-start(bf16[4096,128]{1,0:T(8,128)(2,1)} %bitcast.27), channel_id=1, source_target_pairs={{0,32},{32,0},{1,33},{33,1},{2,34},{34,2},{3,35},{35,3},{4,36},{36... | collective-permute-start | bytes 3145736 | tf_op jit(solution)/shard_map/ppermute | solution.py:19
  23.9 1.9 %collective-permute-start.2 = (bf16[512,1024]{1,0:T(8,128)(2,1)}, bf16[512,1024]{1,0:T(8,128)(2,1)S(1)}, u32[]{:S(2)}, u32[]{:S(2)}) collective-permute-start(bf16[512,1024]{1,0:T(8,128)(2,1)} %bitcast.22), channel_id=1, source_target_pairs={{0,32},{32,0},{1,33},{33,1},{2,34},{34,2},{3,35},{35,3},{4,36},{36... | collective-permute-start | bytes 3145736 | tf_op jit(solution)/shard_map/ppermute | solution.py:19
  25.9 5.6 %all-to-all-done = bf16[8,64,256]{2,1,0:T(8,128)(2,1)S(1)} async-done(((bf16[8,64,256]{2,1,0:T(8,128)(2,1)}), bf16[8,64,256]{2,1,0:T(8,128)(2,1)S(1)}, u32[]{:S(2)}, u32[]{:S(2)}) %all-to-all-start) | async-done | bytes 262176 | tf_op jit(solution)/shard_map/all_to_all | solution.py:270
  31.6 1.9 %collective-permute-start.3 = (f32[8,8,128]{2,1,0:T(8,128)S(1)}, f32[8,8,128]{2,1,0:T(8,128)S(1)}, u32[]{:S(2)}, u32[]{:S(2)}) collective-permute-start(f32[8,8,128]{2,1,0:T(8,128)S(1)} %convert_reduce_fusion), channel_id=1, source_target_pairs={{0,32},{32,0},{1,33},{33,1},{2,34},{34,2},{3,35},{35,3},{4,36},{36... | collective-permute-start | bytes 98312 | tf_op jit(solution)/shard_map/ppermute | solution.py:19
  33.5 15.1 %all_gather.13.last_hbm = bf16[4,384,256]{2,1,0:T(8,128)(2,1)} all-gather(bf16[1,384,256]{2,1,0:T(8,128)(2,1)S(1)} %bitcast.29), channel_id=1, replica_groups=mesh['y'=8,'core'=2,'exp'=8,'tp'=4] {'tp'}, dimensions={0}, use_global_device_ids=true | all-gather | bytes 983040 | tf_op jit(solution)/shard_map/all_gather | solution.py:274
  48.6 0.0 collective-permute-done.3
  48.6 0.1 multiply_reduce_fusion.3
  48.8 0.1 fusion.3
  48.9 0.2 multiply_reduce_fusion.2
  49.1 0.1 fusion.15
  49.2 0.1 multiply_reduce_fusion.1
  49.4 0.0 collective-permute-done.gate2_hbm
  49.4 0.0 collective-permute-done.1.up2_hbm
  49.4 9.1 %all-gather.3.cloned.1.call-done.rows_hbm = bf16[384,3072]{1,0:T(8,128)(2,1)} async-done(((bf16[48,3072]{1,0:T(8,128)(2,1)}), bf16[384,3072]{1,0:T(8,128)(2,1)}) %all-gather.3.cloned.1.call-update) | async-done | bytes 2359312 | tf_op jit(solution)/shard_map/all_gather | solution.py:251
  58.5 4.7 %ffn.1 = bf16[384,256]{1,0:T(8,128)(2,1)} custom-call(bf16[384,3072]{1,0:T(8,128)(2,1)} %all-gather.3.cloned.1.call-done.rows_hbm, bf16[4,384,256]{2,1,0:T(8,128)(2,1)} %all_gather.13.last_hbm, bf16[4096,128]{1,0:T(8,128)(2,1)} %bitcast.26, bf16[4096,128]{1,0:T(8,128)(2,1)} %bitcast.28, bf16[4096,128]{1,0:T(8,128)(2,1)} %copy-done.2, ...), custom_call_target="tpu_custom_call" | custom-call | flops 1610612736 | bytes 7340032 | tf_op jit(solution)/shard_map/ffn/pallas_call | solution.py:163
  63.2 13.8 %all-gather = bf16[1536,256]{1,0:T(8,128)(2,1)S(1)} all-gather(bf16[384,256]{1,0:T(8,128)(2,1)} %ffn.1), channel_id=2, replica_groups=mesh['y'=8,'core'=2,'exp'=8,'tp'=4] {'tp'}, dimensions={0}, use_global_device_ids=true | all-gather | bytes 983040 | tf_op jit(solution)/shard_map/all_gather | solution.py:286
  77.1 1.9 %down.1 = bf16[384,1024]{1,0:T(8,128)(2,1)} custom-call(bf16[4,384,256]{2,1,0:T(8,128)(2,1)S(1)} %bitcast.21, bf16[512,1024]{1,0:T(8,128)(2,1)S(1)} %bitcast.23, bf16[512,1024]{1,0:T(8,128)(2,1)S(1)} %collective-permute-done.2.down2_ref), custom_call_target="tpu_custom_call" | custom-call | flops 805306368 | bytes 3670016 | tf_op jit(solution)/shard_map/down/pallas_call | solution.py:198
  78.9 4.8 %all-to-all-start.1 = ((bf16[8,48,1024]{2,1,0:T(8,128)(2,1)}), bf16[8,48,1024]{2,1,0:T(8,128)(2,1)S(1)}, u32[]{:S(2)}, u32[]{:S(2)}) async-start(bf16[8,48,1024]{2,1,0:T(8,128)(2,1)} %bitcast.9), calls=%async_computation.1 | async-start | bytes 1572864 | tf_op jit(solution)/shard_map/all_to_all | solution.py:288
  83.8 0.1 fusion.4
  83.9 0.2 multiply_reduce_fusion
  84.1 0.1 fusion.14
  84.2 16.5 %all-to-all-done.1.parts_ref = bf16[8,48,1024]{2,1,0:T(8,128)(2,1)S(1)} async-done(((bf16[8,48,1024]{2,1,0:T(8,128)(2,1)}), bf16[8,48,1024]{2,1,0:T(8,128)(2,1)S(1)}, u32[]{:S(2)}, u32[]{:S(2)}) %all-to-all-start.1) | async-done | bytes 786464 | tf_op jit(solution)/shard_map/all_to_all | solution.py:288
  100.8 0.3 weigh.1
  101.1 17.9 %all_to_all.15 = bf16[8,16,1024]{2,1,0:T(8,128)(2,1)S(1)} all-to-all(bf16[8,16,1024]{2,1,0:T(8,128)(2,1)S(1)} %bitcast.24), channel_id=1, replica_groups=mesh['y'=8,'core'=2,'exp'=8,'tp'=4] {'exp'}, dimensions={0} | all-to-all | bytes 524288 | tf_op jit(solution)/shard_map/all_to_all | solution.py:290
  119.0 0.7 reduce_sum.112
  (26 shorter events, 0.2 us)
Async XLA Ops:
  6.5 52.0 %all-gather.3.cloned.1.call-start = ((), (), s32[]{:S(2)}) async-start(), calls=%async_computation.3 | async-start | bytes 2654208 | tf_op jit(solution)/shard_map/all_gather | solution.py:251
  12.5 19.0 %all-to-all-start = ((bf16[8,64,256]{2,1,0:T(8,128)(2,1)}), bf16[8,64,256]{2,1,0:T(8,128)(2,1)S(1)}, u32[]{:S(2)}, u32[]{:S(2)}) async-start(bf16[8,64,256]{2,1,0:T(8,128)(2,1)} %broadcast_in_dim.2), calls=%async_computation | async-start | bytes 524288 | tf_op jit(solution)/shard_map/all_to_all | solution.py:270
  19.6 29.8 %collective-permute-start = (bf16[4096,128]{1,0:T(8,128)(2,1)}, bf16[4096,128]{1,0:T(8,128)(2,1)S(1)}, u32[]{:S(2)}, u32[]{:S(2)}) collective-permute-start(bf16[4096,128]{1,0:T(8,128)(2,1)} %bitcast.25), channel_id=1, source_target_pairs={{0,32},{32,0},{1,33},{33,1},{2,34},{34,2},{3,35},{35,3},{4,36},{36... | collective-permute-start | bytes 3145736 | tf_op jit(solution)/shard_map/ppermute | solution.py:19
  21.5 27.9 %collective-permute-start.1 = (bf16[4096,128]{1,0:T(8,128)(2,1)}, bf16[4096,128]{1,0:T(8,128)(2,1)}, u32[]{:S(2)}, u32[]{:S(2)}) collective-permute-start(bf16[4096,128]{1,0:T(8,128)(2,1)} %bitcast.27), channel_id=1, source_target_pairs={{0,32},{32,0},{1,33},{33,1},{2,34},{34,2},{3,35},{35,3},{4,36},{36... | collective-permute-start | bytes 3145736 | tf_op jit(solution)/shard_map/ppermute | solution.py:19
  23.9 53.1 %collective-permute-start.2 = (bf16[512,1024]{1,0:T(8,128)(2,1)}, bf16[512,1024]{1,0:T(8,128)(2,1)S(1)}, u32[]{:S(2)}, u32[]{:S(2)}) collective-permute-start(bf16[512,1024]{1,0:T(8,128)(2,1)} %bitcast.22), channel_id=1, source_target_pairs={{0,32},{32,0},{1,33},{33,1},{2,34},{34,2},{3,35},{35,3},{4,36},{36... | collective-permute-start | bytes 3145736 | tf_op jit(solution)/shard_map/ppermute | solution.py:19
  31.6 17.0 %collective-permute-start.3 = (f32[8,8,128]{2,1,0:T(8,128)S(1)}, f32[8,8,128]{2,1,0:T(8,128)S(1)}, u32[]{:S(2)}, u32[]{:S(2)}) collective-permute-start(f32[8,8,128]{2,1,0:T(8,128)S(1)} %convert_reduce_fusion), channel_id=1, source_target_pairs={{0,32},{32,0},{1,33},{33,1},{2,34},{34,2},{3,35},{35,3},{4,36},{36... | collective-permute-start | bytes 98312 | tf_op jit(solution)/shard_map/ppermute | solution.py:19
  49.4 27.7 %copy-start = (bf16[1,512,1024]{2,1,0:T(8,128)(2,1)S(1)}, bf16[1,512,1024]{2,1,0:T(8,128)(2,1)}, u32[]{:S(2)}) copy-start(bf16[1,512,1024]{2,1,0:T(8,128)(2,1)} %param.11) | copy-start | bytes 3145732
  49.4 9.1 %copy-start.2 = (bf16[4096,128]{1,0:T(8,128)(2,1)}, bf16[4096,128]{1,0:T(8,128)(2,1)S(1)}, u32[]{:S(2)}) copy-start(bf16[4096,128]{1,0:T(8,128)(2,1)S(1)} %collective-permute-done.gate2_hbm) | copy-start | bytes 3145732
  77.1 23.7 %copy-start.1 = (bf16[48,128]{1,0:T(8,128)(2,1)S(1)}, bf16[48,128]{1,0:T(8,128)(2,1)}, u32[]{:S(2)}) copy-start(bf16[48,128]{1,0:T(8,128)(2,1)} %get-tuple-element.20.select_ref) | copy-start | bytes 36868
  78.9 21.8 %all-to-all-start.1 = ((bf16[8,48,1024]{2,1,0:T(8,128)(2,1)}), bf16[8,48,1024]{2,1,0:T(8,128)(2,1)S(1)}, u32[]{:S(2)}, u32[]{:S(2)}) async-start(bf16[8,48,1024]{2,1,0:T(8,128)(2,1)} %bitcast.9), calls=%async_computation.1 | async-start | bytes 1572864 | tf_op jit(solution)/shard_map/all_to_all | solution.py:288
Sparse Core Ops, SparseCore 0:
  9.5 48.9 all-gather.2

commit v7 on v6

--- a/solution.py
+++ b/solution.py
@@ -108,26 +108,66 @@
     )(owner, part, limits, assignments, tokens)
 
 
+def prepare_kernel(
+    last_hbm, gate_hbm, up_hbm, gate2_hbm, up2_hbm, total_ref, last_ref, weight_ref, sems
+):
+    shares, _, share = last_ref.shape
+    width, units = gate_hbm.shape
+    tail = pl.ds(width - shares * share, shares * share)
+    copies = [pltpu.make_async_copy(last_hbm, last_ref, sems.at[0])]
+    for place, ref in enumerate((gate_hbm, up_hbm, gate2_hbm, up2_hbm)):
+        copies.append(
+            pltpu.make_async_copy(
+                ref.at[tail, :], weight_ref.at[:, pl.ds(place * units, units)], sems.at[1 + place]
+            )
+        )
+    for copy in copies:
+        copy.start()
+    for copy in copies:
+        copy.wait()
+    total = None
+    for index in range(shares):
+        product = jnp.dot(
+            last_ref[index],
+            weight_ref[pl.ds(index * share, share), :],
+            preferred_element_type=jnp.float32,
+        )
+        total = product if index == 0 else total + product
+    total_ref[...] = total
+
+
+def prepare(last, gate, up, gate2, up2):
+    shares, count, share = last.shape
+    units = gate.shape[1]
+    return pl.pallas_call(
+        prepare_kernel,
+        in_specs=[pl.BlockSpec(memory_space=pltpu.HBM)] * 5,
+        out_specs=pl.BlockSpec(memory_space=pltpu.VMEM),
+        out_shape=pltpu.VMEM((count, 4 * units), jnp.float32),
+        scratch_shapes=[
+            pltpu.VMEM(last.shape, jnp.bfloat16),
+            pltpu.VMEM((shares * share, 4 * units), jnp.bfloat16),
+            pltpu.SemaphoreType.DMA((5,)),
+        ],
+        compiler_params=pltpu.CompilerParams(vmem_limit_bytes=FFN_VMEM),
+        cost_estimate=pl.CostEstimate(
+            flops=8 * count * shares * share * units,
+            bytes_accessed=2 * shares * share * (count + 4 * units) + 16 * count * units,
+            transcendentals=0,
+        ),
+        name="prepare",
+    )(last, gate, up, gate2, up2)
+
+
 def ffn_kernel(
-    rows_hbm, last_hbm, gate_hbm, up_hbm, gate2_hbm, up2_hbm, out_ref, rows_ref, weight_ref, sems
+    rows_hbm, gate_hbm, up_hbm, gate2_hbm, up2_hbm, start_ref, out_ref, rows_ref, weight_ref, sems
 ):
     chunks, chunk, columns = weight_ref.shape
     units = columns // 4
-    share = last_hbm.shape[2]
-    main = rows_hbm.shape[1] // chunk
     copies = []
     for index in range(chunks):
         part = pl.ds(index * chunk, chunk)
-        if index < main:
-            ends = [(rows_hbm.at[:, part], rows_ref.at[index])]
-        else:
-            ends = [
-                (
-                    last_hbm.at[(index - main) * (chunk // share) + place],
-                    rows_ref.at[index, :, pl.ds(place * share, share)],
-                )
-                for place in range(chunk // share)
-            ]
+        ends = [(rows_hbm.at[:, part], rows_ref.at[index])]
         for place, ref in enumerate((gate_hbm, up_hbm, gate2_hbm, up2_hbm)):
             ends.append(
                 (ref.at[part, :], weight_ref.at[index, :, pl.ds(place * units, units)])
@@ -141,14 +181,13 @@
     for group in copies:
         for copy in group:
             copy.start()
-    total = None
+    total = start_ref[...]
     for index, group in enumerate(copies):
         for copy in group:
             copy.wait()
-        product = jnp.dot(
+        total = total + jnp.dot(
             rows_ref[index], weight_ref[index], preferred_element_type=jnp.float32
         )
-        total = product if index == 0 else total + product
     for side in range(2):
         gate = total[:, 2 * side * units : (2 * side + 1) * units]
         up = total[:, (2 * side + 1) * units : (2 * side + 2) * units]
@@ -156,28 +195,28 @@
         out_ref[:, side * units : (side + 1) * units] = hidden.astype(out_ref.dtype)
 
 
-def ffn(rows, last, gate, up, gate2, up2, chunk=512):
-    count = rows.shape[0]
-    width, units = gate.shape
-    chunks = width // chunk
+def ffn(rows, gate, up, gate2, up2, start, chunk=512):
+    count, main = rows.shape
+    units = gate.shape[1]
+    near = pl.BlockSpec(memory_space=pltpu.VMEM)
     return pl.pallas_call(
         ffn_kernel,
-        in_specs=[pl.BlockSpec(memory_space=pltpu.HBM)] * 6,
-        out_specs=pl.BlockSpec(memory_space=pltpu.VMEM),
-        out_shape=jax.ShapeDtypeStruct((count, 2 * units), jnp.bfloat16),
+        in_specs=[pl.BlockSpec(memory_space=pltpu.HBM)] * 5 + [near],
+        out_specs=near,
+        out_shape=pltpu.VMEM((count, 2 * units), jnp.bfloat16),
         scratch_shapes=[
-            pltpu.VMEM((chunks, count, chunk), jnp.bfloat16),
-            pltpu.VMEM((chunks, chunk, 4 * units), jnp.bfloat16),
-            pltpu.SemaphoreType.DMA((chunks, 4 + chunk // last.shape[2])),
+            pltpu.VMEM((main // chunk, count, chunk), jnp.bfloat16),
+            pltpu.VMEM((main // chunk, chunk, 4 * units), jnp.bfloat16),
+            pltpu.SemaphoreType.DMA((main // chunk, 5)),
         ],
         compiler_params=pltpu.CompilerParams(vmem_limit_bytes=FFN_VMEM),
         cost_estimate=pl.CostEstimate(
-            flops=8 * count * width * units,
-            bytes_accessed=2 * count * width + 8 * width * units,
+            flops=8 * count * main * units,
+            bytes_accessed=2 * count * main + 8 * main * units,
             transcendentals=2 * count * units,
         ),
         name="ffn",
-    )(rows, last, gate, up, gate2, up2)
+    )(rows, gate, up, gate2, up2, start)
 
 
 def down_kernel(hidden_ref, down_ref, down2_ref, out_ref):
@@ -197,7 +236,7 @@
     columns = weight.shape[1]
     return pl.pallas_call(
         down_kernel,
-        out_shape=jax.ShapeDtypeStruct((count, columns), jnp.bfloat16),
+        out_shape=pltpu.VMEM((count, columns), jnp.bfloat16),
         compiler_params=pltpu.CompilerParams(vmem_limit_bytes=24 << 20),
         cost_estimate=pl.CostEstimate(
             flops=2 * parts * count * units * columns,
@@ -282,7 +321,9 @@
         weights = weights * (TOP / jnp.sum(weights, axis=1, keepdims=True))
     own = lax.dynamic_slice(weights, (lax.axis_index("y"), owner, 0), (1, 1, local_rows))[0]
 
-    hidden = ffn(rows, last, w_gate, w_up, gate2, up2)
+    start = prepare(last, w_gate, w_up, gate2, up2)
+    start = pltpu.with_memory_space_constraint(start, pltpu.VMEM)
+    hidden = ffn(rows, w_gate, w_up, gate2, up2, start)
     full_hidden = lax.all_gather(hidden, "tp", axis=0)
     partial = down(full_hidden, w_down, down2)
     sums = lax.all_to_all(partial.reshape(rings, capacity, partial.shape[1]), "y", 0, 0)

time: 127 us -> 126 us (level)
  waiting for transfers between devices: 31.3 us -> 28.9 us
    all_gather x1, waiting for transfers between devices: 9.1 us -> 6.07 us  [local(): rows = lax.all_gather(main, 'y', axis=0, tiled=True)]
    pallas_call x1 -> x2, Pallas kernels: 1.87 us -> 3.92 us  [the longest x1 2.05 us: prepare(): pl.pallas_call(prepare_kernel, in_specs=[pl.BlockSpec(memory_space=pltpu....]
    pallas_call x1, Pallas kernels: 4.7 us -> 3.24 us  [ffn(): pl.pallas_call(ffn_kernel, in_specs=[pl.BlockSpec(memory_space=pltpu.HBM)...]
where the time goes in v7:
time: 126 us; the launch traced here: 125 us
  blocking collectives  47.1 us (37%)
  waiting for transfers between devices  28.9 us (23%)
  starting transfers between devices  19.6 us (16%)
  between operations  13.6 us (11%)
  Pallas kernels  10.3 us (8%)
  other arithmetic  2.56 us (2%)
  local copies, waits for them, and re-layouts  1.79 us (1%)
  matrix products  1.61 us (1%)
    all_to_all x1, blocking collectives, local(): lax.all_to_all(shares.reshape(owners, out_rows, shares.shape[1]), 'exp',...  18.4 us
    all_to_all x1, waiting for transfers between devices, local(): lax.all_to_all(partial.reshape(rings, capacity, partial.shape[1]), 'y', 0...  17.2 us
    all_gather x1, blocking collectives, local(): last = lax.all_gather(own_share, 'tp', axis=0)  15.1 us
    all_gather x1, blocking collectives, local(): full_hidden = lax.all_gather(hidden, 'tp', axis=0)  13.6 us
    ppermute x4, starting transfers between devices, swap_cores(): return lax.ppermute(value, 'core', [(0, 1), (1, 0)])  8.16 us
    all_to_all x1, starting transfers between devices, local(): lax.all_to_all(jnp.broadcast_to(payload, (rings,) + payload.shape), 'y',...  7.1 us
    all_gather x1, waiting for transfers between devices, local(): rows = lax.all_gather(main, 'y', axis=0, tiled=True)  6.07 us
    all_to_all x1, waiting for transfers between devices, local(): lax.all_to_all(jnp.broadcast_to(payload, (rings,) + payload.shape), 'y',...  5.62 us
  transfers between devices with their start and end apart: 7, of which 3 were waited for; matrix products, arithmetic and copies ran while one was open for 3% of the time, Pallas kernels for 4%

profile of v7, /device:TPU:2, one launch (start us, length us, event | category | flops | bytes accessed | tf_op | source)
XLA Modules:
  0.0 125.5 jit_solution(7695205195109239578)
XLA Ops:
  6.5 2.8 %route.1 = (bf16[48,128]{1,0:T(8,128)(2,1)}, bf16[48,3072]{1,0:T(8,128)(2,1)}, bf16[48,256]{1,0:T(8,128)(2,1)}) custom-call(s32[1]{0:T(128)} %bitcast.owner_ref, s32[1]{0:T(128)} %bitcast.1.part_ref, s32[1,8]{1,0:T(1,128)} %limits_hbm.1, s32[2,128]{1,0:T(2,128)} %bitcast.32, bf16[128,4096]{1,0:T(8,128)(2,1)} %tokens_hbm.1), custom_call_target="tpu_custom_call" | custom-call | flops 40894464 | bytes 1171456 | tf_op jit(solution)/shard_map/route/pallas_call | solution.py:83
  9.4 0.0 all-gather.3.cloned.1.call-update
  9.4 1.6 %reduce-precision_convert_fusion.1 = (bf16[8,128]{1,0:T(8,128)(2,1)S(1)}, bf16[8,128]{1,0:T(8,128)(2,1)S(1)}, bf16[8,128]{1,0:T(8,128)(2,1)S(1)}) fusion(bf16[128,4096]{1,0:T(8,128)(2,1)} %tokens_hbm.1, bf16[4096,8]{0,1:T(8,128)(2,1)} %param.8), kind=kOutput, calls=%fused_computation.27 | convolution fusion | flops 8398848 | bytes 1120256 | tf_op jit(solution)/shard_map/dot_general | solution.py:296
  11.0 0.7 pad_maximum_fusion
  11.8 0.7 broadcast_in_dim.2
  12.5 7.1 %all-to-all-start = ((bf16[8,64,256]{2,1,0:T(8,128)(2,1)}), bf16[8,64,256]{2,1,0:T(8,128)(2,1)S(1)}, u32[]{:S(2)}, u32[]{:S(2)}) async-start(bf16[8,64,256]{2,1,0:T(8,128)(2,1)} %broadcast_in_dim.2), calls=%async_computation | async-start | bytes 524288 | tf_op jit(solution)/shard_map/all_to_all | solution.py:309
  19.6 1.9 %collective-permute-start = (bf16[4096,128]{1,0:T(8,128)(2,1)}, bf16[4096,128]{1,0:T(8,128)(2,1)S(1)}, u32[]{:S(2)}, u32[]{:S(2)}) collective-permute-start(bf16[4096,128]{1,0:T(8,128)(2,1)} %bitcast.25), channel_id=1, source_target_pairs={{0,32},{32,0},{1,33},{33,1},{2,34},{34,2},{3,35},{35,3},{4,36},{36... | collective-permute-start | bytes 3145736 | tf_op jit(solution)/shard_map/ppermute | solution.py:19
  21.5 2.4 %collective-permute-start.1 = (bf16[4096,128]{1,0:T(8,128)(2,1)}, bf16[4096,128]{1,0:T(8,128)(2,1)}, u32[]{:S(2)}, u32[]{:S(2)}) collective-permute-start(bf16[4096,128]{1,0:T(8,128)(2,1)} %bitcast.28), channel_id=1, source_target_pairs={{0,32},{32,0},{1,33},{33,1},{2,34},{34,2},{3,35},{35,3},{4,36},{36... | collective-permute-start | bytes 3145736 | tf_op jit(solution)/shard_map/ppermute | solution.py:19
  23.9 1.9 %collective-permute-start.2 = (bf16[512,1024]{1,0:T(8,128)(2,1)}, bf16[512,1024]{1,0:T(8,128)(2,1)S(1)}, u32[]{:S(2)}, u32[]{:S(2)}) collective-permute-start(bf16[512,1024]{1,0:T(8,128)(2,1)} %bitcast.22), channel_id=1, source_target_pairs={{0,32},{32,0},{1,33},{33,1},{2,34},{34,2},{3,35},{35,3},{4,36},{36... | collective-permute-start | bytes 3145736 | tf_op jit(solution)/shard_map/ppermute | solution.py:19
  25.9 5.6 %all-to-all-done = bf16[8,64,256]{2,1,0:T(8,128)(2,1)S(1)} async-done(((bf16[8,64,256]{2,1,0:T(8,128)(2,1)}), bf16[8,64,256]{2,1,0:T(8,128)(2,1)S(1)}, u32[]{:S(2)}, u32[]{:S(2)}) %all-to-all-start) | async-done | bytes 262176 | tf_op jit(solution)/shard_map/all_to_all | solution.py:309
  31.6 1.9 %collective-permute-start.3 = (f32[8,8,128]{2,1,0:T(8,128)S(1)}, f32[8,8,128]{2,1,0:T(8,128)S(1)}, u32[]{:S(2)}, u32[]{:S(2)}) collective-permute-start(f32[8,8,128]{2,1,0:T(8,128)S(1)} %convert_reduce_fusion), channel_id=1, source_target_pairs={{0,32},{32,0},{1,33},{33,1},{2,34},{34,2},{3,35},{35,3},{4,36},{36... | collective-permute-start | bytes 98312 | tf_op jit(solution)/shard_map/ppermute | solution.py:19
  33.5 15.1 %all_gather.13.last_hbm = bf16[4,384,256]{2,1,0:T(8,128)(2,1)} all-gather(bf16[1,384,256]{2,1,0:T(8,128)(2,1)S(1)} %bitcast.31), channel_id=1, replica_groups=mesh['y'=8,'core'=2,'exp'=8,'tp'=4] {'tp'}, dimensions={0}, use_global_device_ids=true | all-gather | bytes 983040 | tf_op jit(solution)/shard_map/all_gather | solution.py:313
  48.6 0.1 multiply_reduce_fusion.3
  48.8 0.1 fusion.3
  48.9 0.2 multiply_reduce_fusion.2
  49.1 0.1 fusion.15
  49.2 0.1 multiply_reduce_fusion.1
  49.4 1.0 copy-done.2
  50.4 2.0 %prepare.1.start_ref = f32[384,512]{1,0:T(8,128)S(1)} custom-call(bf16[4,384,256]{2,1,0:T(8,128)(2,1)} %all_gather.13.last_hbm, bf16[4096,128]{1,0:T(8,128)(2,1)} %bitcast.26, bf16[4096,128]{1,0:T(8,128)(2,1)} %bitcast.29, bf16[4096,128]{1,0:T(8,128)(2,1)} %copy-done.2, bf16[4096,128]{1,0:T(8,128)(2,1)} %collective-permute-done.1.up2_hbm), custom_call_target="tpu_custom_call" | custom-call | flops 402653184 | bytes 2621440 | tf_op jit(solution)/shard_map/prepare/pallas_call | solution.py:142
  52.4 0.0 copy-start
  52.5 6.1 %all-gather.3.cloned.1.call-done.rows_hbm = bf16[384,3072]{1,0:T(8,128)(2,1)} async-done(((bf16[48,3072]{1,0:T(8,128)(2,1)}), bf16[384,3072]{1,0:T(8,128)(2,1)}) %all-gather.3.cloned.1.call-update) | async-done | bytes 2359312 | tf_op jit(solution)/shard_map/all_gather | solution.py:290
  58.5 3.2 %ffn.1 = bf16[384,256]{1,0:T(8,128)(2,1)S(1)} custom-call(bf16[384,3072]{1,0:T(8,128)(2,1)} %all-gather.3.cloned.1.call-done.rows_hbm, bf16[4096,128]{1,0:T(8,128)(2,1)} %bitcast.27, bf16[4096,128]{1,0:T(8,128)(2,1)} %bitcast.30, bf16[4096,128]{1,0:T(8,128)(2,1)} %copy-done.2, bf16[4096,128]{1,0:T(8,128)(2,1)} %collective-permute-done.1.up2_hbm, ...), custom_call_target="tpu_custom_call" | custom-call | flops 1207959552 | bytes 5505024 | tf_op jit(solution)/shard_map/ffn/pallas_call | solution.py:202
  61.8 13.6 %all-gather = bf16[1536,256]{1,0:T(8,128)(2,1)S(1)} all-gather(bf16[384,256]{1,0:T(8,128)(2,1)S(1)} %ffn.1), channel_id=2, replica_groups=mesh['y'=8,'core'=2,'exp'=8,'tp'=4] {'tp'}, dimensions={0}, use_global_device_ids=true | all-gather | bytes 983040 | tf_op jit(solution)/shard_map/all_gather | solution.py:327
  75.4 1.9 %down.1 = bf16[384,1024]{1,0:T(8,128)(2,1)} custom-call(bf16[4,384,256]{2,1,0:T(8,128)(2,1)S(1)} %bitcast.21, bf16[512,1024]{1,0:T(8,128)(2,1)S(1)} %bitcast.23, bf16[512,1024]{1,0:T(8,128)(2,1)S(1)} %collective-permute-done.2.down2_ref), custom_call_target="tpu_custom_call" | custom-call | flops 805306368 | bytes 3670016 | tf_op jit(solution)/shard_map/down/pallas_call | solution.py:237
  77.3 4.3 %all-to-all-start.1 = ((bf16[8,48,1024]{2,1,0:T(8,128)(2,1)}), bf16[8,48,1024]{2,1,0:T(8,128)(2,1)S(1)}, u32[]{:S(2)}, u32[]{:S(2)}) async-start(bf16[8,48,1024]{2,1,0:T(8,128)(2,1)} %bitcast.9), calls=%async_computation.1 | async-start | bytes 1572864 | tf_op jit(solution)/shard_map/all_to_all | solution.py:329
  81.6 0.1 fusion.4
  81.7 0.2 multiply_reduce_fusion
  81.9 0.1 fusion.14
  82.1 17.2 %all-to-all-done.1.parts_ref = bf16[8,48,1024]{2,1,0:T(8,128)(2,1)S(1)} async-done(((bf16[8,48,1024]{2,1,0:T(8,128)(2,1)}), bf16[8,48,1024]{2,1,0:T(8,128)(2,1)S(1)}, u32[]{:S(2)}, u32[]{:S(2)}) %all-to-all-start.1) | async-done | bytes 786464 | tf_op jit(solution)/shard_map/all_to_all | solution.py:329
  99.3 0.3 weigh.1
  99.6 18.4 %all_to_all.15 = bf16[8,16,1024]{2,1,0:T(8,128)(2,1)S(1)} all-to-all(bf16[8,16,1024]{2,1,0:T(8,128)(2,1)S(1)} %bitcast.24), channel_id=1, replica_groups=mesh['y'=8,'core'=2,'exp'=8,'tp'=4] {'exp'}, dimensions={0} | all-to-all | bytes 524288 | tf_op jit(solution)/shard_map/all_to_all | solution.py:331
  118.0 0.7 reduce_sum.112
  (27 shorter events, 0.2 us)
Async XLA Ops:
  6.5 52.0 %all-gather.3.cloned.1.call-start = ((), (), s32[]{:S(2)}) async-start(), calls=%async_computation.3 | async-start | bytes 2654208 | tf_op jit(solution)/shard_map/all_gather | solution.py:290
  12.5 19.0 %all-to-all-start = ((bf16[8,64,256]{2,1,0:T(8,128)(2,1)}), bf16[8,64,256]{2,1,0:T(8,128)(2,1)S(1)}, u32[]{:S(2)}, u32[]{:S(2)}) async-start(bf16[8,64,256]{2,1,0:T(8,128)(2,1)} %broadcast_in_dim.2), calls=%async_computation | async-start | bytes 524288 | tf_op jit(solution)/shard_map/all_to_all | solution.py:309
  19.6 29.8 %collective-permute-start = (bf16[4096,128]{1,0:T(8,128)(2,1)}, bf16[4096,128]{1,0:T(8,128)(2,1)S(1)}, u32[]{:S(2)}, u32[]{:S(2)}) collective-permute-start(bf16[4096,128]{1,0:T(8,128)(2,1)} %bitcast.25), channel_id=1, source_target_pairs={{0,32},{32,0},{1,33},{33,1},{2,34},{34,2},{3,35},{35,3},{4,36},{36... | collective-permute-start | bytes 3145736 | tf_op jit(solution)/shard_map/ppermute | solution.py:19
  21.5 27.9 %collective-permute-start.1 = (bf16[4096,128]{1,0:T(8,128)(2,1)}, bf16[4096,128]{1,0:T(8,128)(2,1)}, u32[]{:S(2)}, u32[]{:S(2)}) collective-permute-start(bf16[4096,128]{1,0:T(8,128)(2,1)} %bitcast.28), channel_id=1, source_target_pairs={{0,32},{32,0},{1,33},{33,1},{2,34},{34,2},{3,35},{35,3},{4,36},{36... | collective-permute-start | bytes 3145736 | tf_op jit(solution)/shard_map/ppermute | solution.py:19
  23.9 51.4 %collective-permute-start.2 = (bf16[512,1024]{1,0:T(8,128)(2,1)}, bf16[512,1024]{1,0:T(8,128)(2,1)S(1)}, u32[]{:S(2)}, u32[]{:S(2)}) collective-permute-start(bf16[512,1024]{1,0:T(8,128)(2,1)} %bitcast.22), channel_id=1, source_target_pairs={{0,32},{32,0},{1,33},{33,1},{2,34},{34,2},{3,35},{35,3},{4,36},{36... | collective-permute-start | bytes 3145736 | tf_op jit(solution)/shard_map/ppermute | solution.py:19
  31.6 17.0 %collective-permute-start.3 = (f32[8,8,128]{2,1,0:T(8,128)S(1)}, f32[8,8,128]{2,1,0:T(8,128)S(1)}, u32[]{:S(2)}, u32[]{:S(2)}) collective-permute-start(f32[8,8,128]{2,1,0:T(8,128)S(1)} %convert_reduce_fusion), channel_id=1, source_target_pairs={{0,32},{32,0},{1,33},{33,1},{2,34},{34,2},{3,35},{35,3},{4,36},{36... | collective-permute-start | bytes 98312 | tf_op jit(solution)/shard_map/ppermute | solution.py:19
  49.4 1.0 copy-start.2
  52.4 22.9 %copy-start = (bf16[1,512,1024]{2,1,0:T(8,128)(2,1)S(1)}, bf16[1,512,1024]{2,1,0:T(8,128)(2,1)}, u32[]{:S(2)}) copy-start(bf16[1,512,1024]{2,1,0:T(8,128)(2,1)} %param.11) | copy-start | bytes 3145732
  75.4 23.9 %copy-start.1 = (bf16[48,128]{1,0:T(8,128)(2,1)S(1)}, bf16[48,128]{1,0:T(8,128)(2,1)}, u32[]{:S(2)}) copy-start(bf16[48,128]{1,0:T(8,128)(2,1)} %get-tuple-element.20.select_ref) | copy-start | bytes 36868
  77.3 22.0 %all-to-all-start.1 = ((bf16[8,48,1024]{2,1,0:T(8,128)(2,1)}), bf16[8,48,1024]{2,1,0:T(8,128)(2,1)S(1)}, u32[]{:S(2)}, u32[]{:S(2)}) async-start(bf16[8,48,1024]{2,1,0:T(8,128)(2,1)} %bitcast.9), calls=%async_computation.1 | async-start | bytes 1572864 | tf_op jit(solution)/shard_map/all_to_all | solution.py:329
Sparse Core Ops, SparseCore 0:
  9.5 48.9 all-gather.2

commit v8 on v7

--- a/solution.py
+++ b/solution.py
@@ -323,6 +323,7 @@
 
     start = prepare(last, w_gate, w_up, gate2, up2)
     start = pltpu.with_memory_space_constraint(start, pltpu.VMEM)
+    own, start = lax.optimization_barrier((own, start))
     hidden = ffn(rows, w_gate, w_up, gate2, up2, start)
     full_hidden = lax.all_gather(hidden, "tp", axis=0)
     partial = down(full_hidden, w_down, down2)

time: 126 us -> 137 us (1.087)
  blocking collectives: 47.1 us -> 68.1 us
  waiting for transfers between devices: 28.9 us -> 24.2 us
  starting transfers between devices: 19.6 us -> 15.3 us
    all_to_all x0 -> x1, blocking collectives: none -> 21.4 us  [local(): lax.all_to_all(partial.reshape(rings, capacity, partial.shape[1]), 'y', 0...]
    all_to_all x1 -> x0, waiting for transfers between devices: 17.2 us -> none  [local(): lax.all_to_all(partial.reshape(rings, capacity, partial.shape[1]), 'y', 0...]
    all_gather x1, waiting for transfers between devices: 6.07 us -> 18.6 us  [local(): rows = lax.all_gather(main, 'y', axis=0, tiled=True)]
    all_to_all x1 -> x0, starting transfers between devices: 4.34 us -> none  [local(): lax.all_to_all(partial.reshape(rings, capacity, partial.shape[1]), 'y', 0...]
  transfers between devices with their start and end apart: 7 -> 6, of which waited for: 3 -> 2; matrix products, arithmetic and copies ran while one was open for 3% -> 1% of each run, Pallas kernels for 4% -> 4%
where the time goes in v8:
time: 137 us
  blocking collectives  68.1 us (50%)
  waiting for transfers between devices  24.2 us (18%)
  starting transfers between devices  15.3 us (11%)
  between operations  13.6 us (10%)
  Pallas kernels  9.39 us (7%)
  other arithmetic  2.57 us (2%)
  local copies, waits for them, and re-layouts  1.79 us (1%)
  matrix products  1.61 us (1%)
    all_to_all x1, blocking collectives, local(): lax.all_to_all(partial.reshape(rings, capacity, partial.shape[1]), 'y', 0...  21.4 us
    all_gather x1, waiting for transfers between devices, local(): rows = lax.all_gather(main, 'y', axis=0, tiled=True)  18.6 us
    all_to_all x1, blocking collectives, local(): lax.all_to_all(shares.reshape(owners, out_rows, shares.shape[1]), 'exp',...  17.7 us
    all_gather x1, blocking collectives, local(): last = lax.all_gather(own_share, 'tp', axis=0)  15.1 us
    all_gather x1, blocking collectives, local(): full_hidden = lax.all_gather(hidden, 'tp', axis=0)  13.9 us
    ppermute x4, starting transfers between devices, swap_cores(): return lax.ppermute(value, 'core', [(0, 1), (1, 0)])  8.18 us
    all_to_all x1, starting transfers between devices, local(): lax.all_to_all(jnp.broadcast_to(payload, (rings,) + payload.shape), 'y',...  7.1 us
    all_to_all x1, waiting for transfers between devices, local(): lax.all_to_all(jnp.broadcast_to(payload, (rings,) + payload.shape), 'y',...  4.86 us
  transfers between devices with their start and end apart: 6, of which 2 were waited for; matrix products, arithmetic and copies ran while one was open for 1% of the time, Pallas kernels for 4%

profile of v8, /device:TPU:2, one launch (start us, length us, event | category | flops | bytes accessed | tf_op | source)
XLA Modules:
  0.0 136.6 jit_solution(3054702161854657435)
XLA Ops:
  6.5 2.8 %route.1 = (bf16[48,128]{1,0:T(8,128)(2,1)}, bf16[48,3072]{1,0:T(8,128)(2,1)}, bf16[48,256]{1,0:T(8,128)(2,1)}) custom-call(s32[1]{0:T(128)} %bitcast.owner_ref, s32[1]{0:T(128)} %bitcast.1.part_ref, s32[1,8]{1,0:T(1,128)} %limits_hbm.1, s32[2,128]{1,0:T(2,128)} %bitcast.33, bf16[128,4096]{1,0:T(8,128)(2,1)} %tokens_hbm.1), custom_call_target="tpu_custom_call" | custom-call | flops 40894464 | bytes 1171456 | tf_op jit(solution)/shard_map/route/pallas_call | solution.py:83
  9.4 1.6 %reduce-precision_convert_fusion.1 = (bf16[8,128]{1,0:T(8,128)(2,1)S(1)}, bf16[8,128]{1,0:T(8,128)(2,1)S(1)}, bf16[8,128]{1,0:T(8,128)(2,1)S(1)}) fusion(bf16[128,4096]{1,0:T(8,128)(2,1)} %tokens_hbm.1, bf16[4096,8]{0,1:T(8,128)(2,1)} %param.8), kind=kOutput, calls=%fused_computation.27 | convolution fusion | flops 8398848 | bytes 1120256 | tf_op jit(solution)/shard_map/dot_general | solution.py:296
  11.0 0.7 pad_maximum_fusion
  11.8 0.7 broadcast_in_dim.2
  12.5 7.1 %all-to-all-start = ((bf16[8,64,256]{2,1,0:T(8,128)(2,1)}), bf16[8,64,256]{2,1,0:T(8,128)(2,1)S(1)}, u32[]{:S(2)}, u32[]{:S(2)}) async-start(bf16[8,64,256]{2,1,0:T(8,128)(2,1)} %broadcast_in_dim.2), calls=%async_computation | async-start | bytes 524288 | tf_op jit(solution)/shard_map/all_to_all | solution.py:309
  19.6 0.0 all-gather.3.cloned.1.call-start
  19.6 0.7 all-gather.3.cloned.1.call-update
  20.3 1.9 %collective-permute-start = (bf16[4096,128]{1,0:T(8,128)(2,1)}, bf16[4096,128]{1,0:T(8,128)(2,1)S(1)}, u32[]{:S(2)}, u32[]{:S(2)}) collective-permute-start(bf16[4096,128]{1,0:T(8,128)(2,1)} %bitcast.26), channel_id=1, source_target_pairs={{0,32},{32,0},{1,33},{33,1},{2,34},{34,2},{3,35},{35,3},{4,36},{36... | collective-permute-start | bytes 3145736 | tf_op jit(solution)/shard_map/ppermute | solution.py:19
  22.2 2.4 %collective-permute-start.1 = (bf16[4096,128]{1,0:T(8,128)(2,1)}, bf16[4096,128]{1,0:T(8,128)(2,1)}, u32[]{:S(2)}, u32[]{:S(2)}) collective-permute-start(bf16[4096,128]{1,0:T(8,128)(2,1)} %bitcast.29), channel_id=1, source_target_pairs={{0,32},{32,0},{1,33},{33,1},{2,34},{34,2},{3,35},{35,3},{4,36},{36... | collective-permute-start | bytes 3145736 | tf_op jit(solution)/shard_map/ppermute | solution.py:19
  24.7 1.9 %collective-permute-start.3 = (bf16[512,1024]{1,0:T(8,128)(2,1)}, bf16[512,1024]{1,0:T(8,128)(2,1)S(1)}, u32[]{:S(2)}, u32[]{:S(2)}) collective-permute-start(bf16[512,1024]{1,0:T(8,128)(2,1)} %bitcast.23), channel_id=1, source_target_pairs={{0,32},{32,0},{1,33},{33,1},{2,34},{34,2},{3,35},{35,3},{4,36},{36... | collective-permute-start | bytes 3145736 | tf_op jit(solution)/shard_map/ppermute | solution.py:19
  26.6 4.9 %all-to-all-done = bf16[8,64,256]{2,1,0:T(8,128)(2,1)S(1)} async-done(((bf16[8,64,256]{2,1,0:T(8,128)(2,1)}), bf16[8,64,256]{2,1,0:T(8,128)(2,1)S(1)}, u32[]{:S(2)}, u32[]{:S(2)}) %all-to-all-start) | async-done | bytes 262176 | tf_op jit(solution)/shard_map/all_to_all | solution.py:309
  31.5 1.9 %collective-permute-start.2 = (f32[8,8,128]{2,1,0:T(8,128)S(1)}, f32[8,8,128]{2,1,0:T(8,128)S(1)}, u32[]{:S(2)}, u32[]{:S(2)}) collective-permute-start(f32[8,8,128]{2,1,0:T(8,128)S(1)} %convert_reduce_fusion), channel_id=1, source_target_pairs={{0,32},{32,0},{1,33},{33,1},{2,34},{34,2},{3,35},{35,3},{4,36},{36... | collective-permute-start | bytes 98312 | tf_op jit(solution)/shard_map/ppermute | solution.py:19
  33.5 15.1 %all_gather.13.last_hbm = bf16[4,384,256]{2,1,0:T(8,128)(2,1)} all-gather(bf16[1,384,256]{2,1,0:T(8,128)(2,1)S(1)} %bitcast.32), channel_id=1, replica_groups=mesh['y'=8,'core'=2,'exp'=8,'tp'=4] {'tp'}, dimensions={0}, use_global_device_ids=true | all-gather | bytes 983040 | tf_op jit(solution)/shard_map/all_gather | solution.py:313
  48.6 0.1 multiply_reduce_fusion.3
  48.8 0.1 fusion.3
  48.9 0.2 multiply_reduce_fusion.2
  49.1 0.1 fusion.15
  49.2 0.1 multiply_reduce_fusion.1
  49.4 0.1 fusion.4
  49.5 0.2 multiply_reduce_fusion
  49.7 0.1 fusion.14
  49.9 1.0 copy-done.2
  50.9 2.0 %prepare.1.start_ref = f32[384,512]{1,0:T(8,128)S(1)} custom-call(bf16[4,384,256]{2,1,0:T(8,128)(2,1)} %all_gather.13.last_hbm, bf16[4096,128]{1,0:T(8,128)(2,1)} %bitcast.27, bf16[4096,128]{1,0:T(8,128)(2,1)} %bitcast.30, bf16[4096,128]{1,0:T(8,128)(2,1)} %copy-done.2, bf16[4096,128]{1,0:T(8,128)(2,1)} %collective-permute-done.1.up2_hbm), custom_call_target="tpu_custom_call" | custom-call | flops 402653184 | bytes 2621440 | tf_op jit(solution)/shard_map/prepare/pallas_call | solution.py:142
  52.9 0.0 copy-start
  52.9 18.6 %all-gather.3.cloned.1.call-done.rows_hbm = bf16[384,3072]{1,0:T(8,128)(2,1)} async-done(((bf16[48,3072]{1,0:T(8,128)(2,1)}), bf16[384,3072]{1,0:T(8,128)(2,1)}) %all-gather.3.cloned.1.call-update) | async-done | bytes 2359312 | tf_op jit(solution)/shard_map/all_gather | solution.py:290
  71.6 3.2 %ffn.1 = bf16[384,256]{1,0:T(8,128)(2,1)S(1)} custom-call(bf16[384,3072]{1,0:T(8,128)(2,1)} %all-gather.3.cloned.1.call-done.rows_hbm, bf16[4096,128]{1,0:T(8,128)(2,1)} %bitcast.28, bf16[4096,128]{1,0:T(8,128)(2,1)} %bitcast.31, bf16[4096,128]{1,0:T(8,128)(2,1)} %copy-done.2, bf16[4096,128]{1,0:T(8,128)(2,1)} %collective-permute-done.1.up2_hbm, ...), custom_call_target="tpu_custom_call" | custom-call | flops 1207959552 | bytes 5505024 | tf_op jit(solution)/shard_map/ffn/pallas_call | solution.py:202
  74.8 13.9 %all-gather = bf16[1536,256]{1,0:T(8,128)(2,1)S(1)} all-gather(bf16[384,256]{1,0:T(8,128)(2,1)S(1)} %ffn.1), channel_id=2, replica_groups=mesh['y'=8,'core'=2,'exp'=8,'tp'=4] {'tp'}, dimensions={0}, use_global_device_ids=true | all-gather | bytes 983040 | tf_op jit(solution)/shard_map/all_gather | solution.py:328
  88.7 1.0 down.1
  89.7 21.4 %all_to_all.15.parts_ref = bf16[8,48,1024]{2,1,0:T(8,128)(2,1)S(1)} all-to-all(bf16[8,48,1024]{2,1,0:T(8,128)(2,1)S(1)} %bitcast.21), channel_id=1, replica_groups=mesh['y'=8,'core'=2,'exp'=8,'tp'=4] {'y'}, dimensions={0} | all-to-all | bytes 1572864 | tf_op jit(solution)/shard_map/all_to_all | solution.py:330
  111.1 0.3 weigh.1
  111.4 17.7 %all_to_all.16 = bf16[8,16,1024]{2,1,0:T(8,128)(2,1)S(1)} all-to-all(bf16[8,16,1024]{2,1,0:T(8,128)(2,1)S(1)} %bitcast.25), channel_id=1, replica_groups=mesh['y'=8,'core'=2,'exp'=8,'tp'=4] {'exp'}, dimensions={0} | all-to-all | bytes 524288 | tf_op jit(solution)/shard_map/all_to_all | solution.py:332
  129.1 0.7 reduce_sum.112
  (26 shorter events, 0.2 us)
Async XLA Ops:
  12.5 19.0 %all-to-all-start = ((bf16[8,64,256]{2,1,0:T(8,128)(2,1)}), bf16[8,64,256]{2,1,0:T(8,128)(2,1)S(1)}, u32[]{:S(2)}, u32[]{:S(2)}) async-start(bf16[8,64,256]{2,1,0:T(8,128)(2,1)} %broadcast_in_dim.2), calls=%async_computation | async-start | bytes 524288 | tf_op jit(solution)/shard_map/all_to_all | solution.py:309
  19.6 52.0 %all-gather.3.cloned.1.call-start = ((), (), s32[]{:S(2)}) async-start(), calls=%async_computation.3 | async-start | bytes 2654208 | tf_op jit(solution)/shard_map/all_gather | solution.py:290
  20.3 29.5 %collective-permute-start = (bf16[4096,128]{1,0:T(8,128)(2,1)}, bf16[4096,128]{1,0:T(8,128)(2,1)S(1)}, u32[]{:S(2)}, u32[]{:S(2)}) collective-permute-start(bf16[4096,128]{1,0:T(8,128)(2,1)} %bitcast.26), channel_id=1, source_target_pairs={{0,32},{32,0},{1,33},{33,1},{2,34},{34,2},{3,35},{35,3},{4,36},{36... | collective-permute-start | bytes 3145736 | tf_op jit(solution)/shard_map/ppermute | solution.py:19
  22.2 27.6 %collective-permute-start.1 = (bf16[4096,128]{1,0:T(8,128)(2,1)}, bf16[4096,128]{1,0:T(8,128)(2,1)}, u32[]{:S(2)}, u32[]{:S(2)}) collective-permute-start(bf16[4096,128]{1,0:T(8,128)(2,1)} %bitcast.29), channel_id=1, source_target_pairs={{0,32},{32,0},{1,33},{33,1},{2,34},{34,2},{3,35},{35,3},{4,36},{36... | collective-permute-start | bytes 3145736 | tf_op jit(solution)/shard_map/ppermute | solution.py:19
  24.7 64.0 %collective-permute-start.3 = (bf16[512,1024]{1,0:T(8,128)(2,1)}, bf16[512,1024]{1,0:T(8,128)(2,1)S(1)}, u32[]{:S(2)}, u32[]{:S(2)}) collective-permute-start(bf16[512,1024]{1,0:T(8,128)(2,1)} %bitcast.23), channel_id=1, source_target_pairs={{0,32},{32,0},{1,33},{33,1},{2,34},{34,2},{3,35},{35,3},{4,36},{36... | collective-permute-start | bytes 3145736 | tf_op jit(solution)/shard_map/ppermute | solution.py:19
  31.5 17.1 %collective-permute-start.2 = (f32[8,8,128]{2,1,0:T(8,128)S(1)}, f32[8,8,128]{2,1,0:T(8,128)S(1)}, u32[]{:S(2)}, u32[]{:S(2)}) collective-permute-start(f32[8,8,128]{2,1,0:T(8,128)S(1)} %convert_reduce_fusion), channel_id=1, source_target_pairs={{0,32},{32,0},{1,33},{33,1},{2,34},{34,2},{3,35},{35,3},{4,36},{36... | collective-permute-start | bytes 98312 | tf_op jit(solution)/shard_map/ppermute | solution.py:19
  49.9 1.0 copy-start.2
  52.9 35.8 %copy-start = (bf16[1,512,1024]{2,1,0:T(8,128)(2,1)S(1)}, bf16[1,512,1024]{2,1,0:T(8,128)(2,1)}, u32[]{:S(2)}) copy-start(bf16[1,512,1024]{2,1,0:T(8,128)(2,1)} %param.11) | copy-start | bytes 3145732
  88.7 22.4 %copy-start.1 = (bf16[48,128]{1,0:T(8,128)(2,1)S(1)}, bf16[48,128]{1,0:T(8,128)(2,1)}, u32[]{:S(2)}) copy-start(bf16[48,128]{1,0:T(8,128)(2,1)} %get-tuple-element.23.select_ref) | copy-start | bytes 36868
Sparse Core Ops, SparseCore 0:
  22.5 49.0 all-gather.2

commit v9 on v8

--- a/solution.py
+++ b/solution.py
@@ -150,11 +150,7 @@
             pltpu.SemaphoreType.DMA((5,)),
         ],
         compiler_params=pltpu.CompilerParams(vmem_limit_bytes=FFN_VMEM),
-        cost_estimate=pl.CostEstimate(
-            flops=8 * count * shares * share * units,
-            bytes_accessed=2 * shares * share * (count + 4 * units) + 16 * count * units,
-            transcendentals=0,
-        ),
+        cost_estimate=pl.CostEstimate(flops=1, bytes_accessed=1, transcendentals=0),
         name="prepare",
     )(last, gate, up, gate2, up2)
 
@@ -247,6 +243,33 @@
     )(hidden, weight, weight2)
 
 
+def balance_kernel(place_ref, mine_ref, other_ref, gate_ref, kept_ref):
+    shards, experts, count = mine_ref.shape
+    target = 2.0 * shards * count * TOP / experts
+    weights = jnp.exp(jnp.concatenate([mine_ref[...], other_ref[...]], axis=0))
+    weights = weights * (TOP / jnp.sum(weights, axis=1, keepdims=True))
+    for repeat in range(ITERS):
+        column = jnp.sum(jnp.sum(weights, axis=0, keepdims=True), axis=2, keepdims=True)
+        weights = weights * (target / column)
+        weights = weights * (TOP / jnp.sum(weights, axis=1, keepdims=True))
+    kept_ref[...] = weights[:shards]
+    gate_ref[...] = kept_ref[place_ref[0], pl.ds(place_ref[1], 1), :]
+
+
+def balance(place, mine, other):
+    near = pl.BlockSpec(memory_space=pltpu.VMEM)
+    return pl.pallas_call(
+        balance_kernel,
+        in_specs=[pl.BlockSpec(memory_space=pltpu.SMEM), near, near],
+        out_specs=near,
+        out_shape=jax.ShapeDtypeStruct((1, mine.shape[2]), jnp.float32),
+        scratch_shapes=[pltpu.VMEM(mine.shape, jnp.float32)],
+        compiler_params=pltpu.CompilerParams(vmem_limit_bytes=24 << 20),
+        cost_estimate=pl.CostEstimate(flops=1, bytes_accessed=1, transcendentals=0),
+        name="balance",
+    )(place, mine, other)
+
+
 def weigh_kernel(parts_ref, select_ref, gate_ref, out_ref):
     select = select_ref[...]
     total = jnp.sum(parts_ref[...].astype(jnp.float32), axis=0).astype(jnp.bfloat16)
@@ -277,12 +300,10 @@
     local_rows = tokens.shape[0]
     experts = router_weight.shape[1]
     rings = lax.axis_size("y")
-    shards = rings * CORES
     owners = lax.axis_size("exp")
     parts = lax.axis_size("tp")
     capacity = min(local_rows, max(2, 3 * local_rows * TOP // (2 * experts)))
     out_rows = local_rows // owners
-    target = local_rows * shards * TOP / experts
     owner = lax.axis_index("exp")
 
     place = [jnp.reshape(lax.axis_index(axis), (1,)) for axis in ("exp", "tp")]
@@ -314,12 +335,7 @@
 
     tail = near[:, capacity:].reshape(rings, slots, local_rows)[:, :count]
     tail = jnp.sum(tail.reshape(rings, 3, experts, local_rows).astype(jnp.float32), axis=1)
-    weights = jnp.exp(jnp.concatenate([tail, swap_cores(tail)], axis=0))
-    weights = weights * (TOP / jnp.sum(weights, axis=1, keepdims=True))
-    for repeat in range(ITERS):
-        weights = weights * (target / jnp.sum(weights, axis=(0, 2), keepdims=True))
-        weights = weights * (TOP / jnp.sum(weights, axis=1, keepdims=True))
-    own = lax.dynamic_slice(weights, (lax.axis_index("y"), owner, 0), (1, 1, local_rows))[0]
+    own = balance(jnp.stack([lax.axis_index("y"), owner]), tail, swap_cores(tail))
 
     start = prepare(last, w_gate, w_up, gate2, up2)
     start = pltpu.with_memory_space_constraint(start, pltpu.VMEM)

time: 137 us -> 129 us (0.942)
  waiting for transfers between devices: 24.2 us -> 12.9 us
  blocking collectives: 68.1 us -> 71.9 us
    all_gather x1, waiting for transfers between devices: 18.6 us -> 1.47 us  [local(): rows = lax.all_gather(main, 'y', axis=0, tiled=True)]
    all_to_all x1, waiting for transfers between devices: 4.86 us -> 11.4 us  [local(): lax.all_to_all(jnp.broadcast_to(payload, (rings,) + payload.shape), 'y',...]
    all_to_all x1, blocking collectives: 17.7 us -> 21.8 us  [local(): lax.all_to_all(shares.reshape(owners, out_rows, shares.shape[1]), 'exp',...]
  transfers between devices with their start and end apart: 6 -> 6, of which waited for: 2 -> 2; matrix products, arithmetic and copies ran while one was open for 1% -> 3% of each run, Pallas kernels for 4% -> 5%
where the time goes in v9:
time: 129 us
  blocking collectives  71.9 us (56%)
  starting transfers between devices  15.3 us (12%)
  between operations  13.5 us (10%)
  waiting for transfers between devices  12.9 us (10%)
  Pallas kernels  10.4 us (8%)
  local copies, waits for them, and re-layouts  1.76 us (1%)
  matrix products  1.61 us (1%)
  other arithmetic  1.5 us (1%)
    all_to_all x1, blocking collectives, local(): lax.all_to_all(shares.reshape(owners, out_rows, shares.shape[1]), 'exp',...  21.8 us
    all_to_all x1, blocking collectives, local(): lax.all_to_all(partial.reshape(rings, capacity, partial.shape[1]), 'y', 0...  20.7 us
    all_gather x1, blocking collectives, local(): last = lax.all_gather(own_share, 'tp', axis=0)  15 us
    all_gather x1, blocking collectives, local(): full_hidden = lax.all_gather(hidden, 'tp', axis=0)  14.4 us
    all_to_all x1, waiting for transfers between devices, local(): lax.all_to_all(jnp.broadcast_to(payload, (rings,) + payload.shape), 'y',...  11.4 us
    ppermute x4, starting transfers between devices, swap_cores(): return lax.ppermute(value, 'core', [(0, 1), (1, 0)])  8.16 us
    all_to_all x1, starting transfers between devices, local(): lax.all_to_all(jnp.broadcast_to(payload, (rings,) + payload.shape), 'y',...  7.1 us
    pallas_call x1, Pallas kernels, ffn(): pl.pallas_call(ffn_kernel, in_specs=[pl.BlockSpec(memory_space=pltpu.HBM)...  3.24 us
  transfers between devices with their start and end apart: 6, of which 2 were waited for; matrix products, arithmetic and copies ran while one was open for 3% of the time, Pallas kernels for 5%

profile of v9, /device:TPU:2, one launch (start us, length us, event | category | flops | bytes accessed | tf_op | source)
XLA Modules:
  0.0 128.8 jit_solution(11228305634707214315)
XLA Ops:
  6.5 0.0 all-gather.3.cloned.1.call-start
  6.5 2.8 %route.1 = (bf16[48,128]{1,0:T(8,128)(2,1)}, bf16[48,3072]{1,0:T(8,128)(2,1)}, bf16[48,256]{1,0:T(8,128)(2,1)}) custom-call(s32[1]{0:T(128)} %bitcast.owner_ref, s32[1]{0:T(128)} %bitcast.1.part_ref, s32[1,8]{1,0:T(1,128)} %limits_hbm.1, s32[2,128]{1,0:T(2,128)} %bitcast.32, bf16[128,4096]{1,0:T(8,128)(2,1)} %tokens_hbm.1), custom_call_target="tpu_custom_call" | custom-call | flops 40894464 | bytes 1171456 | tf_op jit(solution)/shard_map/route/pallas_call | solution.py:83
  9.4 0.0 all-gather.3.cloned.1.call-update
  9.4 1.9 %collective-permute-start = (bf16[4096,128]{1,0:T(8,128)(2,1)}, bf16[4096,128]{1,0:T(8,128)(2,1)S(1)}, u32[]{:S(2)}, u32[]{:S(2)}) collective-permute-start(bf16[4096,128]{1,0:T(8,128)(2,1)} %bitcast.25), channel_id=1, source_target_pairs={{0,32},{32,0},{1,33},{33,1},{2,34},{34,2},{3,35},{35,3},{4,36},{36... | collective-permute-start | bytes 3145736 | tf_op jit(solution)/shard_map/ppermute | solution.py:19
  11.3 2.4 %collective-permute-start.1 = (bf16[4096,128]{1,0:T(8,128)(2,1)}, bf16[4096,128]{1,0:T(8,128)(2,1)}, u32[]{:S(2)}, u32[]{:S(2)}) collective-permute-start(bf16[4096,128]{1,0:T(8,128)(2,1)} %bitcast.28), channel_id=1, source_target_pairs={{0,32},{32,0},{1,33},{33,1},{2,34},{34,2},{3,35},{35,3},{4,36},{36... | collective-permute-start | bytes 3145736 | tf_op jit(solution)/shard_map/ppermute | solution.py:19
  13.7 1.6 %reduce-precision_convert_fusion.1 = (bf16[8,128]{1,0:T(8,128)(2,1)S(1)}, bf16[8,128]{1,0:T(8,128)(2,1)S(1)}, bf16[8,128]{1,0:T(8,128)(2,1)S(1)}) fusion(bf16[128,4096]{1,0:T(8,128)(2,1)} %tokens_hbm.1, bf16[4096,8]{0,1:T(8,128)(2,1)} %param.8), kind=kOutput, calls=%fused_computation.16 | convolution fusion | flops 8398848 | bytes 1120256 | tf_op jit(solution)/shard_map/dot_general | solution.py:317
  15.4 0.7 pad_maximum_fusion
  16.1 0.7 broadcast_in_dim.3
  16.9 7.1 %all-to-all-start = ((bf16[8,64,256]{2,1,0:T(8,128)(2,1)}), bf16[8,64,256]{2,1,0:T(8,128)(2,1)S(1)}, u32[]{:S(2)}, u32[]{:S(2)}) async-start(bf16[8,64,256]{2,1,0:T(8,128)(2,1)} %broadcast_in_dim.3), calls=%async_computation | async-start | bytes 524288 | tf_op jit(solution)/shard_map/all_to_all | solution.py:330
  24.0 1.9 %collective-permute-start.3 = (bf16[512,1024]{1,0:T(8,128)(2,1)}, bf16[512,1024]{1,0:T(8,128)(2,1)S(1)}, u32[]{:S(2)}, u32[]{:S(2)}) collective-permute-start(bf16[512,1024]{1,0:T(8,128)(2,1)} %bitcast.22), channel_id=1, source_target_pairs={{0,32},{32,0},{1,33},{33,1},{2,34},{34,2},{3,35},{35,3},{4,36},{36... | collective-permute-start | bytes 3145736 | tf_op jit(solution)/shard_map/ppermute | solution.py:19
  25.9 0.1 pad_add_fusion.place_ref
  26.0 11.4 %all-to-all-done = bf16[8,64,256]{2,1,0:T(8,128)(2,1)S(1)} async-done(((bf16[8,64,256]{2,1,0:T(8,128)(2,1)}), bf16[8,64,256]{2,1,0:T(8,128)(2,1)S(1)}, u32[]{:S(2)}, u32[]{:S(2)}) %all-to-all-start) | async-done | bytes 262176 | tf_op jit(solution)/shard_map/all_to_all | solution.py:330
  37.4 1.9 %collective-permute-start.2 = (f32[8,8,128]{2,1,0:T(8,128)S(1)}, f32[8,8,128]{2,1,0:T(8,128)S(1)}, u32[]{:S(2)}, u32[]{:S(2)}) collective-permute-start(f32[8,8,128]{2,1,0:T(8,128)S(1)} %convert_reduce_fusion.mine_ref), channel_id=1, source_target_pairs={{0,32},{32,0},{1,33},{33,1},{2,34},{34,2},{3,35},{35,3},{4,36},{36... | collective-permute-start | bytes 98312 | tf_op jit(solution)/shard_map/ppermute | solution.py:19
  39.3 15.0 %all_gather.13.last_hbm = bf16[4,384,256]{2,1,0:T(8,128)(2,1)} all-gather(bf16[1,384,256]{2,1,0:T(8,128)(2,1)S(1)} %bitcast.31), channel_id=1, replica_groups=mesh['y'=8,'core'=2,'exp'=8,'tp'=4] {'tp'}, dimensions={0}, use_global_device_ids=true | all-gather | bytes 983040 | tf_op jit(solution)/shard_map/all_gather | solution.py:334
  54.3 0.0 collective-permute-done.2.other_ref
  54.3 1.0 balance.1.gate_ref
  55.4 0.0 collective-permute-done.gate2_hbm
  55.4 0.0 copy-start.2
  55.4 1.0 copy-done.2
  56.3 0.0 collective-permute-done.1.up2_hbm
  56.3 2.1 %prepare.1.start_ref = f32[384,512]{1,0:T(8,128)S(1)} custom-call(bf16[4,384,256]{2,1,0:T(8,128)(2,1)} %all_gather.13.last_hbm, bf16[4096,128]{1,0:T(8,128)(2,1)} %bitcast.26, bf16[4096,128]{1,0:T(8,128)(2,1)} %bitcast.29, bf16[4096,128]{1,0:T(8,128)(2,1)} %copy-done.2, bf16[4096,128]{1,0:T(8,128)(2,1)} %collective-permute-done.1.up2_hbm), custom_call_target="tpu_custom_call" | custom-call | flops 1 | bytes 1 | tf_op jit(solution)/shard_map/prepare/pallas_call | solution.py:142
  58.4 0.0 copy-start
  58.4 1.5 %all-gather.3.cloned.1.call-done.rows_hbm = bf16[384,3072]{1,0:T(8,128)(2,1)} async-done(((bf16[48,3072]{1,0:T(8,128)(2,1)}), bf16[384,3072]{1,0:T(8,128)(2,1)}) %all-gather.3.cloned.1.call-update) | async-done | bytes 2359312 | tf_op jit(solution)/shard_map/all_gather | solution.py:311
  59.9 3.2 %ffn.1 = bf16[384,256]{1,0:T(8,128)(2,1)S(1)} custom-call(bf16[384,3072]{1,0:T(8,128)(2,1)} %all-gather.3.cloned.1.call-done.rows_hbm, bf16[4096,128]{1,0:T(8,128)(2,1)} %bitcast.27, bf16[4096,128]{1,0:T(8,128)(2,1)} %bitcast.30, bf16[4096,128]{1,0:T(8,128)(2,1)} %copy-done.2, bf16[4096,128]{1,0:T(8,128)(2,1)} %collective-permute-done.1.up2_hbm, ...), custom_call_target="tpu_custom_call" | custom-call | flops 1207959552 | bytes 5505024 | tf_op jit(solution)/shard_map/ffn/pallas_call | solution.py:198
  63.1 14.4 %all-gather = bf16[1536,256]{1,0:T(8,128)(2,1)S(1)} all-gather(bf16[384,256]{1,0:T(8,128)(2,1)S(1)} %ffn.1), channel_id=2, replica_groups=mesh['y'=8,'core'=2,'exp'=8,'tp'=4] {'tp'}, dimensions={0}, use_global_device_ids=true | all-gather | bytes 983040 | tf_op jit(solution)/shard_map/all_gather | solution.py:344
  77.5 0.0 collective-permute-done.3.down2_ref
  77.5 0.0 copy-done
  77.5 1.0 down.1
  78.5 20.7 %all_to_all.15.parts_ref = bf16[8,48,1024]{2,1,0:T(8,128)(2,1)S(1)} all-to-all(bf16[8,48,1024]{2,1,0:T(8,128)(2,1)S(1)} %bitcast.20), channel_id=1, replica_groups=mesh['y'=8,'core'=2,'exp'=8,'tp'=4] {'y'}, dimensions={0} | all-to-all | bytes 1572864 | tf_op jit(solution)/shard_map/all_to_all | solution.py:346
  99.2 0.3 weigh.1
  99.5 21.8 %all_to_all.16 = bf16[8,16,1024]{2,1,0:T(8,128)(2,1)S(1)} all-to-all(bf16[8,16,1024]{2,1,0:T(8,128)(2,1)S(1)} %bitcast.24), channel_id=1, replica_groups=mesh['y'=8,'core'=2,'exp'=8,'tp'=4] {'exp'}, dimensions={0} | all-to-all | bytes 524288 | tf_op jit(solution)/shard_map/all_to_all | solution.py:348
  121.3 0.7 reduce_sum.22
  (8 shorter events, 0.1 us)
Async XLA Ops:
  6.5 53.4 %all-gather.3.cloned.1.call-start = ((), (), s32[]{:S(2)}) async-start(), calls=%async_computation.3 | async-start | bytes 2654208 | tf_op jit(solution)/shard_map/all_gather | solution.py:311
  9.4 46.0 %collective-permute-start = (bf16[4096,128]{1,0:T(8,128)(2,1)}, bf16[4096,128]{1,0:T(8,128)(2,1)S(1)}, u32[]{:S(2)}, u32[]{:S(2)}) collective-permute-start(bf16[4096,128]{1,0:T(8,128)(2,1)} %bitcast.25), channel_id=1, source_target_pairs={{0,32},{32,0},{1,33},{33,1},{2,34},{34,2},{3,35},{35,3},{4,36},{36... | collective-permute-start | bytes 3145736 | tf_op jit(solution)/shard_map/ppermute | solution.py:19
  11.3 45.0 %collective-permute-start.1 = (bf16[4096,128]{1,0:T(8,128)(2,1)}, bf16[4096,128]{1,0:T(8,128)(2,1)}, u32[]{:S(2)}, u32[]{:S(2)}) collective-permute-start(bf16[4096,128]{1,0:T(8,128)(2,1)} %bitcast.28), channel_id=1, source_target_pairs={{0,32},{32,0},{1,33},{33,1},{2,34},{34,2},{3,35},{35,3},{4,36},{36... | collective-permute-start | bytes 3145736 | tf_op jit(solution)/shard_map/ppermute | solution.py:19
  16.9 20.5 %all-to-all-start = ((bf16[8,64,256]{2,1,0:T(8,128)(2,1)}), bf16[8,64,256]{2,1,0:T(8,128)(2,1)S(1)}, u32[]{:S(2)}, u32[]{:S(2)}) async-start(bf16[8,64,256]{2,1,0:T(8,128)(2,1)} %broadcast_in_dim.3), calls=%async_computation | async-start | bytes 524288 | tf_op jit(solution)/shard_map/all_to_all | solution.py:330
  24.0 53.6 %collective-permute-start.3 = (bf16[512,1024]{1,0:T(8,128)(2,1)}, bf16[512,1024]{1,0:T(8,128)(2,1)S(1)}, u32[]{:S(2)}, u32[]{:S(2)}) collective-permute-start(bf16[512,1024]{1,0:T(8,128)(2,1)} %bitcast.22), channel_id=1, source_target_pairs={{0,32},{32,0},{1,33},{33,1},{2,34},{34,2},{3,35},{35,3},{4,36},{36... | collective-permute-start | bytes 3145736 | tf_op jit(solution)/shard_map/ppermute | solution.py:19
  37.4 17.0 %collective-permute-start.2 = (f32[8,8,128]{2,1,0:T(8,128)S(1)}, f32[8,8,128]{2,1,0:T(8,128)S(1)}, u32[]{:S(2)}, u32[]{:S(2)}) collective-permute-start(f32[8,8,128]{2,1,0:T(8,128)S(1)} %convert_reduce_fusion.mine_ref), channel_id=1, source_target_pairs={{0,32},{32,0},{1,33},{33,1},{2,34},{34,2},{3,35},{35,3},{4,36},{36... | collective-permute-start | bytes 98312 | tf_op jit(solution)/shard_map/ppermute | solution.py:19
  55.4 1.0 copy-start.2
  58.4 19.1 %copy-start = (bf16[1,512,1024]{2,1,0:T(8,128)(2,1)S(1)}, bf16[1,512,1024]{2,1,0:T(8,128)(2,1)}, u32[]{:S(2)}) copy-start(bf16[1,512,1024]{2,1,0:T(8,128)(2,1)} %param.11) | copy-start | bytes 3145732
  77.5 21.7 %copy-start.1 = (bf16[48,128]{1,0:T(8,128)(2,1)S(1)}, bf16[48,128]{1,0:T(8,128)(2,1)}, u32[]{:S(2)}) copy-start(bf16[48,128]{1,0:T(8,128)(2,1)} %get-tuple-element.23.select_ref) | copy-start | bytes 36868
Sparse Core Ops, SparseCore 0:
  9.5 50.3 all-gather.2

commit v10 on v7

--- a/solution.py
+++ b/solution.py
@@ -219,24 +219,41 @@
     )(rows, gate, up, gate2, up2, start)
 
 
-def down_kernel(hidden_ref, down_ref, down2_ref, out_ref):
+def down_kernel(hidden_ref, down_ref, down2_ref, out_hbm, out_ref, sems):
     parts = hidden_ref.shape[0]
     units = down_ref.shape[0] // parts
-    total = None
-    for index in range(parts):
-        part = pl.ds(index * units, units)
-        both = jnp.concatenate([down_ref[part, :], down2_ref[part, :]], axis=0)
-        product = jnp.dot(hidden_ref[index], both, preferred_element_type=jnp.float32)
-        total = product if index == 0 else total + product
-    out_ref[...] = total.astype(out_ref.dtype)
-
-
-def down(hidden, weight, weight2):
+    chunks, _, chunk = out_ref.shape
+    copies = []
+    for place in range(chunks):
+        column = pl.ds(place * chunk, chunk)
+        total = None
+        for index in range(parts):
+            part = pl.ds(index * units, units)
+            both = jnp.concatenate([down_ref[part, column], down2_ref[part, column]], axis=0)
+            product = jnp.dot(hidden_ref[index], both, preferred_element_type=jnp.float32)
+            total = product if index == 0 else total + product
+        out_ref[place] = total.astype(out_ref.dtype)
+        copies.append(
+            pltpu.make_async_copy(out_ref.at[place], out_hbm.at[:, column], sems.at[place])
+        )
+        copies[-1].start()
+    for copy in copies:
+        copy.wait()
+
+
+def down(hidden, weight, weight2, chunks=4):
     parts, count, units = hidden.shape
     columns = weight.shape[1]
+    near = pl.BlockSpec(memory_space=pltpu.VMEM)
     return pl.pallas_call(
         down_kernel,
-        out_shape=pltpu.VMEM((count, columns), jnp.bfloat16),
+        in_specs=[near] * 3,
+        out_specs=pl.BlockSpec(memory_space=pltpu.HBM),
+        out_shape=jax.ShapeDtypeStruct((count, columns), jnp.bfloat16),
+        scratch_shapes=[
+            pltpu.VMEM((chunks, count, columns // chunks), jnp.bfloat16),
+            pltpu.SemaphoreType.DMA((chunks,)),
+        ],
         compiler_params=pltpu.CompilerParams(vmem_limit_bytes=24 << 20),
         cost_estimate=pl.CostEstimate(
             flops=2 * parts * count * units * columns,

time: 126 us -> 126 us (level)
  no operation moved by 1% of the time
where the time goes in v10:
time: 126 us; the launch traced here: 125 us
  blocking collectives  47.1 us (37%)
  waiting for transfers between devices  28.9 us (23%)
  starting transfers between devices  19.6 us (16%)
  between operations  13.6 us (11%)
  Pallas kernels  10.2 us (8%)
  other arithmetic  2.56 us (2%)
  local copies, waits for them, and re-layouts  1.79 us (1%)
  matrix products  1.61 us (1%)
    all_to_all x1, blocking collectives, local(): lax.all_to_all(shares.reshape(owners, out_rows, shares.shape[1]), 'exp',...  18.4 us
    all_to_all x1, waiting for transfers between devices, local(): lax.all_to_all(partial.reshape(rings, capacity, partial.shape[1]), 'y', 0...  17.2 us
    all_gather x1, blocking collectives, local(): last = lax.all_gather(own_share, 'tp', axis=0)  15.1 us
    all_gather x1, blocking collectives, local(): full_hidden = lax.all_gather(hidden, 'tp', axis=0)  13.6 us
    ppermute x4, starting transfers between devices, swap_cores(): return lax.ppermute(value, 'core', [(0, 1), (1, 0)])  8.16 us
    all_to_all x1, starting transfers between devices, local(): lax.all_to_all(jnp.broadcast_to(payload, (rings,) + payload.shape), 'y',...  7.1 us
    all_gather x1, waiting for transfers between devices, local(): rows = lax.all_gather(main, 'y', axis=0, tiled=True)  6.07 us
    all_to_all x1, waiting for transfers between devices, local(): lax.all_to_all(jnp.broadcast_to(payload, (rings,) + payload.shape), 'y',...  5.62 us
  transfers between devices with their start and end apart: 7, of which 3 were waited for; matrix products, arithmetic and copies ran while one was open for 3% of the time, Pallas kernels for 4%

profile of v10, /device:TPU:2, one launch (start us, length us, event | category | flops | bytes accessed | tf_op | source)
XLA Modules:
  0.0 125.5 jit_solution(13626587770205257940)
XLA Ops:
  6.5 2.8 %route.1 = (bf16[48,128]{1,0:T(8,128)(2,1)}, bf16[48,3072]{1,0:T(8,128)(2,1)}, bf16[48,256]{1,0:T(8,128)(2,1)}) custom-call(s32[1]{0:T(128)} %bitcast.owner_ref, s32[1]{0:T(128)} %bitcast.1.part_ref, s32[1,8]{1,0:T(1,128)} %limits_hbm.1, s32[2,128]{1,0:T(2,128)} %bitcast.32, bf16[128,4096]{1,0:T(8,128)(2,1)} %tokens_hbm.1), custom_call_target="tpu_custom_call" | custom-call | flops 40894464 | bytes 1171456 | tf_op jit(solution)/shard_map/route/pallas_call | solution.py:83
  9.4 0.0 all-gather.3.cloned.1.call-update
  9.4 1.6 %reduce-precision_convert_fusion.1 = (bf16[8,128]{1,0:T(8,128)(2,1)S(1)}, bf16[8,128]{1,0:T(8,128)(2,1)S(1)}, bf16[8,128]{1,0:T(8,128)(2,1)S(1)}) fusion(bf16[128,4096]{1,0:T(8,128)(2,1)} %tokens_hbm.1, bf16[4096,8]{0,1:T(8,128)(2,1)} %param.8), kind=kOutput, calls=%fused_computation.27 | convolution fusion | flops 8398848 | bytes 1120256 | tf_op jit(solution)/shard_map/dot_general | solution.py:313
  11.0 0.7 pad_maximum_fusion
  11.8 0.7 broadcast_in_dim.2
  12.5 7.1 %all-to-all-start = ((bf16[8,64,256]{2,1,0:T(8,128)(2,1)}), bf16[8,64,256]{2,1,0:T(8,128)(2,1)S(1)}, u32[]{:S(2)}, u32[]{:S(2)}) async-start(bf16[8,64,256]{2,1,0:T(8,128)(2,1)} %broadcast_in_dim.2), calls=%async_computation | async-start | bytes 524288 | tf_op jit(solution)/shard_map/all_to_all | solution.py:326
  19.6 1.9 %collective-permute-start = (bf16[4096,128]{1,0:T(8,128)(2,1)}, bf16[4096,128]{1,0:T(8,128)(2,1)S(1)}, u32[]{:S(2)}, u32[]{:S(2)}) collective-permute-start(bf16[4096,128]{1,0:T(8,128)(2,1)} %bitcast.25), channel_id=1, source_target_pairs={{0,32},{32,0},{1,33},{33,1},{2,34},{34,2},{3,35},{35,3},{4,36},{36... | collective-permute-start | bytes 3145736 | tf_op jit(solution)/shard_map/ppermute | solution.py:19
  21.5 2.4 %collective-permute-start.1 = (bf16[4096,128]{1,0:T(8,128)(2,1)}, bf16[4096,128]{1,0:T(8,128)(2,1)}, u32[]{:S(2)}, u32[]{:S(2)}) collective-permute-start(bf16[4096,128]{1,0:T(8,128)(2,1)} %bitcast.28), channel_id=1, source_target_pairs={{0,32},{32,0},{1,33},{33,1},{2,34},{34,2},{3,35},{35,3},{4,36},{36... | collective-permute-start | bytes 3145736 | tf_op jit(solution)/shard_map/ppermute | solution.py:19
  23.9 1.9 %collective-permute-start.2 = (bf16[512,1024]{1,0:T(8,128)(2,1)}, bf16[512,1024]{1,0:T(8,128)(2,1)S(1)}, u32[]{:S(2)}, u32[]{:S(2)}) collective-permute-start(bf16[512,1024]{1,0:T(8,128)(2,1)} %bitcast.22), channel_id=1, source_target_pairs={{0,32},{32,0},{1,33},{33,1},{2,34},{34,2},{3,35},{35,3},{4,36},{36... | collective-permute-start | bytes 3145736 | tf_op jit(solution)/shard_map/ppermute | solution.py:19
  25.9 5.6 %all-to-all-done = bf16[8,64,256]{2,1,0:T(8,128)(2,1)S(1)} async-done(((bf16[8,64,256]{2,1,0:T(8,128)(2,1)}), bf16[8,64,256]{2,1,0:T(8,128)(2,1)S(1)}, u32[]{:S(2)}, u32[]{:S(2)}) %all-to-all-start) | async-done | bytes 262176 | tf_op jit(solution)/shard_map/all_to_all | solution.py:326
  31.6 1.9 %collective-permute-start.3 = (f32[8,8,128]{2,1,0:T(8,128)S(1)}, f32[8,8,128]{2,1,0:T(8,128)S(1)}, u32[]{:S(2)}, u32[]{:S(2)}) collective-permute-start(f32[8,8,128]{2,1,0:T(8,128)S(1)} %convert_reduce_fusion), channel_id=1, source_target_pairs={{0,32},{32,0},{1,33},{33,1},{2,34},{34,2},{3,35},{35,3},{4,36},{36... | collective-permute-start | bytes 98312 | tf_op jit(solution)/shard_map/ppermute | solution.py:19
  33.5 15.1 %all_gather.13.last_hbm = bf16[4,384,256]{2,1,0:T(8,128)(2,1)} all-gather(bf16[1,384,256]{2,1,0:T(8,128)(2,1)S(1)} %bitcast.31), channel_id=1, replica_groups=mesh['y'=8,'core'=2,'exp'=8,'tp'=4] {'tp'}, dimensions={0}, use_global_device_ids=true | all-gather | bytes 983040 | tf_op jit(solution)/shard_map/all_gather | solution.py:330
  48.6 0.1 multiply_reduce_fusion.3
  48.8 0.1 fusion.3
  48.9 0.2 multiply_reduce_fusion.2
  49.1 0.1 fusion.15
  49.2 0.1 multiply_reduce_fusion.1
  49.4 1.0 copy-done.2
  50.4 2.0 %prepare.1.start_ref = f32[384,512]{1,0:T(8,128)S(1)} custom-call(bf16[4,384,256]{2,1,0:T(8,128)(2,1)} %all_gather.13.last_hbm, bf16[4096,128]{1,0:T(8,128)(2,1)} %bitcast.26, bf16[4096,128]{1,0:T(8,128)(2,1)} %bitcast.29, bf16[4096,128]{1,0:T(8,128)(2,1)} %copy-done.2, bf16[4096,128]{1,0:T(8,128)(2,1)} %collective-permute-done.1.up2_hbm), custom_call_target="tpu_custom_call" | custom-call | flops 402653184 | bytes 2621440 | tf_op jit(solution)/shard_map/prepare/pallas_call | solution.py:142
  52.4 0.0 copy-start
  52.5 6.1 %all-gather.3.cloned.1.call-done.rows_hbm = bf16[384,3072]{1,0:T(8,128)(2,1)} async-done(((bf16[48,3072]{1,0:T(8,128)(2,1)}), bf16[384,3072]{1,0:T(8,128)(2,1)}) %all-gather.3.cloned.1.call-update) | async-done | bytes 2359312 | tf_op jit(solution)/shard_map/all_gather | solution.py:307
  58.5 3.2 %ffn.1 = bf16[384,256]{1,0:T(8,128)(2,1)S(1)} custom-call(bf16[384,3072]{1,0:T(8,128)(2,1)} %all-gather.3.cloned.1.call-done.rows_hbm, bf16[4096,128]{1,0:T(8,128)(2,1)} %bitcast.27, bf16[4096,128]{1,0:T(8,128)(2,1)} %bitcast.30, bf16[4096,128]{1,0:T(8,128)(2,1)} %copy-done.2, bf16[4096,128]{1,0:T(8,128)(2,1)} %collective-permute-done.1.up2_hbm, ...), custom_call_target="tpu_custom_call" | custom-call | flops 1207959552 | bytes 5505024 | tf_op jit(solution)/shard_map/ffn/pallas_call | solution.py:202
  61.8 13.6 %all-gather = bf16[1536,256]{1,0:T(8,128)(2,1)S(1)} all-gather(bf16[384,256]{1,0:T(8,128)(2,1)S(1)} %ffn.1), channel_id=2, replica_groups=mesh['y'=8,'core'=2,'exp'=8,'tp'=4] {'tp'}, dimensions={0}, use_global_device_ids=true | all-gather | bytes 983040 | tf_op jit(solution)/shard_map/all_gather | solution.py:344
  75.4 1.8 %down.1 = bf16[384,1024]{1,0:T(8,128)(2,1)} custom-call(bf16[4,384,256]{2,1,0:T(8,128)(2,1)S(1)} %bitcast.21, bf16[512,1024]{1,0:T(8,128)(2,1)S(1)} %bitcast.23, bf16[512,1024]{1,0:T(8,128)(2,1)S(1)} %collective-permute-done.2.down2_ref), custom_call_target="tpu_custom_call" | custom-call | flops 805306368 | bytes 3670016 | tf_op jit(solution)/shard_map/down/pallas_call | solution.py:248
  77.2 4.4 %all-to-all-start.1 = ((bf16[8,48,1024]{2,1,0:T(8,128)(2,1)}), bf16[8,48,1024]{2,1,0:T(8,128)(2,1)S(1)}, u32[]{:S(2)}, u32[]{:S(2)}) async-start(bf16[8,48,1024]{2,1,0:T(8,128)(2,1)} %bitcast.9), calls=%async_computation.1 | async-start | bytes 1572864 | tf_op jit(solution)/shard_map/all_to_all | solution.py:346
  81.6 0.1 fusion.4
  81.7 0.2 multiply_reduce_fusion
  81.9 0.1 fusion.14
  82.0 17.2 %all-to-all-done.1.parts_ref = bf16[8,48,1024]{2,1,0:T(8,128)(2,1)S(1)} async-done(((bf16[8,48,1024]{2,1,0:T(8,128)(2,1)}), bf16[8,48,1024]{2,1,0:T(8,128)(2,1)S(1)}, u32[]{:S(2)}, u32[]{:S(2)}) %all-to-all-start.1) | async-done | bytes 786464 | tf_op jit(solution)/shard_map/all_to_all | solution.py:346
  99.3 0.3 weigh.1
  99.5 18.4 %all_to_all.15 = bf16[8,16,1024]{2,1,0:T(8,128)(2,1)S(1)} all-to-all(bf16[8,16,1024]{2,1,0:T(8,128)(2,1)S(1)} %bitcast.24), channel_id=1, replica_groups=mesh['y'=8,'core'=2,'exp'=8,'tp'=4] {'exp'}, dimensions={0} | all-to-all | bytes 524288 | tf_op jit(solution)/shard_map/all_to_all | solution.py:348
  118.0 0.7 reduce_sum.112
  (27 shorter events, 0.2 us)
Async XLA Ops:
  6.5 52.0 %all-gather.3.cloned.1.call-start = ((), (), s32[]{:S(2)}) async-start(), calls=%async_computation.3 | async-start | bytes 2654208 | tf_op jit(solution)/shard_map/all_gather | solution.py:307
  12.5 19.0 %all-to-all-start = ((bf16[8,64,256]{2,1,0:T(8,128)(2,1)}), bf16[8,64,256]{2,1,0:T(8,128)(2,1)S(1)}, u32[]{:S(2)}, u32[]{:S(2)}) async-start(bf16[8,64,256]{2,1,0:T(8,128)(2,1)} %broadcast_in_dim.2), calls=%async_computation | async-start | bytes 524288 | tf_op jit(solution)/shard_map/all_to_all | solution.py:326
  19.6 29.8 %collective-permute-start = (bf16[4096,128]{1,0:T(8,128)(2,1)}, bf16[4096,128]{1,0:T(8,128)(2,1)S(1)}, u32[]{:S(2)}, u32[]{:S(2)}) collective-permute-start(bf16[4096,128]{1,0:T(8,128)(2,1)} %bitcast.25), channel_id=1, source_target_pairs={{0,32},{32,0},{1,33},{33,1},{2,34},{34,2},{3,35},{35,3},{4,36},{36... | collective-permute-start | bytes 3145736 | tf_op jit(solution)/shard_map/ppermute | solution.py:19
  21.5 27.9 %collective-permute-start.1 = (bf16[4096,128]{1,0:T(8,128)(2,1)}, bf16[4096,128]{1,0:T(8,128)(2,1)}, u32[]{:S(2)}, u32[]{:S(2)}) collective-permute-start(bf16[4096,128]{1,0:T(8,128)(2,1)} %bitcast.28), channel_id=1, source_target_pairs={{0,32},{32,0},{1,33},{33,1},{2,34},{34,2},{3,35},{35,3},{4,36},{36... | collective-permute-start | bytes 3145736 | tf_op jit(solution)/shard_map/ppermute | solution.py:19
  23.9 51.4 %collective-permute-start.2 = (bf16[512,1024]{1,0:T(8,128)(2,1)}, bf16[512,1024]{1,0:T(8,128)(2,1)S(1)}, u32[]{:S(2)}, u32[]{:S(2)}) collective-permute-start(bf16[512,1024]{1,0:T(8,128)(2,1)} %bitcast.22), channel_id=1, source_target_pairs={{0,32},{32,0},{1,33},{33,1},{2,34},{34,2},{3,35},{35,3},{4,36},{36... | collective-permute-start | bytes 3145736 | tf_op jit(solution)/shard_map/ppermute | solution.py:19
  31.6 17.0 %collective-permute-start.3 = (f32[8,8,128]{2,1,0:T(8,128)S(1)}, f32[8,8,128]{2,1,0:T(8,128)S(1)}, u32[]{:S(2)}, u32[]{:S(2)}) collective-permute-start(f32[8,8,128]{2,1,0:T(8,128)S(1)} %convert_reduce_fusion), channel_id=1, source_target_pairs={{0,32},{32,0},{1,33},{33,1},{2,34},{34,2},{3,35},{35,3},{4,36},{36... | collective-permute-start | bytes 98312 | tf_op jit(solution)/shard_map/ppermute | solution.py:19
  49.4 1.0 copy-start.2
  52.4 22.9 %copy-start = (bf16[1,512,1024]{2,1,0:T(8,128)(2,1)S(1)}, bf16[1,512,1024]{2,1,0:T(8,128)(2,1)}, u32[]{:S(2)}) copy-start(bf16[1,512,1024]{2,1,0:T(8,128)(2,1)} %param.11) | copy-start | bytes 3145732
  75.4 23.9 %copy-start.1 = (bf16[48,128]{1,0:T(8,128)(2,1)S(1)}, bf16[48,128]{1,0:T(8,128)(2,1)}, u32[]{:S(2)}) copy-start(bf16[48,128]{1,0:T(8,128)(2,1)} %get-tuple-element.20.select_ref) | copy-start | bytes 36868
  77.2 22.0 %all-to-all-start.1 = ((bf16[8,48,1024]{2,1,0:T(8,128)(2,1)}), bf16[8,48,1024]{2,1,0:T(8,128)(2,1)S(1)}, u32[]{:S(2)}, u32[]{:S(2)}) async-start(bf16[8,48,1024]{2,1,0:T(8,128)(2,1)} %bitcast.9), calls=%async_computation.1 | async-start | bytes 1572864 | tf_op jit(solution)/shard_map/all_to_all | solution.py:346
Sparse Core Ops, SparseCore 0:
  9.5 48.9 all-gather.2

commit v11 on v7

--- a/solution.py
+++ b/solution.py
@@ -195,7 +195,7 @@
         out_ref[:, side * units : (side + 1) * units] = hidden.astype(out_ref.dtype)
 
 
-def ffn(rows, gate, up, gate2, up2, start, chunk=512):
+def ffn(rows, gate, up, gate2, up2, start, chunk=256):
     count, main = rows.shape
     units = gate.shape[1]
     near = pl.BlockSpec(memory_space=pltpu.VMEM)

time: 126 us -> 126 us (level)
  no operation moved by 1% of the time
where the time goes in v11:
time: 126 us
  blocking collectives  47.2 us (37%)
  waiting for transfers between devices  28.9 us (23%)
  starting transfers between devices  19.6 us (16%)
  between operations  13.6 us (11%)
  Pallas kernels  10.6 us (8%)
  other arithmetic  2.56 us (2%)
  local copies, waits for them, and re-layouts  1.79 us (1%)
  matrix products  1.61 us (1%)
    all_to_all x1, blocking collectives, local(): lax.all_to_all(shares.reshape(owners, out_rows, shares.shape[1]), 'exp',...  18.5 us
    all_to_all x1, waiting for transfers between devices, local(): lax.all_to_all(partial.reshape(rings, capacity, partial.shape[1]), 'y', 0...  17.2 us
    all_gather x1, blocking collectives, local(): last = lax.all_gather(own_share, 'tp', axis=0)  15.1 us
    all_gather x1, blocking collectives, local(): full_hidden = lax.all_gather(hidden, 'tp', axis=0)  13.7 us
    ppermute x4, starting transfers between devices, swap_cores(): return lax.ppermute(value, 'core', [(0, 1), (1, 0)])  8.16 us
    all_to_all x1, starting transfers between devices, local(): lax.all_to_all(jnp.broadcast_to(payload, (rings,) + payload.shape), 'y',...  7.1 us
    all_gather x1, waiting for transfers between devices, local(): rows = lax.all_gather(main, 'y', axis=0, tiled=True)  6.07 us
    all_to_all x1, waiting for transfers between devices, local(): lax.all_to_all(jnp.broadcast_to(payload, (rings,) + payload.shape), 'y',...  5.62 us
  transfers between devices with their start and end apart: 7, of which 3 were waited for; matrix products, arithmetic and copies ran while one was open for 3% of the time, Pallas kernels for 4%

profile of v11, /device:TPU:2, one launch (start us, length us, event | category | flops | bytes accessed | tf_op | source)
XLA Modules:
  0.0 125.9 jit_solution(4287498666398133340)
XLA Ops:
  6.5 2.8 %route.1 = (bf16[48,128]{1,0:T(8,128)(2,1)}, bf16[48,3072]{1,0:T(8,128)(2,1)}, bf16[48,256]{1,0:T(8,128)(2,1)}) custom-call(s32[1]{0:T(128)} %bitcast.owner_ref, s32[1]{0:T(128)} %bitcast.1.part_ref, s32[1,8]{1,0:T(1,128)} %limits_hbm.1, s32[2,128]{1,0:T(2,128)} %bitcast.32, bf16[128,4096]{1,0:T(8,128)(2,1)} %tokens_hbm.1), custom_call_target="tpu_custom_call" | custom-call | flops 40894464 | bytes 1171456 | tf_op jit(solution)/shard_map/route/pallas_call | solution.py:83
  9.4 0.0 all-gather.3.cloned.1.call-update
  9.4 1.6 %reduce-precision_convert_fusion.1 = (bf16[8,128]{1,0:T(8,128)(2,1)S(1)}, bf16[8,128]{1,0:T(8,128)(2,1)S(1)}, bf16[8,128]{1,0:T(8,128)(2,1)S(1)}) fusion(bf16[128,4096]{1,0:T(8,128)(2,1)} %tokens_hbm.1, bf16[4096,8]{0,1:T(8,128)(2,1)} %param.8), kind=kOutput, calls=%fused_computation.27 | convolution fusion | flops 8398848 | bytes 1120256 | tf_op jit(solution)/shard_map/dot_general | solution.py:296
  11.0 0.7 pad_maximum_fusion
  11.8 0.7 broadcast_in_dim.2
  12.5 7.1 %all-to-all-start = ((bf16[8,64,256]{2,1,0:T(8,128)(2,1)}), bf16[8,64,256]{2,1,0:T(8,128)(2,1)S(1)}, u32[]{:S(2)}, u32[]{:S(2)}) async-start(bf16[8,64,256]{2,1,0:T(8,128)(2,1)} %broadcast_in_dim.2), calls=%async_computation | async-start | bytes 524288 | tf_op jit(solution)/shard_map/all_to_all | solution.py:309
  19.6 1.9 %collective-permute-start = (bf16[4096,128]{1,0:T(8,128)(2,1)}, bf16[4096,128]{1,0:T(8,128)(2,1)S(1)}, u32[]{:S(2)}, u32[]{:S(2)}) collective-permute-start(bf16[4096,128]{1,0:T(8,128)(2,1)} %bitcast.25), channel_id=1, source_target_pairs={{0,32},{32,0},{1,33},{33,1},{2,34},{34,2},{3,35},{35,3},{4,36},{36... | collective-permute-start | bytes 3145736 | tf_op jit(solution)/shard_map/ppermute | solution.py:19
  21.5 2.4 %collective-permute-start.1 = (bf16[4096,128]{1,0:T(8,128)(2,1)}, bf16[4096,128]{1,0:T(8,128)(2,1)}, u32[]{:S(2)}, u32[]{:S(2)}) collective-permute-start(bf16[4096,128]{1,0:T(8,128)(2,1)} %bitcast.28), channel_id=1, source_target_pairs={{0,32},{32,0},{1,33},{33,1},{2,34},{34,2},{3,35},{35,3},{4,36},{36... | collective-permute-start | bytes 3145736 | tf_op jit(solution)/shard_map/ppermute | solution.py:19
  23.9 1.9 %collective-permute-start.2 = (bf16[512,1024]{1,0:T(8,128)(2,1)}, bf16[512,1024]{1,0:T(8,128)(2,1)S(1)}, u32[]{:S(2)}, u32[]{:S(2)}) collective-permute-start(bf16[512,1024]{1,0:T(8,128)(2,1)} %bitcast.22), channel_id=1, source_target_pairs={{0,32},{32,0},{1,33},{33,1},{2,34},{34,2},{3,35},{35,3},{4,36},{36... | collective-permute-start | bytes 3145736 | tf_op jit(solution)/shard_map/ppermute | solution.py:19
  25.9 5.6 %all-to-all-done = bf16[8,64,256]{2,1,0:T(8,128)(2,1)S(1)} async-done(((bf16[8,64,256]{2,1,0:T(8,128)(2,1)}), bf16[8,64,256]{2,1,0:T(8,128)(2,1)S(1)}, u32[]{:S(2)}, u32[]{:S(2)}) %all-to-all-start) | async-done | bytes 262176 | tf_op jit(solution)/shard_map/all_to_all | solution.py:309
  31.6 1.9 %collective-permute-start.3 = (f32[8,8,128]{2,1,0:T(8,128)S(1)}, f32[8,8,128]{2,1,0:T(8,128)S(1)}, u32[]{:S(2)}, u32[]{:S(2)}) collective-permute-start(f32[8,8,128]{2,1,0:T(8,128)S(1)} %convert_reduce_fusion), channel_id=1, source_target_pairs={{0,32},{32,0},{1,33},{33,1},{2,34},{34,2},{3,35},{35,3},{4,36},{36... | collective-permute-start | bytes 98312 | tf_op jit(solution)/shard_map/ppermute | solution.py:19
  33.5 15.1 %all_gather.13.last_hbm = bf16[4,384,256]{2,1,0:T(8,128)(2,1)} all-gather(bf16[1,384,256]{2,1,0:T(8,128)(2,1)S(1)} %bitcast.31), channel_id=1, replica_groups=mesh['y'=8,'core'=2,'exp'=8,'tp'=4] {'tp'}, dimensions={0}, use_global_device_ids=true | all-gather | bytes 983040 | tf_op jit(solution)/shard_map/all_gather | solution.py:313
  48.6 0.1 multiply_reduce_fusion.3
  48.8 0.1 fusion.3
  48.9 0.2 multiply_reduce_fusion.2
  49.1 0.1 fusion.15
  49.2 0.1 multiply_reduce_fusion.1
  49.4 1.0 copy-done.2
  50.4 2.0 %prepare.1.start_ref = f32[384,512]{1,0:T(8,128)S(1)} custom-call(bf16[4,384,256]{2,1,0:T(8,128)(2,1)} %all_gather.13.last_hbm, bf16[4096,128]{1,0:T(8,128)(2,1)} %bitcast.26, bf16[4096,128]{1,0:T(8,128)(2,1)} %bitcast.29, bf16[4096,128]{1,0:T(8,128)(2,1)} %copy-done.2, bf16[4096,128]{1,0:T(8,128)(2,1)} %collective-permute-done.1.up2_hbm), custom_call_target="tpu_custom_call" | custom-call | flops 402653184 | bytes 2621440 | tf_op jit(solution)/shard_map/prepare/pallas_call | solution.py:142
  52.4 0.0 copy-start
  52.5 6.1 %all-gather.3.cloned.1.call-done.rows_hbm = bf16[384,3072]{1,0:T(8,128)(2,1)} async-done(((bf16[48,3072]{1,0:T(8,128)(2,1)}), bf16[384,3072]{1,0:T(8,128)(2,1)}) %all-gather.3.cloned.1.call-update) | async-done | bytes 2359312 | tf_op jit(solution)/shard_map/all_gather | solution.py:290
  58.5 3.6 %ffn.1 = bf16[384,256]{1,0:T(8,128)(2,1)S(1)} custom-call(bf16[384,3072]{1,0:T(8,128)(2,1)} %all-gather.3.cloned.1.call-done.rows_hbm, bf16[4096,128]{1,0:T(8,128)(2,1)} %bitcast.27, bf16[4096,128]{1,0:T(8,128)(2,1)} %bitcast.30, bf16[4096,128]{1,0:T(8,128)(2,1)} %copy-done.2, bf16[4096,128]{1,0:T(8,128)(2,1)} %collective-permute-done.1.up2_hbm, ...), custom_call_target="tpu_custom_call" | custom-call | flops 1207959552 | bytes 5505024 | tf_op jit(solution)/shard_map/ffn/pallas_call | solution.py:202
  62.1 13.7 %all-gather = bf16[1536,256]{1,0:T(8,128)(2,1)S(1)} all-gather(bf16[384,256]{1,0:T(8,128)(2,1)S(1)} %ffn.1), channel_id=2, replica_groups=mesh['y'=8,'core'=2,'exp'=8,'tp'=4] {'tp'}, dimensions={0}, use_global_device_ids=true | all-gather | bytes 983040 | tf_op jit(solution)/shard_map/all_gather | solution.py:327
  75.8 1.9 %down.1 = bf16[384,1024]{1,0:T(8,128)(2,1)} custom-call(bf16[4,384,256]{2,1,0:T(8,128)(2,1)S(1)} %bitcast.21, bf16[512,1024]{1,0:T(8,128)(2,1)S(1)} %bitcast.23, bf16[512,1024]{1,0:T(8,128)(2,1)S(1)} %collective-permute-done.2.down2_ref), custom_call_target="tpu_custom_call" | custom-call | flops 805306368 | bytes 3670016 | tf_op jit(solution)/shard_map/down/pallas_call | solution.py:237
  77.7 4.3 %all-to-all-start.1 = ((bf16[8,48,1024]{2,1,0:T(8,128)(2,1)}), bf16[8,48,1024]{2,1,0:T(8,128)(2,1)S(1)}, u32[]{:S(2)}, u32[]{:S(2)}) async-start(bf16[8,48,1024]{2,1,0:T(8,128)(2,1)} %bitcast.9), calls=%async_computation.1 | async-start | bytes 1572864 | tf_op jit(solution)/shard_map/all_to_all | solution.py:329
  82.0 0.1 fusion.4
  82.1 0.2 multiply_reduce_fusion
  82.3 0.1 fusion.14
  82.5 17.2 %all-to-all-done.1.parts_ref = bf16[8,48,1024]{2,1,0:T(8,128)(2,1)S(1)} async-done(((bf16[8,48,1024]{2,1,0:T(8,128)(2,1)}), bf16[8,48,1024]{2,1,0:T(8,128)(2,1)S(1)}, u32[]{:S(2)}, u32[]{:S(2)}) %all-to-all-start.1) | async-done | bytes 786464 | tf_op jit(solution)/shard_map/all_to_all | solution.py:329
  99.6 0.3 weigh.1
  99.9 18.5 %all_to_all.15 = bf16[8,16,1024]{2,1,0:T(8,128)(2,1)S(1)} all-to-all(bf16[8,16,1024]{2,1,0:T(8,128)(2,1)S(1)} %bitcast.24), channel_id=1, replica_groups=mesh['y'=8,'core'=2,'exp'=8,'tp'=4] {'exp'}, dimensions={0} | all-to-all | bytes 524288 | tf_op jit(solution)/shard_map/all_to_all | solution.py:331
  118.4 0.7 reduce_sum.112
  (27 shorter events, 0.2 us)
Async XLA Ops:
  6.5 52.0 %all-gather.3.cloned.1.call-start = ((), (), s32[]{:S(2)}) async-start(), calls=%async_computation.3 | async-start | bytes 2654208 | tf_op jit(solution)/shard_map/all_gather | solution.py:290
  12.5 19.0 %all-to-all-start = ((bf16[8,64,256]{2,1,0:T(8,128)(2,1)}), bf16[8,64,256]{2,1,0:T(8,128)(2,1)S(1)}, u32[]{:S(2)}, u32[]{:S(2)}) async-start(bf16[8,64,256]{2,1,0:T(8,128)(2,1)} %broadcast_in_dim.2), calls=%async_computation | async-start | bytes 524288 | tf_op jit(solution)/shard_map/all_to_all | solution.py:309
  19.6 29.8 %collective-permute-start = (bf16[4096,128]{1,0:T(8,128)(2,1)}, bf16[4096,128]{1,0:T(8,128)(2,1)S(1)}, u32[]{:S(2)}, u32[]{:S(2)}) collective-permute-start(bf16[4096,128]{1,0:T(8,128)(2,1)} %bitcast.25), channel_id=1, source_target_pairs={{0,32},{32,0},{1,33},{33,1},{2,34},{34,2},{3,35},{35,3},{4,36},{36... | collective-permute-start | bytes 3145736 | tf_op jit(solution)/shard_map/ppermute | solution.py:19
  21.5 27.9 %collective-permute-start.1 = (bf16[4096,128]{1,0:T(8,128)(2,1)}, bf16[4096,128]{1,0:T(8,128)(2,1)}, u32[]{:S(2)}, u32[]{:S(2)}) collective-permute-start(bf16[4096,128]{1,0:T(8,128)(2,1)} %bitcast.28), channel_id=1, source_target_pairs={{0,32},{32,0},{1,33},{33,1},{2,34},{34,2},{3,35},{35,3},{4,36},{36... | collective-permute-start | bytes 3145736 | tf_op jit(solution)/shard_map/ppermute | solution.py:19
  23.9 51.8 %collective-permute-start.2 = (bf16[512,1024]{1,0:T(8,128)(2,1)}, bf16[512,1024]{1,0:T(8,128)(2,1)S(1)}, u32[]{:S(2)}, u32[]{:S(2)}) collective-permute-start(bf16[512,1024]{1,0:T(8,128)(2,1)} %bitcast.22), channel_id=1, source_target_pairs={{0,32},{32,0},{1,33},{33,1},{2,34},{34,2},{3,35},{35,3},{4,36},{36... | collective-permute-start | bytes 3145736 | tf_op jit(solution)/shard_map/ppermute | solution.py:19
  31.6 17.0 %collective-permute-start.3 = (f32[8,8,128]{2,1,0:T(8,128)S(1)}, f32[8,8,128]{2,1,0:T(8,128)S(1)}, u32[]{:S(2)}, u32[]{:S(2)}) collective-permute-start(f32[8,8,128]{2,1,0:T(8,128)S(1)} %convert_reduce_fusion), channel_id=1, source_target_pairs={{0,32},{32,0},{1,33},{33,1},{2,34},{34,2},{3,35},{35,3},{4,36},{36... | collective-permute-start | bytes 98312 | tf_op jit(solution)/shard_map/ppermute | solution.py:19
  49.4 1.0 copy-start.2
  52.4 23.3 %copy-start = (bf16[1,512,1024]{2,1,0:T(8,128)(2,1)S(1)}, bf16[1,512,1024]{2,1,0:T(8,128)(2,1)}, u32[]{:S(2)}) copy-start(bf16[1,512,1024]{2,1,0:T(8,128)(2,1)} %param.11) | copy-start | bytes 3145732
  75.8 23.9 %copy-start.1 = (bf16[48,128]{1,0:T(8,128)(2,1)S(1)}, bf16[48,128]{1,0:T(8,128)(2,1)}, u32[]{:S(2)}) copy-start(bf16[48,128]{1,0:T(8,128)(2,1)} %get-tuple-element.20.select_ref) | copy-start | bytes 36868
  77.7 22.0 %all-to-all-start.1 = ((bf16[8,48,1024]{2,1,0:T(8,128)(2,1)}), bf16[8,48,1024]{2,1,0:T(8,128)(2,1)S(1)}, u32[]{:S(2)}, u32[]{:S(2)}) async-start(bf16[8,48,1024]{2,1,0:T(8,128)(2,1)} %bitcast.9), calls=%async_computation.1 | async-start | bytes 1572864 | tf_op jit(solution)/shard_map/all_to_all | solution.py:329
Sparse Core Ops, SparseCore 0:
  9.5 48.9 all-gather.2
